TPU v7x, 256 devices: a whole 4x4x8 slice. The times are simulated.
256 devices in a mesh: seq: 16 (over z, core), head: 4 (over x), dp: 4 (over y).
Axes of the slice: x: 4, y: 4, z: 8, core: 2. Of those that a mesh axis runs over, the one named last changes fastest.
Arguments:
- self_queries: bfloat16 [4, 2048, 2560], P('dp', ('seq', 'head')), may hold values from -8 to 8
- self_keys: bfloat16 [4, 2048, 2560], P('dp', ('seq', 'head')), may hold values from -4 to 4
- self_values: bfloat16 [4, 2048, 2560], P('dp', ('seq', 'head')), may hold values from -6 to 6
- self_cotangent: bfloat16 [4, 2048, 2560], P('dp', ('seq', 'head')), may hold values from -6 to 6
- text_queries: bfloat16 [4, 4096, 2560], P('dp', 'seq', 'head'), may hold values from -8 to 8
- memory_keys: bfloat16 [4, 2048, 2560], P('dp', 'seq', 'head'), may hold values from -4 to 4
- memory_values: bfloat16 [4, 2048, 2560], P('dp', 'seq', 'head'), may hold values from -6 to 6
- text_cotangent: bfloat16 [4, 4096, 2560], P('dp', 'seq', 'head'), may hold values from -6 to 6
- slopes: float32 [2, 20], P(None, 'head'), may hold values from 0.01 to 0.3
- page_counts: int32 [4, 4], P('dp'), may hold values from 1 to 1024, as said below
- page_cols: int32 [4, 4], P('dp'), may hold values from 4 to 64
- text_page: int32 [4, 4096], P('dp'), may hold values from 0 to 3, as said below
Outputs:
- self_query_grad: bfloat16 [4, 2048, 2560], P('dp', ('seq', 'head'))
- self_key_grad: bfloat16 [4, 2048, 2560], P('dp', ('seq', 'head'))
- self_value_grad: bfloat16 [4, 2048, 2560], P('dp', ('seq', 'head'))
- slope_grad: float32 [2, 20], P(None, 'head')
- text_query_grad: bfloat16 [4, 4096, 2560], P('dp', 'seq', 'head')
- memory_key_grad: bfloat16 [4, 2048, 2560], P('dp', 'seq', 'head')
- memory_value_grad: bfloat16 [4, 2048, 2560], P('dp', 'seq', 'head')
Inputs may be any that keep to these rules, and one draw needn't show every extreme that they name: `page_counts`: each pack's counts sum to 2048; one page of every pack has exactly 1024 patches. `text_page`: never falls along a pack's text rows; every page has at least one text row.
All inputs are finite; a program needn't handle non-finite values.
Results may differ from a plain program's by a relative error of at most 0.006.
Values may be sent and summed in bfloat16 or wider, within the bound.
No kernel may reach another device: no remote copies, remote signals or barrier semaphores. Data moves between devices by JAX's collectives and lax.ppermute only.
A program may use at most 128 MiB of HBM per device.

v0:
```python
import jax
import jax.numpy as jnp
from jax import lax
from jax.sharding import PartitionSpec as P

MASK_FILL = -1e30


def page_layout(counts, widths, patch_total):
    page_ends = jnp.cumsum(counts)
    starts = page_ends - counts
    positions = jnp.arange(patch_total, dtype=jnp.int32)
    page_ids = jnp.sum((positions[:, None] >= page_ends[None, :]).astype(jnp.int32), axis=1)
    one_hot = page_ids[:, None] == jnp.arange(counts.shape[0], dtype=jnp.int32)[None, :]
    page_start = jnp.sum(jnp.where(one_hot, starts[None, :], 0), axis=1)
    page_width = jnp.sum(jnp.where(one_hot, widths[None, :], 0), axis=1)
    offsets = positions - page_start
    return (page_ids, offsets // page_width, offsets % page_width)


def take_rows(vector, row_start, row_count):
    return lax.dynamic_slice_in_dim(vector, row_start, row_count, 0)


def heads_of(matrix, head_count):
    return matrix.reshape(matrix.shape[0], head_count, -1)


def alibi(slopes, query_layout, key_layout):
    row_gap = jnp.abs(query_layout[1][:, None] - key_layout[1][None, :]).astype(jnp.float32)
    col_gap = jnp.abs(query_layout[2][:, None] - key_layout[2][None, :]).astype(jnp.float32)
    same_page = query_layout[0][:, None] == key_layout[0][None, :]
    decay = -(slopes[0][:, None, None] * row_gap[None] + slopes[1][:, None, None] * col_gap[None])
    return (jnp.where(same_page[None], decay, MASK_FILL), row_gap, col_gap)


def query_side(queries, key_rows, value_rows, grad_rows, logit_bias):
    inv_root = queries.shape[2] ** (-0.5)
    scores = (
        jnp.einsum("rhs,khs->hrk", queries, key_rows, preferred_element_type=jnp.float32) * inv_root
        + logit_bias
    )
    row_max = jnp.max(scores, axis=2, keepdims=True)
    weights = jnp.exp(scores - row_max)
    row_total = jnp.sum(weights, axis=2, keepdims=True)
    softmax_w = weights / row_total
    log_total = (row_max + jnp.log(row_total))[:, :, 0]
    grad_probs = jnp.einsum(
        "rhs,khs->hrk", grad_rows, value_rows, preferred_element_type=jnp.float32
    )
    row_delta = jnp.sum(softmax_w * grad_probs, axis=2, keepdims=True)
    grad_scores = softmax_w * (grad_probs - row_delta)
    grad_scores_b = grad_scores.astype(jnp.bfloat16)
    query_grad = (
        jnp.einsum("hrk,khs->rhs", grad_scores_b, key_rows, preferred_element_type=jnp.float32)
        * inv_root
    )
    return (
        query_grad,
        grad_scores,
        grad_scores_b,
        softmax_w.astype(jnp.bfloat16),
        log_total,
        row_delta[:, :, 0],
    )


def key_terms(grad_scores_b, softmax_b, queries, grad_rows, row_count):
    inv_root = queries.shape[3] ** (-0.5)
    key_grad = (
        jnp.einsum("chrk,crhs->khs", grad_scores_b, queries, preferred_element_type=jnp.float32)
        * inv_root
    )
    value_grad = jnp.einsum(
        "chrk,crhs->khs", softmax_b, grad_rows, preferred_element_type=jnp.float32
    )
    return jnp.stack([key_grad.reshape(row_count, -1), value_grad.reshape(row_count, -1)], axis=1)


def local(
    self_queries,
    self_keys,
    self_values,
    self_cotangent,
    text_queries,
    memory_keys,
    memory_values,
    text_cotangent,
    slopes,
    page_counts,
    page_cols,
    text_page,
):
    head_count = slopes.shape[1]
    regrouped = (
        lax.all_to_all(self_queries[0], "head", split_axis=1, concat_axis=0, tiled=True),
        lax.all_to_all(self_keys[0], "head", split_axis=1, concat_axis=0, tiled=True),
        lax.all_to_all(self_values[0], "head", split_axis=1, concat_axis=0, tiled=True),
        lax.all_to_all(self_cotangent[0], "head", split_axis=1, concat_axis=0, tiled=True),
    )
    local_queries, local_keys, local_values, local_grads = regrouped
    patch_rows = local_queries.shape[0]
    all_keys, all_values = (
        lax.all_gather(local_keys, "seq", axis=0, tiled=True),
        lax.all_gather(local_values, "seq", axis=0, tiled=True),
    )
    patch_total = all_keys.shape[0]
    whole_layout = page_layout(page_counts[0], page_cols[0], patch_total)
    own_start = lax.axis_index("seq") * patch_rows
    own_layout = tuple((take_rows(item, own_start, patch_rows) for item in whole_layout))
    self_bias, row_gap, col_gap = alibi(slopes, own_layout, whole_layout)
    query_heads = heads_of(local_queries, head_count)
    grad_heads = heads_of(local_grads, head_count)
    self_dq, self_ds, self_ds_b, self_p_b, self_lse, self_delta = query_side(
        query_heads,
        heads_of(all_keys, head_count),
        heads_of(all_values, head_count),
        grad_heads,
        self_bias,
    )
    slope_local = -jnp.stack(
        [
            jnp.sum(self_ds * row_gap[None], axis=(1, 2)),
            jnp.sum(self_ds * col_gap[None], axis=(1, 2)),
        ]
    )
    self_ds_blocks = self_ds_b[None]
    self_p_blocks = self_p_b[None]
    query_blocks = query_heads[None]
    grad_blocks = grad_heads[None]
    self_pair = lax.psum_scatter(
        key_terms(
            self_ds_blocks,
            self_p_blocks,
            query_blocks,
            grad_blocks,
            patch_rows * lax.axis_size("seq"),
        ),
        "seq",
        scatter_dimension=0,
        tiled=True,
    )
    self_dk = self_pair[:, 0]
    self_dv = self_pair[:, 1]
    restored = (
        lax.all_to_all(
            self_dq.reshape(patch_rows, -1).astype(jnp.bfloat16),
            "head",
            split_axis=0,
            concat_axis=1,
            tiled=True,
        ),
        lax.all_to_all(
            self_dk.astype(jnp.bfloat16), "head", split_axis=0, concat_axis=1, tiled=True
        ),
        lax.all_to_all(
            self_dv.astype(jnp.bfloat16), "head", split_axis=0, concat_axis=1, tiled=True
        ),
    )
    slope_grad = lax.psum(slope_local, ("seq", "dp")) / patch_total
    memory_all_keys, memory_all_values = (
        lax.all_gather(memory_keys[0], "seq", axis=0, tiled=True),
        lax.all_gather(memory_values[0], "seq", axis=0, tiled=True),
    )
    memory_all_key_heads = heads_of(memory_all_keys, head_count)
    memory_all_value_heads = heads_of(memory_all_values, head_count)
    text_rows = text_queries.shape[1]
    text_start = lax.axis_index("seq") * text_rows
    text_ids = text_page[0]
    own_text = take_rows(text_ids, text_start, text_rows)
    text_query_heads = heads_of(text_queries[0], head_count)
    text_grad_heads = heads_of(text_cotangent[0], head_count)
    block_count = text_rows // text_rows
    text_query_blocks = text_query_heads.reshape(block_count, text_rows, head_count, -1)
    text_grad_blocks = text_grad_heads.reshape(block_count, text_rows, head_count, -1)

    def cross_block(inputs):
        block_queries, block_grads, block_pages = inputs
        block_bias = jnp.where(
            block_pages[:, None] == whole_layout[0][None, :], 0.0, MASK_FILL
        ).astype(jnp.float32)[None]
        result = query_side(
            block_queries, memory_all_key_heads, memory_all_value_heads, block_grads, block_bias
        )
        return (result[0], result[2], result[3], result[4], result[5])

    cross_out = lax.map(
        cross_block, (text_query_blocks, text_grad_blocks, own_text.reshape(block_count, text_rows))
    )
    text_dq = cross_out[0].reshape(text_rows, -1)
    text_ds_b = cross_out[1]
    text_p_b = cross_out[2]
    memory_pair = lax.psum_scatter(
        key_terms(
            text_ds_b,
            text_p_b,
            text_query_blocks,
            text_grad_blocks,
            patch_rows * lax.axis_size("seq"),
        ),
        "seq",
        scatter_dimension=0,
        tiled=True,
    )
    memory_dk = memory_pair[:, 0]
    memory_dv = memory_pair[:, 1]
    return (
        restored[0][None],
        restored[1][None],
        restored[2][None],
        slope_grad,
        text_dq.astype(jnp.bfloat16)[None],
        memory_dk.astype(jnp.bfloat16)[None],
        memory_dv.astype(jnp.bfloat16)[None],
    )


def solution(mesh):
    in_specs = (
        P("dp", ("seq", "head"), None),
        P("dp", ("seq", "head"), None),
        P("dp", ("seq", "head"), None),
        P("dp", ("seq", "head"), None),
        P("dp", "seq", "head"),
        P("dp", "seq", "head"),
        P("dp", "seq", "head"),
        P("dp", "seq", "head"),
        P(None, "head"),
        P("dp", None),
        P("dp", None),
        P("dp", None),
    )
    out_specs = (
        P("dp", ("seq", "head"), None),
        P("dp", ("seq", "head"), None),
        P("dp", ("seq", "head"), None),
        P(None, "head"),
        P("dp", "seq", "head"),
        P("dp", "seq", "head"),
        P("dp", "seq", "head"),
    )
    return jax.shard_map(local, mesh=mesh, in_specs=in_specs, out_specs=out_specs, check_vma=False)
```

profile of v0, /device:TPU:8, one launch (start us, length us, event | category | flops | bytes accessed | tf_op | source)
XLA Modules:
  0.0 403.5 jit_solution(9305916653580052399)
XLA Ops:
  8.3 10.4 %all_to_all.109 = bf16[32,4,640]{2,0,1:T(8,128)(2,1)} all-to-all(bf16[32,4,640]{2,0,1:T(8,128)(2,1)S(1)} %copy.117), channel_id=1, replica_groups=mesh['seq'=16,'head'=4,'dp'=4] {'head'}, dimensions={1} | all-to-all | bytes 327680 | tf_op jit(solution)/shard_map/all_to_all | solution.py:97
  19.7 9.2 %all_to_all.110 = bf16[32,4,640]{2,0,1:T(8,128)(2,1)} all-to-all(bf16[32,4,640]{2,0,1:T(8,128)(2,1)S(1)} %copy.122), channel_id=1, replica_groups=mesh['seq'=16,'head'=4,'dp'=4] {'head'}, dimensions={1} | all-to-all | bytes 327680 | tf_op jit(solution)/shard_map/all_to_all | solution.py:98
  43.2 4.7 %all-to-all-start.2 = ((bf16[32,4,640]{2,0,1:T(8,128)(2,1)}), bf16[32,4,640]{2,0,1:T(8,128)(2,1)S(1)}, u32[]{:S(2)}, u32[]{:S(2)}) async-start(bf16[32,4,640]{2,0,1:T(8,128)(2,1)} %copy.121), calls=%async_computation.2 | async-start | bytes 327680 | tf_op jit(solution)/shard_map/all_to_all | solution.py:99
  48.3 5.7 %all-to-all-done.2 = bf16[32,4,640]{2,0,1:T(8,128)(2,1)S(1)} async-done(((bf16[32,4,640]{2,0,1:T(8,128)(2,1)}), bf16[32,4,640]{2,0,1:T(8,128)(2,1)S(1)}, u32[]{:S(2)}, u32[]{:S(2)}) %all-to-all-start.2) | async-done | bytes 163872 | tf_op jit(solution)/shard_map/all_to_all | solution.py:99
  54.4 5.8 %all-gather.7.cloned.1.call-done = bf16[2048,640]{1,0:T(8,128)(2,1)} async-done(((bf16[128,640]{1,0:T(8,128)(2,1)}), bf16[2048,640]{1,0:T(8,128)(2,1)}) %all-gather.7.cloned.1.call-update) | async-done | bytes 2621456 | tf_op jit(solution)/shard_map/all_gather | solution.py:104
  63.2 37.7 %all-gather.9.cloned.1.call-done = bf16[2048,640]{1,0:T(8,128)(2,1)} async-done(((bf16[128,640]{1,0:T(8,128)(2,1)}), bf16[2048,640]{1,0:T(8,128)(2,1)}) %all-gather.9.cloned.1.call-update) | async-done | bytes 2621456 | tf_op jit(solution)/shard_map/all_gather | solution.py:105
  101.0 4.5 %copy.123 = bf16[2048,640]{0,1:T(8,128)(2,1)} copy(bf16[2048,640]{1,0:T(8,128)(2,1)} %all-gather.9.cloned.1.call-done) | data formatting | bytes 5242880 | tf_op jit(solution)/shard_map/all_gather | solution.py:105
  119.8 6.0 %copy.131 = f32[2048,1,640]{2,0,1:T(8,128)} copy(f32[2048,1,640]{0,2,1:T(8,128)} %bitcast.79) | data formatting | bytes 10485760 | tf_op jit(solution)/shard_map/stack;reshape | solution.py:77
  125.7 8.0 %fusion.7 = f32[5,2048,128]{1,2,0:T(8,128)} fusion(bf16[128,5,128]{0,2,1:T(8,128)(2,1)S(1)} %copy.130, f32[5,128]{1,0:T(8,128)S(1)} %get-tuple-element.85, f32[5,128,2048]{2,1,0:T(8,128)} %copy-done.4), kind=kOutput, calls=%fused_computation.22 | convolution fusion | flops 339479168 | bytes 10652160 | tf_op jit(solution)/shard_map/chrk,crhs->khs/dot_general | solution.py:74
  133.7 5.9 %copy.132 = f32[2048,1,640]{2,0,1:T(8,128)} copy(f32[2048,1,640]{0,2,1:T(8,128)} %bitcast.84) | data formatting | bytes 10485760 | tf_op jit(solution)/shard_map/stack;reshape | solution.py:77
  139.6 8.8 %pad_maximum_fusion = f32[2048,2,640]{2,0,1:T(8,128)} fusion(f32[2048,1,640]{2,0,1:T(8,128)} %copy.132, f32[2048,1,640]{2,0,1:T(8,128)} %copy.131), kind=kLoop, calls=%fused_computation.2 | loop fusion | flops 2621440 | bytes 20971520 | tf_op jit(solution)/shard_map/stack | solution.py:77
  152.3 9.5 %fusion.29 = (f32[5,256]{1,0:T(8,128)S(1)}, f32[5,256,2048]{2,1,0:T(8,128)}) fusion(f32[256,2048]{1,0:T(8,128)} %compare_select_fusion, bf16[256,5,128]{0,2,1:T(8,128)(2,1)S(1)} %bitcast.87, bf16[2048,5,128]{0,2,1:T(8,128)(2,1)} %bitcast.104), kind=kOutput, calls=%fused_computation.62 | convolution fusion | flops 681576448 | bytes 15537152 | tf_op jit(solution)/shard_map/while/body/eval_jaxpr/sub | solution.py:44
  161.8 27.1 %all-gather.13.cloned.1.call-done = bf16[1,2048,640]{1,2,0:T(8,128)(2,1)} async-done(((bf16[1,128,640]{1,2,0:T(8,128)(2,1)}), bf16[1,2048,640]{1,2,0:T(8,128)(2,1)}) %all-gather.13.cloned.1.call-update) | async-done | bytes 2621456 | tf_op jit(solution)/shard_map/all_gather | solution.py:163
  188.9 6.1 %multiply_reduce_fusion = (f32[5,256]{1,0:T(8,128)S(1)}, f32[5,256,2048]{2,1,0:T(8,128)S(1)}) fusion(f32[5,256,2048]{2,1,0:T(8,128)} %get-tuple-element.90, f32[5,256]{1,0:T(8,128)S(1)} %get-tuple-element.89, bf16[256,5,128]{0,2,1:T(8,128)(2,1)S(1)} %bitcast.96, bf16[2048,5,128]{0,2,1:T(8,128)(2,1)} %bitcast.106), kind=kOutput, calls=%fused_computation.5 | convolution fusion | flops 678951680 | bytes 23930880 | tf_op jit(solution)/shard_map/while/body/eval_jaxpr/rhs,khs->hrk/dot_general | solution.py:48
  202.6 5.9 %copy.143 = f32[2048,1,640]{2,0,1:T(8,128)} copy(f32[2048,1,640]{0,2,1:T(8,128)} %bitcast.78) | data formatting | bytes 10485760 | tf_op jit(solution)/shard_map/stack;reshape | solution.py:77
  208.5 7.4 %fusion.3 = f32[5,2048,128]{1,2,0:T(8,128)} fusion(bf16[256,5,128]{0,2,1:T(8,128)(2,1)S(1)} %bitcast.97, f32[5,256,2048]{2,1,0:T(8,128)} %get-tuple-element.90, f32[5,256]{1,0:T(8,128)S(1)} %get-tuple-element.89), kind=kOutput, calls=%fused_computation.9 | convolution fusion | flops 676331520 | bytes 16061440 | tf_op jit(solution)/shard_map/chrk,crhs->khs/dot_general | solution.py:74
  215.9 5.9 %copy.144 = f32[2048,1,640]{2,0,1:T(8,128)} copy(f32[2048,1,640]{0,2,1:T(8,128)} %bitcast.85) | data formatting | bytes 10485760 | tf_op jit(solution)/shard_map/stack;reshape | solution.py:77
  221.8 8.7 %pad_maximum_fusion.1 = f32[2048,2,640]{2,0,1:T(8,128)} fusion(f32[2048,1,640]{2,0,1:T(8,128)} %copy.144, f32[2048,1,640]{2,0,1:T(8,128)} %copy.143), kind=kLoop, calls=%fused_computation.3 | loop fusion | flops 2621440 | bytes 20971520 | tf_op jit(solution)/shard_map/stack | solution.py:77
  230.5 5.3 %fusion.14 = bf16[5,256,128]{1,2,0:T(8,128)(2,1)S(1)} fusion(bf16[5,256,2048]{2,1,0:T(8,128)(2,1)} %copy-done.2, bf16[2048,5,128]{0,2,1:T(8,128)(2,1)} %bitcast.105), kind=kOutput, calls=%fused_computation.31 | convolution fusion | flops 671416320 | bytes 8192000 | tf_op jit(solution)/shard_map/while/body/eval_jaxpr/hrk,khs->rhs/dot_general | solution.py:55
  236.8 125.9 %psum.7 = f32[2,5]{1,0:T(2,128)S(1)} all-reduce(f32[2,5]{1,0:T(2,128)S(1)} %maximum_negate_fusion), channel_id=1, replica_groups=mesh['seq'=16,'head'=4,'dp'=4] {'seq','dp'}, use_global_device_ids=true, to_apply=%region_10.11 | all-reduce | flops 10 | bytes 80 | tf_op jit(solution)/shard_map/psum | solution.py:160
  366.3 4.0 all-to-all-start.4
  372.2 4.3 %all-to-all-done.4 = bf16[4,32,640]{2,1,0:T(8,128)(2,1)S(1)} async-done(((bf16[4,32,640]{2,1,0:T(8,128)(2,1)}), bf16[4,32,640]{2,1,0:T(8,128)(2,1)S(1)}, u32[]{:S(2)}, u32[]{:S(2)}) %all-to-all-start.4) | async-done | bytes 163872 | tf_op jit(solution)/shard_map/all_to_all | solution.py:146
  382.4 4.0 all-to-all-done.5
  391.3 4.5 %all-to-all-done.6 = bf16[4,32,640]{2,1,0:T(8,128)(2,1)S(1)} async-done(((bf16[4,32,640]{2,1,0:T(8,128)(2,1)}), bf16[4,32,640]{2,1,0:T(8,128)(2,1)S(1)}, u32[]{:S(2)}, u32[]{:S(2)}) %all-to-all-start.6) | async-done | bytes 163872 | tf_op jit(solution)/shard_map/all_to_all | solution.py:156
  (101 shorter events, 63.8 us)
Async XLA Ops:
  7.2 143.5 %copy-start = (s32[1,4096]{1,0:T(1,128)S(1)}, s32[1,4096]{1,0:T(1,128)}, u32[]{:S(2)}) copy-start(s32[1,4096]{1,0:T(1,128)} %param.23) | copy-start | bytes 49156
  7.2 35.2 %copy-start.9 = (bf16[1,32,2560]{2,1,0:T(8,128)(2,1)S(1)}, bf16[1,32,2560]{2,1,0:T(8,128)(2,1)}, u32[]{:S(2)}) copy-start(bf16[1,32,2560]{2,1,0:T(8,128)(2,1)} %param.15) | copy-start | bytes 491524
  7.2 40.7 %copy-start.10 = (f32[2,5]{1,0:T(2,128)S(1)}, f32[2,5]{1,0:T(2,128)}, u32[]{:S(2)}) copy-start(f32[2,5]{1,0:T(2,128)} %param.20) | copy-start | bytes 124
  7.2 53.0 %all-gather.7.cloned.1.call-start = ((), (), s32[]{:S(2)}) async-start(), calls=%async_computation.9 | async-start | bytes 2785280 | tf_op jit(solution)/shard_map/all_gather | solution.py:104
  18.7 82.3 %all-gather.9.cloned.1.call-start = ((), (), s32[]{:S(2)}) async-start(), calls=%async_computation.10 | async-start | bytes 2785280 | tf_op jit(solution)/shard_map/all_gather | solution.py:105
  28.9 123.4 %all-gather.11.cloned.1.call-start = ((), (), s32[]{:S(2)}) async-start(), calls=%async_computation.13 | async-start | bytes 2785280 | tf_op jit(solution)/shard_map/all_gather | solution.py:162
  32.4 10.8 %all-to-all-start = ((bf16[32,4,640]{2,0,1:T(8,128)(2,1)}), bf16[32,4,640]{2,0,1:T(8,128)(2,1)S(1)}, u32[]{:S(2)}, u32[]{:S(2)}) async-start(bf16[32,4,640]{2,0,1:T(8,128)(2,1)} %copy.116), calls=%async_computation | async-start | bytes 327680 | tf_op jit(solution)/shard_map/all_to_all | solution.py:96
  35.7 153.2 %all-gather.13.cloned.1.call-start = ((), (), s32[]{:S(2)}) async-start(), calls=%async_computation.14 | async-start | bytes 2785280 | tf_op jit(solution)/shard_map/all_gather | solution.py:163
  43.2 10.9 %all-to-all-start.2 = ((bf16[32,4,640]{2,0,1:T(8,128)(2,1)}), bf16[32,4,640]{2,0,1:T(8,128)(2,1)S(1)}, u32[]{:S(2)}, u32[]{:S(2)}) async-start(bf16[32,4,640]{2,0,1:T(8,128)(2,1)} %copy.121), calls=%async_computation.2 | async-start | bytes 327680 | tf_op jit(solution)/shard_map/all_to_all | solution.py:99
  47.9 322.5 %reduce-scatter.3.cloned.1.call-start = ((), (), s32[]{:S(2)}) async-start(), calls=%async_computation.11 | async-start | bytes 11141120 | tf_op jit(solution)/shard_map/reduce_scatter | solution.py:131
  63.2 45.8 %copy-start.3 = (bf16[2048,640]{0,1:T(8,128)(2,1)}, bf16[2048,640]{0,1:T(8,128)(2,1)S(1)}, u32[]{:S(2)}) copy-start(bf16[2048,640]{0,1:T(8,128)(2,1)S(1)} %copy.118) | copy-start | bytes 7864324
  109.0 2.7 copy-start.4
  109.0 3.6 copy-start.7
  112.7 1.3 copy-start.5
  112.7 1.6 copy-start.6
  148.4 232.9 %reduce-scatter.5.cloned.1.call-start = ((), (), s32[]{:S(2)}) async-start(), calls=%async_computation.12 | async-start | bytes 11141120 | tf_op jit(solution)/shard_map/reduce_scatter | solution.py:193
  188.9 6.1 %slice-start = ((s8[10485760]{0:T(1024)(128)(4,1)}), s8[4194304]{0:T(1024)(128)(4,1)S(1)}, s32[]{:S(2)}) async-start(s8[10485760]{0:T(1024)(128)(4,1)} %bitcast.80), calls=%async_computation.15 | async-start | bytes 8388608
  188.9 7.3 %slice-start.1 = ((s8[10485760]{0:T(1024)(128)(4,1)}), s8[4194304]{0:T(1024)(128)(4,1)S(1)}, s32[]{:S(2)}) async-start(s8[10485760]{0:T(1024)(128)(4,1)} %bitcast.80), calls=%async_computation.16 | async-start | bytes 8388608
  188.9 7.9 %slice-start.2 = ((s8[10485760]{0:T(1024)(128)(4,1)}), s8[2097152]{0:T(1024)(128)(4,1)S(1)}, s32[]{:S(2)}) async-start(s8[10485760]{0:T(1024)(128)(4,1)} %bitcast.80), calls=%async_computation.17 | async-start | bytes 4194304
  198.6 4.0 copy-start.2
  236.8 159.8 %copy-start.1 = (s32[1,4096]{1,0:T(1,128)S(1)}, s32[1,4096]{1,0:T(1,128)}, u32[]{:S(2)}) copy-start(s32[1,4096]{1,0:T(1,128)} %param.23) | copy-start | bytes 49156
  366.3 10.2 %all-to-all-start.4 = ((bf16[4,32,640]{2,1,0:T(8,128)(2,1)}), bf16[4,32,640]{2,1,0:T(8,128)(2,1)S(1)}, u32[]{:S(2)}, u32[]{:S(2)}) async-start(bf16[4,32,640]{2,1,0:T(8,128)(2,1)} %convert_element_type.95), calls=%async_computation.4 | async-start | bytes 327680 | tf_op jit(solution)/shard_map/all_to_all | solution.py:146
  376.5 9.8 %all-to-all-start.5 = ((bf16[4,32,640]{2,1,0:T(8,128)(2,1)}), bf16[4,32,640]{2,1,0:T(8,128)(2,1)S(1)}, u32[]{:S(2)}, u32[]{:S(2)}) async-start(bf16[4,32,640]{2,1,0:T(8,128)(2,1)} %bitcast.21), calls=%async_computation.6 | async-start | bytes 327680 | tf_op jit(solution)/shard_map/all_to_all | solution.py:153
  386.4 9.5 %all-to-all-start.6 = ((bf16[4,32,640]{2,1,0:T(8,128)(2,1)}), bf16[4,32,640]{2,1,0:T(8,128)(2,1)S(1)}, u32[]{:S(2)}, u32[]{:S(2)}) async-start(bf16[4,32,640]{2,1,0:T(8,128)(2,1)} %bitcast.23), calls=%async_computation.7 | async-start | bytes 327680 | tf_op jit(solution)/shard_map/all_to_all | solution.py:156
  (1 other events, 1.0 us)
Sparse Core Ops, SparseCore 0:
  18.8 41.3 all-gather.6
  62.0 38.8 all-gather.8
  103.3 41.4 all-gather.10
  146.9 41.9 all-gather.12
  191.3 73.7 reduce-scatter.2
  267.5 74.0 reduce-scatter.4
where the time goes:
time: 408 us; the launch traced here: 403 us
  blocking collectives  145 us (36%)
  waiting for transfers between devices  89.3 us (22%)
  local copies, waits for them, and re-layouts  52.1 us (13%)
  matrix products  50.7 us (12%)
  other arithmetic  32.3 us (8%)
  starting transfers between devices  19.2 us (5%)
  between operations  14.4 us (4%)
    psum x1, blocking collectives, local(): slope_grad = lax.psum(slope_local, ('seq', 'dp')) / patch_total  126 us
    all_gather x1, waiting for transfers between devices, local(): lax.all_gather(local_values, 'seq', axis=0, tiled=True)  37.7 us
    all_gather x1, waiting for transfers between devices, local(): lax.all_gather(memory_values[0], 'seq', axis=0, tiled=True)  27.1 us
    another operation x4, local copies, waits for them, and re-layouts, key_terms(): jnp.stack([key_grad.reshape(row_count, -1), value_grad.reshape(row_count,...  23.7 us
    another operation x2, other arithmetic, key_terms(): jnp.stack([key_grad.reshape(row_count, -1), value_grad.reshape(row_count,...  17.5 us
    dot_general x2, matrix products, key_terms(): jnp.einsum('chrk,crhs->khs', softmax_b, grad_rows, preferred_element_type...  15.4 us
    unnamed x33, local copies, waits for them, and re-layouts  10.6 us
    all_to_all x1, blocking collectives, local(): lax.all_to_all(self_keys[0], 'head', split_axis=1, concat_axis=0, tiled=T...  10.4 us
  transfers between devices with their start and end apart: 11, of which 7 were waited for; matrix products, arithmetic and copies ran while one was open for 31% of the time, Pallas kernels for 0%

commit v1 on v0

v1 whole, which is shorter than its diff:
```python
import functools
import jax
import jax.numpy as jnp
from jax import lax
from jax.experimental import pallas as pl
from jax.experimental.pallas import tpu as pltpu
from jax.sharding import PartitionSpec as P

MASK_FILL = -1e30
LOG2E = 1.4426950408889634
BF = jnp.bfloat16
F32 = jnp.float32

HEADS = 5
TEXT_TASKS = 10
TASKS = 16
BLK = 128
HS = 128
QB = 256
NARROW = 9


def vmem_call(body, out_shapes, **kw):
    return pl.pallas_call(
        body,
        out_shape=out_shapes,
        compiler_params=pltpu.CompilerParams(vmem_limit_bytes=48 * 2**20),
        **kw,
    )


def pack_self(q_ref, k_ref, v_ref, g_ref, out_ref):
    for a, ref in enumerate((q_ref, k_ref, v_ref, g_ref)):
        for x in range(4):
            for h in range(HEADS):
                c = (x * HEADS + h) * HS
                out_ref[x, h, a] = ref[0, :, c : c + HS]


def pack_tasks(tq_ref, mk_ref, mv_ref, tg_ref, self_ref, out_ref):
    for h in range(HEADS):
        cols = slice(h * HS, (h + 1) * HS)
        for j in range(2):
            t = 2 * h + j
            rows = slice(j * BLK, (j + 1) * BLK)
            out_ref[t, 0] = tq_ref[0, rows, cols]
            out_ref[t, 1] = mk_ref[0, :, cols]
            out_ref[t, 2] = mv_ref[0, :, cols]
            out_ref[t, 3] = tg_ref[0, rows, cols]
        for a in range(4):
            for x in range(4):
                out_ref[TEXT_TASKS + h, a, x * 32 : (x + 1) * 32] = self_ref[x, h, a]
    out_ref[TASKS - 1] = jnp.zeros((4, BLK, HS), BF)


def unpack_tasks(in_ref, tq_ref, mk_ref, mv_ref, self_ref):
    for h in range(HEADS):
        cols = slice(h * HS, (h + 1) * HS)
        for j in range(2):
            tq_ref[0, j * BLK : (j + 1) * BLK, cols] = in_ref[2 * h + j, 0]
        mk = in_ref[2 * h, 1].astype(F32) + in_ref[2 * h + 1, 1].astype(F32)
        mv = in_ref[2 * h, 2].astype(F32) + in_ref[2 * h + 1, 2].astype(F32)
        mk_ref[0, :, cols] = mk.astype(BF)
        mv_ref[0, :, cols] = mv.astype(BF)
        for a in range(3):
            for x in range(4):
                self_ref[x, h, a] = in_ref[TEXT_TASKS + h, a, x * 32 : (x + 1) * 32]


def unpack_self(in_ref, q_ref, k_ref, v_ref):
    for a, ref in enumerate((q_ref, k_ref, v_ref)):
        for x in range(4):
            for h in range(HEADS):
                c = (x * HEADS + h) * HS
                ref[0, :, c : c + HS] = in_ref[x, h, a]


def attend(
    win_ref, ka_ref, kb_ref, kp_ref, qi_ref, in_ref, out_ref, slope_ref,
    k_buf, v_buf, t_buf, d_buf, ds_buf, dk_acc, dv_acc,
):
    inv_root = HS ** (-0.5)
    blocks = TASKS * BLK // QB
    per = QB // BLK
    for s in range(TASKS):
        k_buf[s * BLK : (s + 1) * BLK] = in_ref[s, 1]
        v_buf[s * BLK : (s + 1) * BLK] = in_ref[s, 2]
    dk_acc[...] = jnp.zeros_like(dk_acc)
    dv_acc[...] = jnp.zeros_like(dv_acc)
    slope_ref[...] = jnp.zeros_like(slope_ref)
    nt = (((1,), (1,)), ((), ()))
    tn = (((0,), (0,)), ((), ()))

    def wide_lanes(tile):
        return jnp.concatenate([tile] * per, axis=1)

    def fold(x, op):
        return op(x.reshape(BLK // 8, 8, QB), axis=0)

    def work(b, start, tiles):
        q = jnp.concatenate([in_ref[per * b + i, 0] for i in range(per)], axis=0)
        g = jnp.concatenate([in_ref[per * b + i, 3] for i in range(per)], axis=0)
        at = pl.ds(pl.multiple_of(b * QB, QB), QB)
        qa, qb, qp = (qi_ref[i : i + 1, at] for i in range(3))

        def rows(t):
            return pl.ds(pl.multiple_of(start + t * BLK, BLK), BLK)

        top = jnp.full((8, QB), -jnp.inf, F32)
        for t in range(tiles):
            r = rows(t)
            s = lax.dot_general(k_buf[r], q, nt, preferred_element_type=F32)
            d_buf[t * BLK : (t + 1) * BLK] = lax.dot_general(
                v_buf[r], g, nt, preferred_element_type=F32
            )
            gap = jnp.abs(wide_lanes(ka_ref[r]) - qa) + jnp.abs(wide_lanes(kb_ref[r]) - qb)
            logit = jnp.where(
                wide_lanes(kp_ref[r]) == qp, s * (inv_root * LOG2E) - gap, MASK_FILL
            )
            t_buf[t * BLK : (t + 1) * BLK] = logit
            top = jnp.maximum(top, fold(logit, jnp.max))
        top = jnp.max(top, axis=0, keepdims=True)
        total = jnp.zeros((8, QB), F32)
        dot = jnp.zeros((8, QB), F32)
        for t in range(tiles):
            here = slice(t * BLK, (t + 1) * BLK)
            e = jnp.exp2(t_buf[here] - top)
            t_buf[here] = e
            total += fold(e, jnp.sum)
            dot += fold(e * d_buf[here], jnp.sum)
        inv = 1.0 / jnp.sum(total, axis=0, keepdims=True)
        delta = jnp.sum(dot, axis=0, keepdims=True) * inv
        sa = jnp.zeros((8, QB), F32)
        sb = jnp.zeros((8, QB), F32)
        for t in range(tiles):
            here = slice(t * BLK, (t + 1) * BLK)
            r = rows(t)
            p = t_buf[here] * inv
            ds = p * (d_buf[here] - delta)
            p_b = p.astype(BF)
            ds_b = ds.astype(BF)
            ds_buf[here] = ds_b
            sa += fold(ds * jnp.abs(wide_lanes(ka_ref[r]) - qa), jnp.sum)
            sb += fold(ds * jnp.abs(wide_lanes(kb_ref[r]) - qb), jnp.sum)
            dv_acc[r] += jnp.dot(p_b, g, preferred_element_type=F32)
            dk_acc[r] += jnp.dot(ds_b, q, preferred_element_type=F32)
        w = pl.ds(pl.multiple_of(start, BLK), tiles * BLK)
        dq = lax.dot_general(
            ds_buf[: tiles * BLK], k_buf[w], tn, preferred_element_type=F32
        )
        dq = (dq * inv_root).astype(BF)
        for i in range(per):
            out_ref[per * b + i, 0] = dq[i * BLK : (i + 1) * BLK]
        for row, v in ((0, sa), (1, sb)):
            v = jnp.sum(v, axis=0, keepdims=True)
            slope_ref[row : row + 1] += sum(v[:, i * BLK : (i + 1) * BLK] for i in range(per))

    def step(b, _):
        wide = win_ref[1, b]

        @pl.when(wide == 0)
        def _():
            work(b, win_ref[0, b] * BLK, NARROW)

        @pl.when(wide != 0)
        def _():
            work(b, 0, TASKS)

        return 0

    lax.fori_loop(0, blocks, step, 0)
    for s in range(TASKS):
        here = slice(s * BLK, (s + 1) * BLK)
        out_ref[s, 1] = (dk_acc[here] * inv_root).astype(BF)
        out_ref[s, 2] = dv_acc[here].astype(BF)


def local(
    self_queries, self_keys, self_values, self_cotangent,
    text_queries, memory_keys, memory_values, text_cotangent,
    slopes, page_counts, page_cols, text_page,
):
    patches = TASKS * BLK
    sds = jax.ShapeDtypeStruct
    task = lax.axis_index("seq")
    is_text = task < TEXT_TASKS

    counts, widths = page_counts[0], page_cols[0]
    ends = [counts[0]]
    for i in range(1, 4):
        ends.append(ends[-1] + counts[i])
    starts = [jnp.int32(0)] + ends[:-1]

    def by_page(ids, per_page):
        out = jnp.broadcast_to(per_page[3], ids.shape)
        for i in (2, 1, 0):
            out = jnp.where(ids == i, per_page[i], out)
        return out

    def layout(pos):
        ids = sum((pos >= e).astype(jnp.int32) for e in ends[:3])
        width = by_page(ids, [widths[i] for i in range(4)])
        off = pos - by_page(ids, starts)
        row = off // width
        return ids, row.astype(F32), (off - row * width).astype(F32)

    own = jnp.clip(task - TEXT_TASKS, 0, HEADS - 1)
    slope = jnp.where(is_text, 0.0, lax.dynamic_slice_in_dim(slopes, own, 1, 1)[:, 0])
    sa, sb = slope[0] * LOG2E, slope[1] * LOG2E
    key_id, key_row, key_col = layout(
        lax.broadcasted_iota(jnp.int32, (patches, BLK), 0)
    )
    pos_id, pos_row, pos_col = layout(jnp.arange(patches, dtype=jnp.int32))
    halves = text_page[0].reshape(TASKS, 2, BLK)
    text_id = lax.dynamic_index_in_dim(halves, task % 2, 1, keepdims=False).reshape(-1)
    q_id = jnp.where(is_text, text_id, pos_id)
    q_info = jnp.stack([pos_row * sa, pos_col * sb, q_id.astype(F32)])
    q_info = jnp.concatenate([q_info, jnp.zeros((5, patches), F32)])
    blocks = q_id.reshape(-1, QB)
    low = jnp.minimum(by_page(blocks[:, 0], starts) // BLK, TASKS - NARROW)
    wide = by_page(blocks[:, -1], ends) > (low + NARROW) * BLK
    window = jnp.stack([low, wide.astype(jnp.int32)])

    by_head = vmem_call(pack_self, sds((4, HEADS, 4, 32, HS), BF))(
        self_queries, self_keys, self_values, self_cotangent
    )
    by_head = lax.all_to_all(by_head, "head", split_axis=0, concat_axis=0, tiled=True)
    sent = vmem_call(pack_tasks, sds((TASKS, 4, BLK, HS), BF))(
        text_queries, memory_keys, memory_values, text_cotangent, by_head
    )
    held = lax.all_to_all(sent, "seq", split_axis=0, concat_axis=0, tiled=True)

    vm = pl.BlockSpec(memory_space=pltpu.VMEM)
    back, slope_part = vmem_call(
        attend,
        (sds((TASKS, 3, BLK, HS), BF), sds((8, BLK), F32)),
        in_specs=[pl.BlockSpec(memory_space=pltpu.SMEM)] + [vm] * 5,
        scratch_shapes=[
            pltpu.VMEM((patches, HS), BF),
            pltpu.VMEM((patches, HS), BF),
            pltpu.VMEM((patches, QB), F32),
            pltpu.VMEM((patches, QB), F32),
            pltpu.VMEM((patches, QB), BF),
            pltpu.VMEM((patches, HS), F32),
            pltpu.VMEM((patches, HS), F32),
        ],
    )(window, key_row * sa, key_col * sb, key_id.astype(F32), q_info, held)

    slope_sum = jnp.sum(slope_part[:2], axis=1) / jnp.where(
        is_text, 1.0, slope * LOG2E
    )
    slope_all = lax.all_gather(slope_sum, ("seq", "dp"), axis=0)
    slope_all = slope_all.reshape(TASKS, -1, 2)[TEXT_TASKS : TEXT_TASKS + HEADS]
    slope_grad = -jnp.sum(slope_all, axis=1).T / patches

    back = lax.all_to_all(back, "seq", split_axis=0, concat_axis=0, tiled=True)
    text_dq, mem_dk, mem_dv, self_out = vmem_call(
        unpack_tasks,
        (
            sds(text_queries.shape, BF),
            sds(memory_keys.shape, BF),
            sds(memory_values.shape, BF),
            sds((4, HEADS, 3, 32, HS), BF),
        ),
    )(back)
    self_out = lax.all_to_all(self_out, "head", split_axis=0, concat_axis=0, tiled=True)
    shape = sds(self_queries.shape, BF)
    self_dq, self_dk, self_dv = vmem_call(unpack_self, (shape, shape, shape))(self_out)
    return self_dq, self_dk, self_dv, slope_grad, text_dq, mem_dk, mem_dv


def solution(mesh):
    rows = P("dp", ("seq", "head"), None)
    cols = P("dp", "seq", "head")
    in_specs = (rows,) * 4 + (cols,) * 4 + (P(None, "head"),) + (P("dp", None),) * 3
    out_specs = (rows,) * 3 + (P(None, "head"),) + (cols,) * 3
    return jax.shard_map(local, mesh=mesh, in_specs=in_specs, out_specs=out_specs, check_vma=False)
```

time: 408 us -> 214 us (0.52)
  blocking collectives: 145 us -> 78 us
  matrix products: 50.7 us -> 0 us
  local copies, waits for them, and re-layouts: 52.1 us -> 7.69 us
  waiting for transfers between devices: 89.3 us -> 57.1 us
  Pallas kernels: 0 us -> 23.8 us
  between operations: 14.4 us -> 4.8 us
  other arithmetic: 32.3 us -> 24.2 us
    psum x1 -> x0, blocking collectives: 126 us -> none  [local(): slope_grad = lax.psum(slope_local, ('seq', 'dp')) / patch_total]
    all_gather x4 -> x0, waiting for transfers between devices: 70.7 us -> none  [the longest x1 37.7 us: local(): lax.all_gather(local_values, 'seq', axis=0, tiled=True)]
    all_gather x0 -> x1, blocking collectives: none -> 63.1 us  [local(): slope_all = lax.all_gather(slope_sum, ('seq', 'dp'), axis=0)]
    dot_general x9 -> x0, matrix products: 41.2 us -> none  [the longest x2 15.4 us: key_terms(): jnp.einsum('chrk,crhs->khs', softmax_b, grad_rows, preferred_element_type...]
    all_to_all x5 -> x3, waiting for transfers between devices: 18.5 us -> 57.1 us  [the longest x1 37.7 us: local(): back = lax.all_to_all(back, 'seq', split_axis=0, concat_axis=0, tiled=True)]
    pallas_call x0 -> x5, Pallas kernels: none -> 23.8 us  [the longest x1 20.2 us: local(): vmem_call(attend, (sds((TASKS, 3, BLK, HS), BF), sds((8, BLK), F32)), in_...]
    another operation x4 -> x0, local copies, waits for them, and re-layouts: 23.7 us -> none  [key_terms(): jnp.stack([key_grad.reshape(row_count, -1), value_grad.reshape(row_count,...]
    another operation x5 -> x1, other arithmetic: 20.6 us -> 0.01 us  [local(): window = jnp.stack([low, wide.astype(jnp.int32)])]
  transfers between devices with their start and end apart: 11 -> 3, of which waited for: 7 -> 2; matrix products, arithmetic and copies ran while one was open for 31% -> 13% of each run, Pallas kernels for 0% -> 0%
where the time goes in v1:
time: 214 us; the launch traced here: 213 us
  blocking collectives  78 us (36%)
  waiting for transfers between devices  57.1 us (27%)
  other arithmetic  24.2 us (11%)
  Pallas kernels  23.8 us (11%)
  starting transfers between devices  17 us (8%)
  local copies, waits for them, and re-layouts  7.69 us (4%)
  between operations  4.8 us (2%)
    all_gather x1, blocking collectives, local(): slope_all = lax.all_gather(slope_sum, ('seq', 'dp'), axis=0)  63.1 us
    all_to_all x1, waiting for transfers between devices, local(): back = lax.all_to_all(back, 'seq', split_axis=0, concat_axis=0, tiled=True)  37.7 us
    pallas_call x1, Pallas kernels, local(): vmem_call(attend, (sds((TASKS, 3, BLK, HS), BF), sds((8, BLK), F32)), in_...  20.2 us
    all_to_all x1, waiting for transfers between devices, local(): held = lax.all_to_all(sent, 'seq', split_axis=0, concat_axis=0, tiled=True)  19.4 us
    all_to_all x1, blocking collectives, local(): lax.all_to_all(by_head, 'head', split_axis=0, concat_axis=0, tiled=True)  15 us
    mul x1, other arithmetic, local(): key_col * sb  14.3 us
    all_to_all x1, starting transfers between devices, local(): held = lax.all_to_all(sent, 'seq', split_axis=0, concat_axis=0, tiled=True)  8.76 us
    unnamed x27, local copies, waits for them, and re-layouts  5.58 us
  transfers between devices with their start and end apart: 3, of which 2 were waited for; matrix products, arithmetic and copies ran while one was open for 13% of the time, Pallas kernels for 0%

profile of v1, /device:TPU:8, one launch (start us, length us, event | category | flops | bytes accessed | tf_op | source)
XLA Modules:
  0.0 212.6 jit_solution(4512902572708281033)
XLA Ops:
  0.7 1.0 copy-done.5
  1.7 0.9 copy-done.6
  2.6 0.9 copy-done.7
  3.5 0.9 copy-done.8
  4.5 15.0 %all_to_all.20.self_ref = bf16[4,5,4,32,128]{4,3,2,1,0:T(8,128)(2,1)S(1)} all-to-all(bf16[4,5,4,32,128]{4,3,2,1,0:T(8,128)(2,1)S(1)} %shard_map.171), channel_id=1, replica_groups=mesh['seq'=16,'head'=4,'dp'=4] {'head'}, dimensions={0} | all-to-all | bytes 1310720 | tf_op jit(solution)/shard_map/all_to_all | solution.py:227
  19.5 1.6 shard_map.172
  21.1 8.8 %all-to-all-start.1 = ((bf16[16,4,128,128]{3,2,1,0:T(8,128)(2,1)}), bf16[16,4,128,128]{3,2,1,0:T(8,128)(2,1)}, u32[]{:S(2)}, u32[]{:S(2)}) async-start(bf16[16,4,128,128]{3,2,1,0:T(8,128)(2,1)} %shard_map.172), calls=%async_computation.1 | async-start | bytes 4194304 | tf_op jit(solution)/shard_map/all_to_all | solution.py:231
  35.1 0.7 fusion.1
  35.9 0.7 add_select_fusion.1
  36.6 0.8 select_reduce_fusion.1
  37.5 0.7 fusion.7
  38.1 0.7 fusion.5
  39.4 1.9 broadcast_select_fusion.1
  41.4 4.0 %convert_multiply_fusion.2 = (f32[1,2048]{1,0:T(1,128)S(1)}, f32[1,2048]{1,0:T(1,128)S(1)}) fusion(f32[]{:T(128)} %bitcast.10, s32[]{:T(128)S(6)} %add.111, s32[]{:T(128)S(6)} %add.109, s32[]{:T(128)} %bitcast.1, s32[]{:T(128)} %bitcast.8, s32[]{:T(128)} %bitcast.7, s32[]{:T(128)} %bitcast.6, s32[]{:T(128)} %bitcast.5, f32[]{:T(128)} %bitcast.9), kind=kLoop, calls=%fused_computation.24 | loop fusion | flops 67584 | bytes 16420 | tf_op jit(solution)/shard_map/mul | solution.py:217
  45.4 14.3 %convert_multiply_fusion = (f32[2048,128]{1,0:T(8,128)S(1)}, f32[2048,128]{1,0:T(8,128)S(1)}) fusion(f32[]{:T(128)} %bitcast.10, s32[2048]{0:T(1024)S(1)} %get-tuple-element.47, s32[]{:T(128)} %bitcast.6, s32[]{:T(128)} %bitcast.5, s32[2048]{0:T(1024)S(1)} %get-tuple-element.48, s32[]{:T(128)} %bitcast.1, pred[2048]{0:T(1024)(128)(4,1)S(1)} %get-tuple-element.45, ...), kind=kLoop, calls=%fused_computation.1 | loop fusion | flops 5242880 | bytes 2117652 | tf_op jit(solution)/shard_map/mul | solution.py:247
  59.7 19.4 %all-to-all-done.1.in_ref = bf16[16,4,128,128]{3,2,1,0:T(8,128)(2,1)} async-done(((bf16[16,4,128,128]{3,2,1,0:T(8,128)(2,1)}), bf16[16,4,128,128]{3,2,1,0:T(8,128)(2,1)}, u32[]{:S(2)}, u32[]{:S(2)}) %all-to-all-start.1) | async-done | bytes 2097184 | tf_op jit(solution)/shard_map/all_to_all | solution.py:231
  79.5 20.2 %shard_map.173 = (bf16[16,3,128,128]{3,2,1,0:T(8,128)(2,1)S(1)}, f32[8,128]{1,0:T(8,128)S(1)}) custom-call(s32[2,8]{1,0:T(2,128)S(1)} %pad_add_fusion.win_ref, f32[2048,128]{1,0:T(8,128)S(1)} %get-tuple-element.32.ka_ref, f32[2048,128]{1,0:T(8,128)S(1)} %get-tuple-element.31.kb_ref, f32[2048,128]{1,0:T(8,128)S(1)} %iota.81.kp_ref, ...), custom_call_target="tpu_custom_call" | custom-call | tf_op jit(solution)/shard_map/pallas_call | solution.py:234
  99.6 1.2 copy-done
  100.8 4.7 %all-to-all-start.2 = ((bf16[16,3,128,128]{3,2,1,0:T(8,128)(2,1)}), bf16[16,3,128,128]{3,2,1,0:T(8,128)(2,1)S(1)}, u32[]{:S(2)}, u32[]{:S(2)}) async-start(bf16[16,3,128,128]{3,2,1,0:T(8,128)(2,1)} %copy-done), calls=%async_computation.2 | async-start | bytes 3145728 | tf_op jit(solution)/shard_map/all_to_all | solution.py:256
  105.7 37.7 %all-to-all-done.2.in_ref = bf16[16,3,128,128]{3,2,1,0:T(8,128)(2,1)S(1)} async-done(((bf16[16,3,128,128]{3,2,1,0:T(8,128)(2,1)}), bf16[16,3,128,128]{3,2,1,0:T(8,128)(2,1)S(1)}, u32[]{:S(2)}, u32[]{:S(2)}) %all-to-all-start.2) | async-done | bytes 1572896 | tf_op jit(solution)/shard_map/all_to_all | solution.py:256
  143.4 1.1 shard_map.174
  144.5 3.5 %all-to-all-start.3 = ((bf16[4,5,3,32,128]{4,3,2,1,0:T(8,128)(2,1)}), bf16[4,5,3,32,128]{4,3,2,1,0:T(8,128)(2,1)S(1)}, u32[]{:S(2)}, u32[]{:S(2)}) async-start(bf16[4,5,3,32,128]{4,3,2,1,0:T(8,128)(2,1)} %get-tuple-element.17), calls=%async_computation.3 | async-start | bytes 983040 | tf_op jit(solution)/shard_map/all_to_all | solution.py:266
  148.0 63.1 %all-gather = f32[64,1,2]{2,1,0:T(1,128)S(1)} all-gather(f32[1,1,2]{2,1,0:T(1,128)S(1)} %fusion.13), channel_id=1, replica_groups=mesh['seq'=16,'head'=4,'dp'=4] {'seq','dp'}, dimensions={0}, use_global_device_ids=true | all-gather | bytes 520 | tf_op jit(solution)/shard_map/all_gather | solution.py:252
  211.8 0.9 shard_map.175
  (41 shorter events, 3.4 us)
Async XLA Ops:
  0.6 18.9 %copy-start.2 = (bf16[1,256,640]{2,1,0:T(8,128)(2,1)S(1)}, bf16[1,256,640]{2,1,0:T(8,128)(2,1)}, u32[]{:S(2)}) copy-start(bf16[1,256,640]{2,1,0:T(8,128)(2,1)} %tg_ref.1) | copy-start | bytes 983044
  0.6 18.9 %copy-start.4 = (bf16[1,128,640]{2,1,0:T(8,128)(2,1)S(1)}, bf16[1,128,640]{2,1,0:T(8,128)(2,1)}, u32[]{:S(2)}) copy-start(bf16[1,128,640]{2,1,0:T(8,128)(2,1)} %mv_ref.1) | copy-start | bytes 491524
  0.7 18.9 %copy-start.3 = (bf16[1,128,640]{2,1,0:T(8,128)(2,1)S(1)}, bf16[1,128,640]{2,1,0:T(8,128)(2,1)}, u32[]{:S(2)}) copy-start(bf16[1,128,640]{2,1,0:T(8,128)(2,1)} %mk_ref.1) | copy-start | bytes 491524
  0.7 18.9 %copy-start.1 = (bf16[1,256,640]{2,1,0:T(8,128)(2,1)S(1)}, bf16[1,256,640]{2,1,0:T(8,128)(2,1)}, u32[]{:S(2)}) copy-start(bf16[1,256,640]{2,1,0:T(8,128)(2,1)} %tq_ref.1) | copy-start | bytes 983044
  0.7 1.0 copy-start.5
  1.7 0.9 copy-start.6
  2.6 0.9 copy-start.7
  3.5 0.9 copy-start.8
  21.1 8.8 %copy-start.12 = (f32[2,5]{1,0:T(2,128)S(1)}, f32[2,5]{1,0:T(2,128)}, u32[]{:S(2)}) copy-start(f32[2,5]{1,0:T(2,128)} %param.20) | copy-start | bytes 124
  21.1 10.8 %copy-start.9 = (s32[1,4]{1,0:T(1,128)S(1)}, s32[1,4]{1,0:T(1,128)}, u32[]{:S(2)}) copy-start(s32[1,4]{1,0:T(1,128)} %param.21) | copy-start | bytes 52
  21.1 14.0 %copy-start.11 = (s32[1,4096]{1,0:T(1,128)S(1)}, s32[1,4096]{1,0:T(1,128)}, u32[]{:S(2)}) copy-start(s32[1,4096]{1,0:T(1,128)} %param.23) | copy-start | bytes 49156
  21.1 17.7 %copy-start.10 = (s32[1,4]{1,0:T(1,128)S(1)}, s32[1,4]{1,0:T(1,128)}, u32[]{:S(2)}) copy-start(s32[1,4]{1,0:T(1,128)} %param.22) | copy-start | bytes 52
  21.1 58.0 %all-to-all-start.1 = ((bf16[16,4,128,128]{3,2,1,0:T(8,128)(2,1)}), bf16[16,4,128,128]{3,2,1,0:T(8,128)(2,1)}, u32[]{:S(2)}, u32[]{:S(2)}) async-start(bf16[16,4,128,128]{3,2,1,0:T(8,128)(2,1)} %shard_map.172), calls=%async_computation.1 | async-start | bytes 4194304 | tf_op jit(solution)/shard_map/all_to_all | solution.py:231
  99.6 1.2 copy-start
  100.8 42.6 %all-to-all-start.2 = ((bf16[16,3,128,128]{3,2,1,0:T(8,128)(2,1)}), bf16[16,3,128,128]{3,2,1,0:T(8,128)(2,1)S(1)}, u32[]{:S(2)}, u32[]{:S(2)}) async-start(bf16[16,3,128,128]{3,2,1,0:T(8,128)(2,1)} %copy-done), calls=%async_computation.2 | async-start | bytes 3145728 | tf_op jit(solution)/shard_map/all_to_all | solution.py:256
  144.5 67.2 %all-to-all-start.3 = ((bf16[4,5,3,32,128]{4,3,2,1,0:T(8,128)(2,1)}), bf16[4,5,3,32,128]{4,3,2,1,0:T(8,128)(2,1)S(1)}, u32[]{:S(2)}, u32[]{:S(2)}) async-start(bf16[4,5,3,32,128]{4,3,2,1,0:T(8,128)(2,1)} %get-tuple-element.17), calls=%async_computation.3 | async-start | bytes 983040 | tf_op jit(solution)/shard_map/all_to_all | solution.py:266

commit v2 on v1

--- a/solution.py
+++ b/solution.py
@@ -249,11 +249,18 @@
     slope_sum = jnp.sum(slope_part[:2], axis=1) / jnp.where(
         is_text, 1.0, slope * LOG2E
     )
-    slope_all = lax.all_gather(slope_sum, ("seq", "dp"), axis=0)
-    slope_all = slope_all.reshape(TASKS, -1, 2)[TEXT_TASKS : TEXT_TASKS + HEADS]
-    slope_grad = -jnp.sum(slope_all, axis=1).T / patches
+    mine = jnp.arange(HEADS) == task - TEXT_TASKS
+    slope_all = jnp.where(mine[None, :], slope_sum[:, None], 0.0)
+    for axis, size in (("dp", 4), ("seq", TASKS)):
+        gap = 1
+        while gap < size:
+            swap = [(i, i ^ gap) for i in range(size)]
+            slope_all = slope_all + lax.ppermute(slope_all, axis, swap)
+            gap *= 2
+    slope_grad = slope_all * (-1.0 / patches)
 
     back = lax.all_to_all(back, "seq", split_axis=0, concat_axis=0, tiled=True)
+    back, slope_grad = lax.optimization_barrier((back, slope_grad))
     text_dq, mem_dk, mem_dv, self_out = vmem_call(
         unpack_tasks,
         (

time: 214 us -> 170 us (0.79)
  blocking collectives: 78 us -> 25.3 us
  starting transfers between devices: 17 us -> 26.3 us
    all_gather x1 -> x0, blocking collectives: 63.1 us -> none  [local(): slope_all = lax.all_gather(slope_sum, ('seq', 'dp'), axis=0)]
    all_to_all x1, waiting for transfers between devices: 37.7 us -> 0.01 us  [local(): back = lax.all_to_all(back, 'seq', split_axis=0, concat_axis=0, tiled=True)]
    ppermute x0 -> x6, waiting for transfers between devices: none -> 37.3 us  [local(): slope_all = slope_all + lax.ppermute(slope_all, axis, swap)]
    ppermute x0 -> x6, starting transfers between devices: none -> 11.2 us  [local(): slope_all = slope_all + lax.ppermute(slope_all, axis, swap)]
    all_to_all x0 -> x1, blocking collectives: none -> 10.3 us  [local(): lax.all_to_all(self_out, 'head', split_axis=0, concat_axis=0, tiled=True)]
    all_to_all x1 -> x0, starting transfers between devices: 3.47 us -> none  [local(): lax.all_to_all(self_out, 'head', split_axis=0, concat_axis=0, tiled=True)]
  transfers between devices with their start and end apart: 3 -> 8, of which waited for: 2 -> 7; matrix products, arithmetic and copies ran while one was open for 13% -> 16% of each run, Pallas kernels for 0% -> 0%
where the time goes in v2:
time: 170 us
  waiting for transfers between devices  56.6 us (33%)
  starting transfers between devices  26.3 us (15%)
  blocking collectives  25.3 us (15%)
  Pallas kernels  24.8 us (15%)
  other arithmetic  24.8 us (15%)
  local copies, waits for them, and re-layouts  7.3 us (4%)
  between operations  4.8 us (3%)
    ppermute x6, waiting for transfers between devices, local(): slope_all = slope_all + lax.ppermute(slope_all, axis, swap)  37.3 us
    pallas_call x1, Pallas kernels, local(): vmem_call(attend, (sds((TASKS, 3, BLK, HS), BF), sds((8, BLK), F32)), in_...  21.3 us
    all_to_all x1, waiting for transfers between devices, local(): held = lax.all_to_all(sent, 'seq', split_axis=0, concat_axis=0, tiled=True)  19.3 us
    all_to_all x1, blocking collectives, local(): lax.all_to_all(by_head, 'head', split_axis=0, concat_axis=0, tiled=True)  15 us
    mul x1, other arithmetic, local(): key_col * sb  14.3 us
    ppermute x6, starting transfers between devices, local(): slope_all = slope_all + lax.ppermute(slope_all, axis, swap)  11.2 us
    all_to_all x1, blocking collectives, local(): lax.all_to_all(self_out, 'head', split_axis=0, concat_axis=0, tiled=True)  10.3 us
    all_to_all x1, starting transfers between devices, local(): held = lax.all_to_all(sent, 'seq', split_axis=0, concat_axis=0, tiled=True)  8.75 us
  transfers between devices with their start and end apart: 8, of which 7 were waited for; matrix products, arithmetic and copies ran while one was open for 16% of the time, Pallas kernels for 0%

profile of v2, /device:TPU:8, one launch (start us, length us, event | category | flops | bytes accessed | tf_op | source)
XLA Modules:
  0.0 169.8 jit_solution(18270407095363009718)
XLA Ops:
  0.7 1.0 copy-done.6
  1.7 0.9 copy-done.7
  4.6 15.0 %all_to_all.20.self_ref = bf16[4,5,4,32,128]{4,3,2,1,0:T(8,128)(2,1)S(1)} all-to-all(bf16[4,5,4,32,128]{4,3,2,1,0:T(8,128)(2,1)S(1)} %shard_map.171), channel_id=1, replica_groups=mesh['seq'=16,'head'=4,'dp'=4] {'head'}, dimensions={0} | all-to-all | bytes 1310720 | tf_op jit(solution)/shard_map/all_to_all | solution.py:227
  19.5 1.6 shard_map.172
  21.1 8.8 %all-to-all-start.1 = ((bf16[16,4,128,128]{3,2,1,0:T(8,128)(2,1)}), bf16[16,4,128,128]{3,2,1,0:T(8,128)(2,1)}, u32[]{:S(2)}, u32[]{:S(2)}) async-start(bf16[16,4,128,128]{3,2,1,0:T(8,128)(2,1)} %shard_map.172), calls=%async_computation.1 | async-start | bytes 4194304 | tf_op jit(solution)/shard_map/all_to_all | solution.py:231
  39.4 1.9 %broadcast_select_fusion.1 = (s32[2048]{0:T(1024)S(1)}, s32[2048]{0:T(1024)S(1)}) fusion(s32[]{:T(128)} %bitcast.8, s32[]{:T(128)} %bitcast.7, s32[]{:T(128)S(6)} %add.129, s32[]{:T(128)S(6)} %add.127, s32[]{:T(128)} %bitcast.1), kind=kLoop, calls=%fused_computation.39 | loop fusion | flops 22528 | bytes 16404 | tf_op jit(solution)/shard_map/jit(_where)/select_n | solution.py:197
  41.4 4.0 %convert_multiply_fusion.2 = (f32[1,2048]{1,0:T(1,128)S(1)}, f32[1,2048]{1,0:T(1,128)S(1)}) fusion(f32[]{:T(128)} %bitcast.10, s32[]{:T(128)S(6)} %add.129, s32[]{:T(128)S(6)} %add.127, s32[]{:T(128)} %bitcast.1, s32[]{:T(128)} %bitcast.8, s32[]{:T(128)} %bitcast.7, s32[]{:T(128)} %bitcast.6, s32[]{:T(128)} %bitcast.5, f32[]{:T(128)} %bitcast.9), kind=kLoop, calls=%fused_computation.24 | loop fusion | flops 67584 | bytes 16420 | tf_op jit(solution)/shard_map/mul | solution.py:217
  45.4 14.3 %convert_multiply_fusion = (f32[2048,128]{1,0:T(8,128)S(1)}, f32[2048,128]{1,0:T(8,128)S(1)}) fusion(f32[]{:T(128)} %bitcast.10, s32[2048]{0:T(1024)S(1)} %get-tuple-element.49, s32[]{:T(128)} %bitcast.6, s32[]{:T(128)} %bitcast.5, s32[2048]{0:T(1024)S(1)} %get-tuple-element.50, s32[]{:T(128)} %bitcast.1, pred[2048]{0:T(1024)(128)(4,1)S(1)} %get-tuple-element.47, ...), kind=kLoop, calls=%fused_computation.1 | loop fusion | flops 5242880 | bytes 2117652 | tf_op jit(solution)/shard_map/mul | solution.py:247
  59.8 19.3 %all-to-all-done.1.in_ref = bf16[16,4,128,128]{3,2,1,0:T(8,128)(2,1)} async-done(((bf16[16,4,128,128]{3,2,1,0:T(8,128)(2,1)}), bf16[16,4,128,128]{3,2,1,0:T(8,128)(2,1)}, u32[]{:S(2)}, u32[]{:S(2)}) %all-to-all-start.1) | async-done | bytes 2097184 | tf_op jit(solution)/shard_map/all_to_all | solution.py:231
  79.4 21.3 %shard_map.173 = (bf16[16,3,128,128]{3,2,1,0:T(8,128)(2,1)S(1)}, f32[8,128]{1,0:T(8,128)S(1)}) custom-call(s32[2,8]{1,0:T(2,128)S(1)} %pad_add_fusion.win_ref, f32[2048,128]{1,0:T(8,128)S(1)} %get-tuple-element.34.ka_ref, f32[2048,128]{1,0:T(8,128)S(1)} %get-tuple-element.33.kb_ref, f32[2048,128]{1,0:T(8,128)S(1)} %iota.86.kp_ref, ...), custom_call_target="tpu_custom_call" | custom-call | tf_op jit(solution)/shard_map/pallas_call | solution.py:234
  100.8 1.2 copy-done.1
  102.0 6.3 %all-to-all-start.2 = ((bf16[16,3,128,128]{3,2,1,0:T(8,128)(2,1)}), bf16[16,3,128,128]{3,2,1,0:T(8,128)(2,1)S(1)}, u32[]{:S(2)}, u32[]{:S(2)}) async-start(bf16[16,3,128,128]{3,2,1,0:T(8,128)(2,1)} %copy-done.1), calls=%async_computation.2 | async-start | bytes 3145728 | tf_op jit(solution)/shard_map/all_to_all | solution.py:262
  108.6 3.6 %collective-permute-done = f32[2,5]{1,0:T(2,128)S(1)} collective-permute-done((f32[2,5]{1,0:T(2,128)S(1)}, f32[2,5]{1,0:T(2,128)S(1)}, u32[]{:S(2)}, u32[]{:S(2)}) %collective-permute-start) | collective-permute-done | bytes 72 | tf_op jit(solution)/shard_map/ppermute | solution.py:258
  112.2 2.3 %collective-permute-start.1 = (f32[2,5]{1,0:T(2,128)S(1)}, f32[2,5]{1,0:T(2,128)S(1)}, u32[]{:S(2)}, u32[]{:S(2)}) collective-permute-start(f32[2,5]{1,0:T(2,128)S(1)} %fusion.15), channel_id=1, source_target_pairs={{0,2},{1,3},{2,0},{3,1},{4,6},{5,7},{6,4},{7,5},{8,10},{9,11},{10,... | collective-permute-start | bytes 128 | tf_op jit(solution)/shard_map/ppermute | solution.py:258
  114.5 2.8 %collective-permute-done.1 = f32[2,5]{1,0:T(2,128)S(1)} collective-permute-done((f32[2,5]{1,0:T(2,128)S(1)}, f32[2,5]{1,0:T(2,128)S(1)}, u32[]{:S(2)}, u32[]{:S(2)}) %collective-permute-start.1) | collective-permute-done | bytes 72 | tf_op jit(solution)/shard_map/ppermute | solution.py:258
  117.3 1.1 collective-permute-done.2
  118.5 1.9 %collective-permute-start.3 = (f32[2,5]{1,0:T(2,128)S(1)}, f32[2,5]{1,0:T(2,128)S(1)}, u32[]{:S(2)}, u32[]{:S(2)}) collective-permute-start(f32[2,5]{1,0:T(2,128)S(1)} %add.139), channel_id=1, source_target_pairs={{0,32},{16,48},{32,0},{48,16},{64,96},{80,112},{96,64},{112,80},{1... | collective-permute-start | bytes 128 | tf_op jit(solution)/shard_map/ppermute | solution.py:258
  120.4 24.9 %collective-permute-done.3 = f32[2,5]{1,0:T(2,128)S(1)} collective-permute-done((f32[2,5]{1,0:T(2,128)S(1)}, f32[2,5]{1,0:T(2,128)S(1)}, u32[]{:S(2)}, u32[]{:S(2)}) %collective-permute-start.3) | collective-permute-done | bytes 72 | tf_op jit(solution)/shard_map/ppermute | solution.py:258
  145.3 2.5 %collective-permute-start.4 = (f32[2,5]{1,0:T(2,128)S(1)}, f32[2,5]{1,0:T(2,128)S(1)}, u32[]{:S(2)}, u32[]{:S(2)}) collective-permute-start(f32[2,5]{1,0:T(2,128)S(1)} %add.140), channel_id=1, source_target_pairs={{0,64},{16,80},{32,96},{48,112},{64,0},{80,16},{96,32},{112,48},{1... | collective-permute-start | bytes 128 | tf_op jit(solution)/shard_map/ppermute | solution.py:258
  147.8 2.0 %collective-permute-done.4 = f32[2,5]{1,0:T(2,128)S(1)} collective-permute-done((f32[2,5]{1,0:T(2,128)S(1)}, f32[2,5]{1,0:T(2,128)S(1)}, u32[]{:S(2)}, u32[]{:S(2)}) %collective-permute-start.4) | collective-permute-done | bytes 72 | tf_op jit(solution)/shard_map/ppermute | solution.py:258
  149.7 4.4 %collective-permute-start.5 = (f32[2,5]{1,0:T(2,128)S(1)}, f32[2,5]{1,0:T(2,128)S(1)}, u32[]{:S(2)}, u32[]{:S(2)}) collective-permute-start(f32[2,5]{1,0:T(2,128)S(1)} %add.141), channel_id=1, source_target_pairs={{0,128},{16,144},{32,160},{48,176},{64,192},{80,208},{96,224},{112... | collective-permute-start | bytes 128 | tf_op jit(solution)/shard_map/ppermute | solution.py:258
  154.2 3.0 %collective-permute-done.5 = f32[2,5]{1,0:T(2,128)S(1)} collective-permute-done((f32[2,5]{1,0:T(2,128)S(1)}, f32[2,5]{1,0:T(2,128)S(1)}, u32[]{:S(2)}, u32[]{:S(2)}) %collective-permute-start.5) | collective-permute-done | bytes 72 | tf_op jit(solution)/shard_map/ppermute | solution.py:258
  157.8 0.9 shard_map.174
  158.7 10.3 %all_to_all.21.in_ref = bf16[4,5,3,32,128]{4,3,2,1,0:T(8,128)(2,1)S(1)} all-to-all(bf16[4,5,3,32,128]{4,3,2,1,0:T(8,128)(2,1)S(1)} %get-tuple-element.21), channel_id=1, replica_groups=mesh['seq'=16,'head'=4,'dp'=4] {'head'}, dimensions={0} | all-to-all | bytes 983040 | tf_op jit(solution)/shard_map/all_to_all | solution.py:273
  (57 shorter events, 9.7 us)
Async XLA Ops:
  0.6 29.3 %copy-start = (f32[2,5]{1,0:T(2,128)S(1)}, f32[2,5]{1,0:T(2,128)}, u32[]{:S(2)}) copy-start(f32[2,5]{1,0:T(2,128)} %param.20) | copy-start | bytes 124
  0.7 18.9 %copy-start.3 = (bf16[1,256,640]{2,1,0:T(8,128)(2,1)S(1)}, bf16[1,256,640]{2,1,0:T(8,128)(2,1)}, u32[]{:S(2)}) copy-start(bf16[1,256,640]{2,1,0:T(8,128)(2,1)} %tg_ref.1) | copy-start | bytes 983044
  0.7 18.9 %copy-start.5 = (bf16[1,128,640]{2,1,0:T(8,128)(2,1)S(1)}, bf16[1,128,640]{2,1,0:T(8,128)(2,1)}, u32[]{:S(2)}) copy-start(bf16[1,128,640]{2,1,0:T(8,128)(2,1)} %mv_ref.1) | copy-start | bytes 491524
  0.7 18.9 %copy-start.4 = (bf16[1,128,640]{2,1,0:T(8,128)(2,1)S(1)}, bf16[1,128,640]{2,1,0:T(8,128)(2,1)}, u32[]{:S(2)}) copy-start(bf16[1,128,640]{2,1,0:T(8,128)(2,1)} %mk_ref.1) | copy-start | bytes 491524
  0.7 18.9 %copy-start.2 = (bf16[1,256,640]{2,1,0:T(8,128)(2,1)S(1)}, bf16[1,256,640]{2,1,0:T(8,128)(2,1)}, u32[]{:S(2)}) copy-start(bf16[1,256,640]{2,1,0:T(8,128)(2,1)} %tq_ref.1) | copy-start | bytes 983044
  0.7 1.0 copy-start.6
  1.7 0.9 copy-start.7
  2.6 0.9 copy-start.8
  3.5 0.9 copy-start.9
  21.1 10.9 %copy-start.10 = (s32[1,4]{1,0:T(1,128)S(1)}, s32[1,4]{1,0:T(1,128)}, u32[]{:S(2)}) copy-start(s32[1,4]{1,0:T(1,128)} %param.21) | copy-start | bytes 52
  21.1 14.1 %copy-start.12 = (s32[1,4096]{1,0:T(1,128)S(1)}, s32[1,4096]{1,0:T(1,128)}, u32[]{:S(2)}) copy-start(s32[1,4096]{1,0:T(1,128)} %param.23) | copy-start | bytes 49156
  21.1 17.7 %copy-start.11 = (s32[1,4]{1,0:T(1,128)S(1)}, s32[1,4]{1,0:T(1,128)}, u32[]{:S(2)}) copy-start(s32[1,4]{1,0:T(1,128)} %param.22) | copy-start | bytes 52
  21.1 58.0 %all-to-all-start.1 = ((bf16[16,4,128,128]{3,2,1,0:T(8,128)(2,1)}), bf16[16,4,128,128]{3,2,1,0:T(8,128)(2,1)}, u32[]{:S(2)}, u32[]{:S(2)}) async-start(bf16[16,4,128,128]{3,2,1,0:T(8,128)(2,1)} %shard_map.172), calls=%async_computation.1 | async-start | bytes 4194304 | tf_op jit(solution)/shard_map/all_to_all | solution.py:231
  100.8 1.2 copy-start.1
  102.0 55.8 %all-to-all-start.2 = ((bf16[16,3,128,128]{3,2,1,0:T(8,128)(2,1)}), bf16[16,3,128,128]{3,2,1,0:T(8,128)(2,1)S(1)}, u32[]{:S(2)}, u32[]{:S(2)}) async-start(bf16[16,3,128,128]{3,2,1,0:T(8,128)(2,1)} %copy-done.1), calls=%async_computation.2 | async-start | bytes 3145728 | tf_op jit(solution)/shard_map/all_to_all | solution.py:262
  108.5 3.6 %collective-permute-start = (f32[2,5]{1,0:T(2,128)S(1)}, f32[2,5]{1,0:T(2,128)S(1)}, u32[]{:S(2)}, u32[]{:S(2)}) collective-permute-start(f32[2,5]{1,0:T(2,128)S(1)} %broadcast_select_fusion.3), channel_id=1, source_target_pairs={{0,1},{1,0},{2,3},{3,2},{4,5},{5,4},{6,7},{7,6},{8,9},{9,8},{10,11... | collective-permute-start | bytes 128 | tf_op jit(solution)/shard_map/ppermute | solution.py:258
  112.2 5.1 %collective-permute-start.1 = (f32[2,5]{1,0:T(2,128)S(1)}, f32[2,5]{1,0:T(2,128)S(1)}, u32[]{:S(2)}, u32[]{:S(2)}) collective-permute-start(f32[2,5]{1,0:T(2,128)S(1)} %fusion.15), channel_id=1, source_target_pairs={{0,2},{1,3},{2,0},{3,1},{4,6},{5,7},{6,4},{7,5},{8,10},{9,11},{10,... | collective-permute-start | bytes 128 | tf_op jit(solution)/shard_map/ppermute | solution.py:258
  117.3 1.1 collective-permute-start.2
  118.5 26.8 %collective-permute-start.3 = (f32[2,5]{1,0:T(2,128)S(1)}, f32[2,5]{1,0:T(2,128)S(1)}, u32[]{:S(2)}, u32[]{:S(2)}) collective-permute-start(f32[2,5]{1,0:T(2,128)S(1)} %add.139), channel_id=1, source_target_pairs={{0,32},{16,48},{32,0},{48,16},{64,96},{80,112},{96,64},{112,80},{1... | collective-permute-start | bytes 128 | tf_op jit(solution)/shard_map/ppermute | solution.py:258
  145.3 4.5 %collective-permute-start.4 = (f32[2,5]{1,0:T(2,128)S(1)}, f32[2,5]{1,0:T(2,128)S(1)}, u32[]{:S(2)}, u32[]{:S(2)}) collective-permute-start(f32[2,5]{1,0:T(2,128)S(1)} %add.140), channel_id=1, source_target_pairs={{0,64},{16,80},{32,96},{48,112},{64,0},{80,16},{96,32},{112,48},{1... | collective-permute-start | bytes 128 | tf_op jit(solution)/shard_map/ppermute | solution.py:258
  149.7 7.5 %collective-permute-start.5 = (f32[2,5]{1,0:T(2,128)S(1)}, f32[2,5]{1,0:T(2,128)S(1)}, u32[]{:S(2)}, u32[]{:S(2)}) collective-permute-start(f32[2,5]{1,0:T(2,128)S(1)} %add.141), channel_id=1, source_target_pairs={{0,128},{16,144},{32,160},{48,176},{64,192},{80,208},{96,224},{112... | collective-permute-start | bytes 128 | tf_op jit(solution)/shard_map/ppermute | solution.py:258

commit v3 on v1

--- a/solution.py
+++ b/solution.py
@@ -29,12 +29,16 @@
     )
 
 
-def pack_self(q_ref, k_ref, v_ref, g_ref, out_ref):
+def pack_self(q_ref, k_ref, v_ref, g_ref, out_ref, sems):
+    copies = []
+    width = HEADS * HS
     for a, ref in enumerate((q_ref, k_ref, v_ref, g_ref)):
         for x in range(4):
-            for h in range(HEADS):
-                c = (x * HEADS + h) * HS
-                out_ref[x, h, a] = ref[0, :, c : c + HS]
+            part = ref.at[0, :, pl.ds(x * width, width)]
+            copies.append(pltpu.make_async_copy(part, out_ref.at[x, a], sems.at[a, x]))
+            copies[-1].start()
+    for copy in copies:
+        copy.wait()
 
 
 def pack_tasks(tq_ref, mk_ref, mv_ref, tg_ref, self_ref, out_ref):
@@ -49,7 +53,7 @@
             out_ref[t, 3] = tg_ref[0, rows, cols]
         for a in range(4):
             for x in range(4):
-                out_ref[TEXT_TASKS + h, a, x * 32 : (x + 1) * 32] = self_ref[x, h, a]
+                out_ref[TEXT_TASKS + h, a, x * 32 : (x + 1) * 32] = self_ref[x, a, :, cols]
     out_ref[TASKS - 1] = jnp.zeros((4, BLK, HS), BF)
 
 
@@ -77,7 +81,7 @@
 
 def attend(
     win_ref, ka_ref, kb_ref, kp_ref, qi_ref, in_ref, out_ref, slope_ref,
-    k_buf, v_buf, t_buf, d_buf, ds_buf, dk_acc, dv_acc,
+    k_buf, v_buf, kt_buf, t_buf, d_buf, ds_buf, dk_acc, dv_acc,
 ):
     inv_root = HS ** (-0.5)
     blocks = TASKS * BLK // QB
@@ -85,6 +89,7 @@
     for s in range(TASKS):
         k_buf[s * BLK : (s + 1) * BLK] = in_ref[s, 1]
         v_buf[s * BLK : (s + 1) * BLK] = in_ref[s, 2]
+        kt_buf[s] = in_ref[s, 1].astype(F32).T.astype(BF)
     dk_acc[...] = jnp.zeros_like(dk_acc)
     dv_acc[...] = jnp.zeros_like(dv_acc)
     slope_ref[...] = jnp.zeros_like(slope_ref)
@@ -97,7 +102,8 @@
     def fold(x, op):
         return op(x.reshape(BLK // 8, 8, QB), axis=0)
 
-    def work(b, start, tiles):
+    def work(b, first, tiles):
+        start = first * BLK
         q = jnp.concatenate([in_ref[per * b + i, 0] for i in range(per)], axis=0)
         g = jnp.concatenate([in_ref[per * b + i, 3] for i in range(per)], axis=0)
         at = pl.ds(pl.multiple_of(b * QB, QB), QB)
@@ -125,17 +131,18 @@
         for t in range(tiles):
             here = slice(t * BLK, (t + 1) * BLK)
             e = jnp.exp2(t_buf[here] - top)
-            t_buf[here] = e
             total += fold(e, jnp.sum)
             dot += fold(e * d_buf[here], jnp.sum)
-        inv = 1.0 / jnp.sum(total, axis=0, keepdims=True)
+        total = jnp.sum(total, axis=0, keepdims=True)
+        inv = 1.0 / total
+        norm = top + jnp.log2(total)
         delta = jnp.sum(dot, axis=0, keepdims=True) * inv
         sa = jnp.zeros((8, QB), F32)
         sb = jnp.zeros((8, QB), F32)
         for t in range(tiles):
             here = slice(t * BLK, (t + 1) * BLK)
             r = rows(t)
-            p = t_buf[here] * inv
+            p = jnp.exp2(t_buf[here] - norm)
             ds = p * (d_buf[here] - delta)
             p_b = p.astype(BF)
             ds_b = ds.astype(BF)
@@ -144,10 +151,8 @@
             sb += fold(ds * jnp.abs(wide_lanes(kb_ref[r]) - qb), jnp.sum)
             dv_acc[r] += jnp.dot(p_b, g, preferred_element_type=F32)
             dk_acc[r] += jnp.dot(ds_b, q, preferred_element_type=F32)
-        w = pl.ds(pl.multiple_of(start, BLK), tiles * BLK)
-        dq = lax.dot_general(
-            ds_buf[: tiles * BLK], k_buf[w], tn, preferred_element_type=F32
-        )
+        kt = jnp.concatenate([kt_buf[first + t] for t in range(tiles)], axis=1)
+        dq = jnp.dot(kt, ds_buf[: tiles * BLK], preferred_element_type=F32).T
         dq = (dq * inv_root).astype(BF)
         for i in range(per):
             out_ref[per * b + i, 0] = dq[i * BLK : (i + 1) * BLK]
@@ -160,7 +165,7 @@
 
         @pl.when(wide == 0)
         def _():
-            work(b, win_ref[0, b] * BLK, NARROW)
+            work(b, win_ref[0, b], NARROW)
 
         @pl.when(wide != 0)
         def _():
@@ -221,9 +226,14 @@
     wide = by_page(blocks[:, -1], ends) > (low + NARROW) * BLK
     window = jnp.stack([low, wide.astype(jnp.int32)])
 
-    by_head = vmem_call(pack_self, sds((4, HEADS, 4, 32, HS), BF))(
-        self_queries, self_keys, self_values, self_cotangent
-    )
+    hbm = pl.BlockSpec(memory_space=pltpu.HBM)
+    by_head = pl.pallas_call(
+        pack_self,
+        out_shape=sds((4, 4, 32, HEADS * HS), BF),
+        in_specs=[hbm] * 4,
+        out_specs=hbm,
+        scratch_shapes=[pltpu.SemaphoreType.DMA((4, 4))],
+    )(self_queries, self_keys, self_values, self_cotangent)
     by_head = lax.all_to_all(by_head, "head", split_axis=0, concat_axis=0, tiled=True)
     sent = vmem_call(pack_tasks, sds((TASKS, 4, BLK, HS), BF))(
         text_queries, memory_keys, memory_values, text_cotangent, by_head
@@ -238,6 +248,7 @@
         scratch_shapes=[
             pltpu.VMEM((patches, HS), BF),
             pltpu.VMEM((patches, HS), BF),
+            pltpu.VMEM((TASKS, HS, BLK), BF),
             pltpu.VMEM((patches, QB), F32),
             pltpu.VMEM((patches, QB), F32),
             pltpu.VMEM((patches, QB), BF),
@@ -249,11 +260,20 @@
     slope_sum = jnp.sum(slope_part[:2], axis=1) / jnp.where(
         is_text, 1.0, slope * LOG2E
     )
-    slope_all = lax.all_gather(slope_sum, ("seq", "dp"), axis=0)
-    slope_all = slope_all.reshape(TASKS, -1, 2)[TEXT_TASKS : TEXT_TASKS + HEADS]
-    slope_grad = -jnp.sum(slope_all, axis=1).T / patches
-
+    mine = jnp.arange(HEADS) == task - TEXT_TASKS
+    slope_all = jnp.where(mine[None, :], slope_sum[:, None], 0.0)
+    def add_over(total, axis, size, gaps):
+        for gap in gaps:
+            swap = [(i, i ^ gap) for i in range(size)]
+            total = total + lax.ppermute(total, axis, swap)
+        return total
+
+    slope_all = add_over(slope_all, "dp", 4, (1, 2))
+    slope_all = add_over(slope_all, "seq", TASKS, (1,))
     back = lax.all_to_all(back, "seq", split_axis=0, concat_axis=0, tiled=True)
+    back, slope_all = lax.optimization_barrier((back, slope_all))
+    slope_grad = add_over(slope_all, "seq", TASKS, (2, 4, 8)) * (-1.0 / patches)
+
     text_dq, mem_dk, mem_dv, self_out = vmem_call(
         unpack_tasks,
         (

time: 214 us -> 182 us (0.85)
  blocking collectives: 78 us -> 15.2 us
  Pallas kernels: 23.8 us -> 43.1 us
  starting transfers between devices: 17 us -> 25 us
  waiting for transfers between devices: 57.1 us -> 64.3 us
  local copies, waits for them, and re-layouts: 7.69 us -> 3.54 us
    all_gather x1 -> x0, blocking collectives: 63.1 us -> none  [local(): slope_all = lax.all_gather(slope_sum, ('seq', 'dp'), axis=0)]
    pallas_call x1, Pallas kernels: 0.11 us -> 21.1 us  [local(): pl.pallas_call(pack_self, out_shape=sds((4, 4, 32, HEADS * HS), BF), in_s...]
    ppermute x0 -> x6, waiting for transfers between devices: none -> 17.3 us  [add_over(): total = total + lax.ppermute(total, axis, swap)]
    all_to_all x1, waiting for transfers between devices: 37.7 us -> 27.7 us  [local(): back = lax.all_to_all(back, 'seq', split_axis=0, concat_axis=0, tiled=True)]
    ppermute x0 -> x6, starting transfers between devices: none -> 8.09 us  [add_over(): total = total + lax.ppermute(total, axis, swap)]
    unnamed x27 -> x19, local copies, waits for them, and re-layouts: 5.58 us -> 1.28 us
  transfers between devices with their start and end apart: 3 -> 9, of which waited for: 2 -> 8; matrix products, arithmetic and copies ran while one was open for 13% -> 15% of each run, Pallas kernels for 0% -> 0%
where the time goes in v3:
time: 182 us; the launch traced here: 181 us
  waiting for transfers between devices  64.3 us (35%)
  Pallas kernels  43.1 us (24%)
  starting transfers between devices  25 us (14%)
  other arithmetic  24.8 us (14%)
  blocking collectives  15.2 us (8%)
  between operations  4.8 us (3%)
  local copies, waits for them, and re-layouts  3.54 us (2%)
    all_to_all x1, waiting for transfers between devices, local(): back = lax.all_to_all(back, 'seq', split_axis=0, concat_axis=0, tiled=True)  27.7 us
    pallas_call x1, Pallas kernels, local(): pl.pallas_call(pack_self, out_shape=sds((4, 4, 32, HEADS * HS), BF), in_s...  21.1 us
    all_to_all x1, waiting for transfers between devices, local(): held = lax.all_to_all(sent, 'seq', split_axis=0, concat_axis=0, tiled=True)  19.3 us
    pallas_call x1, Pallas kernels, local(): vmem_call(attend, (sds((TASKS, 3, BLK, HS), BF), sds((8, BLK), F32)), in_...  18.4 us
    ppermute x6, waiting for transfers between devices, add_over(): total = total + lax.ppermute(total, axis, swap)  17.3 us
    all_to_all x1, blocking collectives, local(): lax.all_to_all(by_head, 'head', split_axis=0, concat_axis=0, tiled=True)  15.2 us
    mul x1, other arithmetic, local(): key_col * sb  14.3 us
    all_to_all x1, starting transfers between devices, local(): held = lax.all_to_all(sent, 'seq', split_axis=0, concat_axis=0, tiled=True)  8.75 us
  transfers between devices with their start and end apart: 9, of which 8 were waited for; matrix products, arithmetic and copies ran while one was open for 15% of the time, Pallas kernels for 0%

profile of v3, /device:TPU:8, one launch (start us, length us, event | category | flops | bytes accessed | tf_op | source)
XLA Modules:
  0.0 180.7 jit_solution(624158538096208696)
XLA Ops:
  0.7 21.1 %shard_map.171 = bf16[4,4,32,640]{3,2,1,0:T(8,128)(2,1)} custom-call(bf16[1,32,2560]{2,1,0:T(8,128)(2,1)} %q_ref.1, bf16[1,32,2560]{2,1,0:T(8,128)(2,1)} %k_ref.1, bf16[1,32,2560]{2,1,0:T(8,128)(2,1)} %v_ref.1, bf16[1,32,2560]{2,1,0:T(8,128)(2,1)} %g_ref.1), custom_call_target="tpu_custom_call" | custom-call | tf_op jit(solution)/shard_map/pallas_call | solution.py:230
  21.8 15.2 %all_to_all.20.self_ref = bf16[4,4,32,640]{3,2,1,0:T(8,128)(2,1)S(1)} all-to-all(bf16[4,4,32,640]{3,2,1,0:T(8,128)(2,1)} %shard_map.171), channel_id=1, replica_groups=mesh['seq'=16,'head'=4,'dp'=4] {'head'}, dimensions={0} | all-to-all | bytes 1310720 | tf_op jit(solution)/shard_map/all_to_all | solution.py:237
  37.0 1.6 shard_map.172
  38.7 8.8 %all-to-all-start.1 = ((bf16[16,4,128,128]{3,2,1,0:T(8,128)(2,1)}), bf16[16,4,128,128]{3,2,1,0:T(8,128)(2,1)}, u32[]{:S(2)}, u32[]{:S(2)}) async-start(bf16[16,4,128,128]{3,2,1,0:T(8,128)(2,1)} %shard_map.172), calls=%async_computation.1 | async-start | bytes 4194304 | tf_op jit(solution)/shard_map/all_to_all | solution.py:241
  57.0 1.9 %broadcast_select_fusion.1 = (s32[2048]{0:T(1024)S(1)}, s32[2048]{0:T(1024)S(1)}) fusion(s32[]{:T(128)} %bitcast.8, s32[]{:T(128)} %bitcast.7, s32[]{:T(128)S(6)} %add.129, s32[]{:T(128)S(6)} %add.127, s32[]{:T(128)} %bitcast.1), kind=kLoop, calls=%fused_computation.39 | loop fusion | flops 22528 | bytes 16404 | tf_op jit(solution)/shard_map/jit(_where)/select_n | solution.py:202
  58.9 4.0 %convert_multiply_fusion.2 = (f32[1,2048]{1,0:T(1,128)S(1)}, f32[1,2048]{1,0:T(1,128)S(1)}) fusion(f32[]{:T(128)} %bitcast.10, s32[]{:T(128)S(6)} %add.129, s32[]{:T(128)S(6)} %add.127, s32[]{:T(128)} %bitcast.1, s32[]{:T(128)} %bitcast.8, s32[]{:T(128)} %bitcast.7, s32[]{:T(128)} %bitcast.6, s32[]{:T(128)} %bitcast.5, f32[]{:T(128)} %bitcast.9), kind=kLoop, calls=%fused_computation.24 | loop fusion | flops 67584 | bytes 16420 | tf_op jit(solution)/shard_map/mul | solution.py:222
  63.0 14.3 %convert_multiply_fusion = (f32[2048,128]{1,0:T(8,128)S(1)}, f32[2048,128]{1,0:T(8,128)S(1)}) fusion(f32[]{:T(128)} %bitcast.10, s32[2048]{0:T(1024)S(1)} %get-tuple-element.49, s32[]{:T(128)} %bitcast.6, s32[]{:T(128)} %bitcast.5, s32[2048]{0:T(1024)S(1)} %get-tuple-element.50, s32[]{:T(128)} %bitcast.1, pred[2048]{0:T(1024)(128)(4,1)S(1)} %get-tuple-element.47, ...), kind=kLoop, calls=%fused_computation.1 | loop fusion | flops 5242880 | bytes 2117652 | tf_op jit(solution)/shard_map/mul | solution.py:258
  77.3 19.3 %all-to-all-done.1.in_ref = bf16[16,4,128,128]{3,2,1,0:T(8,128)(2,1)} async-done(((bf16[16,4,128,128]{3,2,1,0:T(8,128)(2,1)}), bf16[16,4,128,128]{3,2,1,0:T(8,128)(2,1)}, u32[]{:S(2)}, u32[]{:S(2)}) %all-to-all-start.1) | async-done | bytes 2097184 | tf_op jit(solution)/shard_map/all_to_all | solution.py:241
  97.0 18.4 %shard_map.173 = (bf16[16,3,128,128]{3,2,1,0:T(8,128)(2,1)S(1)}, f32[8,128]{1,0:T(8,128)S(1)}) custom-call(s32[2,8]{1,0:T(2,128)S(1)} %pad_add_fusion.win_ref, f32[2048,128]{1,0:T(8,128)S(1)} %get-tuple-element.34.ka_ref, f32[2048,128]{1,0:T(8,128)S(1)} %get-tuple-element.33.kb_ref, f32[2048,128]{1,0:T(8,128)S(1)} %iota.86.kp_ref, ...), custom_call_target="tpu_custom_call" | custom-call | tf_op jit(solution)/shard_map/pallas_call | solution.py:244
  115.4 1.1 copy-done.1
  116.5 4.7 %all-to-all-start.2 = ((bf16[16,3,128,128]{3,2,1,0:T(8,128)(2,1)}), bf16[16,3,128,128]{3,2,1,0:T(8,128)(2,1)S(1)}, u32[]{:S(2)}, u32[]{:S(2)}) async-start(bf16[16,3,128,128]{3,2,1,0:T(8,128)(2,1)} %copy-done.1), calls=%async_computation.2 | async-start | bytes 3145728 | tf_op jit(solution)/shard_map/all_to_all | solution.py:273
  121.6 3.4 %collective-permute-done = f32[2,5]{1,0:T(2,128)S(1)} collective-permute-done((f32[2,5]{1,0:T(2,128)S(1)}, f32[2,5]{1,0:T(2,128)S(1)}, u32[]{:S(2)}, u32[]{:S(2)}) %collective-permute-start) | collective-permute-done | bytes 72 | tf_op jit(solution)/shard_map/ppermute | solution.py:268
  125.1 2.3 %collective-permute-start.1 = (f32[2,5]{1,0:T(2,128)S(1)}, f32[2,5]{1,0:T(2,128)S(1)}, u32[]{:S(2)}, u32[]{:S(2)}) collective-permute-start(f32[2,5]{1,0:T(2,128)S(1)} %fusion.15), channel_id=1, source_target_pairs={{0,2},{1,3},{2,0},{3,1},{4,6},{5,7},{6,4},{7,5},{8,10},{9,11},{10,... | collective-permute-start | bytes 128 | tf_op jit(solution)/shard_map/ppermute | solution.py:268
  127.4 2.8 %collective-permute-done.1 = f32[2,5]{1,0:T(2,128)S(1)} collective-permute-done((f32[2,5]{1,0:T(2,128)S(1)}, f32[2,5]{1,0:T(2,128)S(1)}, u32[]{:S(2)}, u32[]{:S(2)}) %collective-permute-start.1) | collective-permute-done | bytes 72 | tf_op jit(solution)/shard_map/ppermute | solution.py:268
  130.3 1.1 collective-permute-done.2
  131.4 27.7 %all-to-all-done.2.in_ref = bf16[16,3,128,128]{3,2,1,0:T(8,128)(2,1)S(1)} async-done(((bf16[16,3,128,128]{3,2,1,0:T(8,128)(2,1)}), bf16[16,3,128,128]{3,2,1,0:T(8,128)(2,1)S(1)}, u32[]{:S(2)}, u32[]{:S(2)}) %all-to-all-start.2) | async-done | bytes 1572896 | tf_op jit(solution)/shard_map/all_to_all | solution.py:273
  159.1 1.1 shard_map.174
  160.2 3.5 %all-to-all-start.3 = ((bf16[4,5,3,32,128]{4,3,2,1,0:T(8,128)(2,1)}), bf16[4,5,3,32,128]{4,3,2,1,0:T(8,128)(2,1)S(1)}, u32[]{:S(2)}, u32[]{:S(2)}) async-start(bf16[4,5,3,32,128]{4,3,2,1,0:T(8,128)(2,1)} %get-tuple-element.21), calls=%async_computation.3 | async-start | bytes 983040 | tf_op jit(solution)/shard_map/all_to_all | solution.py:286
  163.9 3.5 %collective-permute-done.3 = f32[2,5]{1,0:T(2,128)S(1)} collective-permute-done((f32[2,5]{1,0:T(2,128)S(1)}, f32[2,5]{1,0:T(2,128)S(1)}, u32[]{:S(2)}, u32[]{:S(2)}) %collective-permute-start.3) | collective-permute-done | bytes 72 | tf_op jit(solution)/shard_map/ppermute | solution.py:268
  167.4 2.0 %collective-permute-start.4 = (f32[2,5]{1,0:T(2,128)S(1)}, f32[2,5]{1,0:T(2,128)S(1)}, u32[]{:S(2)}, u32[]{:S(2)}) collective-permute-start(f32[2,5]{1,0:T(2,128)S(1)} %add.140), channel_id=1, source_target_pairs={{0,64},{16,80},{32,96},{48,112},{64,0},{80,16},{96,32},{112,48},{1... | collective-permute-start | bytes 128 | tf_op jit(solution)/shard_map/ppermute | solution.py:268
  169.3 2.5 %collective-permute-done.4 = f32[2,5]{1,0:T(2,128)S(1)} collective-permute-done((f32[2,5]{1,0:T(2,128)S(1)}, f32[2,5]{1,0:T(2,128)S(1)}, u32[]{:S(2)}, u32[]{:S(2)}) %collective-permute-start.4) | collective-permute-done | bytes 72 | tf_op jit(solution)/shard_map/ppermute | solution.py:268
  171.8 3.4 %collective-permute-start.5 = (f32[2,5]{1,0:T(2,128)S(1)}, f32[2,5]{1,0:T(2,128)S(1)}, u32[]{:S(2)}, u32[]{:S(2)}) collective-permute-start(f32[2,5]{1,0:T(2,128)S(1)} %add.141), channel_id=1, source_target_pairs={{0,128},{16,144},{32,160},{48,176},{64,192},{80,208},{96,224},{112... | collective-permute-start | bytes 128 | tf_op jit(solution)/shard_map/ppermute | solution.py:268
  175.3 4.0 %collective-permute-done.5 = f32[2,5]{1,0:T(2,128)S(1)} collective-permute-done((f32[2,5]{1,0:T(2,128)S(1)}, f32[2,5]{1,0:T(2,128)S(1)}, u32[]{:S(2)}, u32[]{:S(2)}) %collective-permute-start.5) | collective-permute-done | bytes 72 | tf_op jit(solution)/shard_map/ppermute | solution.py:268
  179.9 0.9 shard_map.175
  (50 shorter events, 7.3 us)
Async XLA Ops:
  0.6 46.8 %copy-start = (f32[2,5]{1,0:T(2,128)S(1)}, f32[2,5]{1,0:T(2,128)}, u32[]{:S(2)}) copy-start(f32[2,5]{1,0:T(2,128)} %param.20) | copy-start | bytes 124
  0.7 36.3 %copy-start.3 = (bf16[1,256,640]{2,1,0:T(8,128)(2,1)S(1)}, bf16[1,256,640]{2,1,0:T(8,128)(2,1)}, u32[]{:S(2)}) copy-start(bf16[1,256,640]{2,1,0:T(8,128)(2,1)} %tg_ref.1) | copy-start | bytes 983044
  0.7 36.3 %copy-start.5 = (bf16[1,128,640]{2,1,0:T(8,128)(2,1)S(1)}, bf16[1,128,640]{2,1,0:T(8,128)(2,1)}, u32[]{:S(2)}) copy-start(bf16[1,128,640]{2,1,0:T(8,128)(2,1)} %mv_ref.1) | copy-start | bytes 491524
  0.7 36.3 %copy-start.4 = (bf16[1,128,640]{2,1,0:T(8,128)(2,1)S(1)}, bf16[1,128,640]{2,1,0:T(8,128)(2,1)}, u32[]{:S(2)}) copy-start(bf16[1,128,640]{2,1,0:T(8,128)(2,1)} %mk_ref.1) | copy-start | bytes 491524
  0.7 36.3 %copy-start.2 = (bf16[1,256,640]{2,1,0:T(8,128)(2,1)S(1)}, bf16[1,256,640]{2,1,0:T(8,128)(2,1)}, u32[]{:S(2)}) copy-start(bf16[1,256,640]{2,1,0:T(8,128)(2,1)} %tq_ref.1) | copy-start | bytes 983044
  38.6 10.9 %copy-start.6 = (s32[1,4]{1,0:T(1,128)S(1)}, s32[1,4]{1,0:T(1,128)}, u32[]{:S(2)}) copy-start(s32[1,4]{1,0:T(1,128)} %param.21) | copy-start | bytes 52
  38.6 14.1 %copy-start.8 = (s32[1,4096]{1,0:T(1,128)S(1)}, s32[1,4096]{1,0:T(1,128)}, u32[]{:S(2)}) copy-start(s32[1,4096]{1,0:T(1,128)} %param.23) | copy-start | bytes 49156
  38.6 17.7 %copy-start.7 = (s32[1,4]{1,0:T(1,128)S(1)}, s32[1,4]{1,0:T(1,128)}, u32[]{:S(2)}) copy-start(s32[1,4]{1,0:T(1,128)} %param.22) | copy-start | bytes 52
  38.7 58.0 %all-to-all-start.1 = ((bf16[16,4,128,128]{3,2,1,0:T(8,128)(2,1)}), bf16[16,4,128,128]{3,2,1,0:T(8,128)(2,1)}, u32[]{:S(2)}, u32[]{:S(2)}) async-start(bf16[16,4,128,128]{3,2,1,0:T(8,128)(2,1)} %shard_map.172), calls=%async_computation.1 | async-start | bytes 4194304 | tf_op jit(solution)/shard_map/all_to_all | solution.py:241
  115.3 1.2 copy-start.1
  116.5 42.6 %all-to-all-start.2 = ((bf16[16,3,128,128]{3,2,1,0:T(8,128)(2,1)}), bf16[16,3,128,128]{3,2,1,0:T(8,128)(2,1)S(1)}, u32[]{:S(2)}, u32[]{:S(2)}) async-start(bf16[16,3,128,128]{3,2,1,0:T(8,128)(2,1)} %copy-done.1), calls=%async_computation.2 | async-start | bytes 3145728 | tf_op jit(solution)/shard_map/all_to_all | solution.py:273
  121.5 3.6 %collective-permute-start = (f32[2,5]{1,0:T(2,128)S(1)}, f32[2,5]{1,0:T(2,128)S(1)}, u32[]{:S(2)}, u32[]{:S(2)}) collective-permute-start(f32[2,5]{1,0:T(2,128)S(1)} %broadcast_select_fusion.3), channel_id=1, source_target_pairs={{0,1},{1,0},{2,3},{3,2},{4,5},{5,4},{6,7},{7,6},{8,9},{9,8},{10,11... | collective-permute-start | bytes 128 | tf_op jit(solution)/shard_map/ppermute | solution.py:268
  125.1 5.1 %collective-permute-start.1 = (f32[2,5]{1,0:T(2,128)S(1)}, f32[2,5]{1,0:T(2,128)S(1)}, u32[]{:S(2)}, u32[]{:S(2)}) collective-permute-start(f32[2,5]{1,0:T(2,128)S(1)} %fusion.15), channel_id=1, source_target_pairs={{0,2},{1,3},{2,0},{3,1},{4,6},{5,7},{6,4},{7,5},{8,10},{9,11},{10,... | collective-permute-start | bytes 128 | tf_op jit(solution)/shard_map/ppermute | solution.py:268
  130.3 1.1 collective-permute-start.2
  160.2 19.7 %all-to-all-start.3 = ((bf16[4,5,3,32,128]{4,3,2,1,0:T(8,128)(2,1)}), bf16[4,5,3,32,128]{4,3,2,1,0:T(8,128)(2,1)S(1)}, u32[]{:S(2)}, u32[]{:S(2)}) async-start(bf16[4,5,3,32,128]{4,3,2,1,0:T(8,128)(2,1)} %get-tuple-element.21), calls=%async_computation.3 | async-start | bytes 983040 | tf_op jit(solution)/shard_map/all_to_all | solution.py:286
  163.7 3.7 %collective-permute-start.3 = (f32[2,5]{1,0:T(2,128)S(1)}, f32[2,5]{1,0:T(2,128)S(1)}, u32[]{:S(2)}, u32[]{:S(2)}) collective-permute-start(f32[2,5]{1,0:T(2,128)S(1)} %add.139), channel_id=1, source_target_pairs={{0,32},{16,48},{32,0},{48,16},{64,96},{80,112},{96,64},{112,80},{1... | collective-permute-start | bytes 128 | tf_op jit(solution)/shard_map/ppermute | solution.py:268
  167.4 4.5 %collective-permute-start.4 = (f32[2,5]{1,0:T(2,128)S(1)}, f32[2,5]{1,0:T(2,128)S(1)}, u32[]{:S(2)}, u32[]{:S(2)}) collective-permute-start(f32[2,5]{1,0:T(2,128)S(1)} %add.140), channel_id=1, source_target_pairs={{0,64},{16,80},{32,96},{48,112},{64,0},{80,16},{96,32},{112,48},{1... | collective-permute-start | bytes 128 | tf_op jit(solution)/shard_map/ppermute | solution.py:268
  171.8 7.5 %collective-permute-start.5 = (f32[2,5]{1,0:T(2,128)S(1)}, f32[2,5]{1,0:T(2,128)S(1)}, u32[]{:S(2)}, u32[]{:S(2)}) collective-permute-start(f32[2,5]{1,0:T(2,128)S(1)} %add.141), channel_id=1, source_target_pairs={{0,128},{16,144},{32,160},{48,176},{64,192},{80,208},{96,224},{112... | collective-permute-start | bytes 128 | tf_op jit(solution)/shard_map/ppermute | solution.py:268

commit v4 on v3

--- a/solution.py
+++ b/solution.py
@@ -29,19 +29,23 @@
     )
 
 
-def pack_self(q_ref, k_ref, v_ref, g_ref, out_ref, sems):
+def pack_self(q_ref, k_ref, v_ref, g_ref, *refs):
+    outs, sems = refs[:4], refs[4]
+    me = lax.axis_index("head")
+    width = HEADS * HS
     copies = []
-    width = HEADS * HS
-    for a, ref in enumerate((q_ref, k_ref, v_ref, g_ref)):
-        for x in range(4):
-            part = ref.at[0, :, pl.ds(x * width, width)]
-            copies.append(pltpu.make_async_copy(part, out_ref.at[x, a], sems.at[a, x]))
+    for gap in (2, 1, 3, 0):
+        at = pl.ds(pl.multiple_of((me ^ gap) * width, HS), width)
+        for a, ref in enumerate((q_ref, k_ref, v_ref, g_ref)):
+            copies.append(
+                pltpu.make_async_copy(ref.at[0, :, at], outs[gap].at[a], sems.at[gap, a])
+            )
             copies[-1].start()
     for copy in copies:
         copy.wait()
 
 
-def pack_tasks(tq_ref, mk_ref, mv_ref, tg_ref, self_ref, out_ref):
+def pack_text(tq_ref, mk_ref, mv_ref, tg_ref, out_ref):
     for h in range(HEADS):
         cols = slice(h * HS, (h + 1) * HS)
         for j in range(2):
@@ -51,37 +55,58 @@
             out_ref[t, 1] = mk_ref[0, :, cols]
             out_ref[t, 2] = mv_ref[0, :, cols]
             out_ref[t, 3] = tg_ref[0, rows, cols]
-        for a in range(4):
-            for x in range(4):
-                out_ref[TEXT_TASKS + h, a, x * 32 : (x + 1) * 32] = self_ref[x, a, :, cols]
-    out_ref[TASKS - 1] = jnp.zeros((4, BLK, HS), BF)
-
-
-def unpack_tasks(in_ref, tq_ref, mk_ref, mv_ref, self_ref):
+    out_ref[TEXT_TASKS:] = jnp.zeros((TASKS - TEXT_TASKS, 4, BLK, HS), BF)
+
+
+def pack_heads(s0_ref, s1_ref, s2_ref, s3_ref, text_ref, out_ref, buf, sem):
+    me = lax.axis_index("head")
+    for h in range(HEADS):
+        cols = slice(h * HS, (h + 1) * HS)
+        for gap, ref in enumerate((s0_ref, s1_ref, s2_ref, s3_ref)):
+            at = pl.ds(pl.multiple_of((me ^ gap) * 32, 32), 32)
+            for a in range(4):
+                buf[h, a, at] = ref[a, :, cols]
+    copy = pltpu.make_async_copy(buf, out_ref.at[pl.ds(TEXT_TASKS, HEADS)], sem)
+    copy.start()
+    copy.wait()
+
+
+def unpack_tasks(
+    in_ref, tq_ref, mk_ref, mv_ref, slope_ref, s0_ref, s1_ref, s2_ref, s3_ref
+):
+    me = lax.axis_index("head")
+    k, v = (slice(i * BLK, (i + 1) * BLK) for i in (1, 2))
+    slope_ref[...] = jnp.zeros_like(slope_ref)
     for h in range(HEADS):
         cols = slice(h * HS, (h + 1) * HS)
         for j in range(2):
-            tq_ref[0, j * BLK : (j + 1) * BLK, cols] = in_ref[2 * h + j, 0]
-        mk = in_ref[2 * h, 1].astype(F32) + in_ref[2 * h + 1, 1].astype(F32)
-        mv = in_ref[2 * h, 2].astype(F32) + in_ref[2 * h + 1, 2].astype(F32)
+            tq_ref[0, j * BLK : (j + 1) * BLK, cols] = in_ref[2 * h + j, :BLK]
+        mk = in_ref[2 * h, k].astype(F32) + in_ref[2 * h + 1, k].astype(F32)
+        mv = in_ref[2 * h, v].astype(F32) + in_ref[2 * h + 1, v].astype(F32)
         mk_ref[0, :, cols] = mk.astype(BF)
         mv_ref[0, :, cols] = mv.astype(BF)
-        for a in range(3):
-            for x in range(4):
-                self_ref[x, h, a] = in_ref[TEXT_TASKS + h, a, x * 32 : (x + 1) * 32]
-
-
-def unpack_self(in_ref, q_ref, k_ref, v_ref):
-    for a, ref in enumerate((q_ref, k_ref, v_ref)):
-        for x in range(4):
-            for h in range(HEADS):
-                c = (x * HEADS + h) * HS
-                ref[0, :, c : c + HS] = in_ref[x, h, a]
+        for gap, ref in enumerate((s0_ref, s1_ref, s2_ref, s3_ref)):
+            for a in range(3):
+                at = pl.ds(pl.multiple_of(a * BLK + (me ^ gap) * 32, 32), 32)
+                ref[a, :, cols] = in_ref[TEXT_TASKS + h, at]
+        pieces = in_ref[TEXT_TASKS + h, 3 * BLK :].astype(F32)
+        for i in range(2):
+            whole = pieces[3 * i : 3 * i + 1] + pieces[3 * i + 1 : 3 * i + 2]
+            slope_ref[i, h : h + 1] = whole + pieces[3 * i + 2 : 3 * i + 3]
+
+
+def unpack_self(s0_ref, s1_ref, s2_ref, s3_ref, q_ref, k_ref, v_ref):
+    me = lax.axis_index("head")
+    width = HEADS * HS
+    for gap, part in enumerate((s0_ref, s1_ref, s2_ref, s3_ref)):
+        at = pl.ds(pl.multiple_of((me ^ gap) * width, HS), width)
+        for a, ref in enumerate((q_ref, k_ref, v_ref)):
+            ref[0, :, at] = part[a]
 
 
 def attend(
-    win_ref, ka_ref, kb_ref, kp_ref, qi_ref, in_ref, out_ref, slope_ref,
-    k_buf, v_buf, kt_buf, t_buf, d_buf, ds_buf, dk_acc, dv_acc,
+    win_ref, ka_ref, kb_ref, kp_ref, qi_ref, in_ref, out_ref,
+    k_buf, v_buf, kt_buf, t_buf, d_buf, ds_buf, dk_acc, dv_acc, slope_ref,
 ):
     inv_root = HS ** (-0.5)
     blocks = TASKS * BLK // QB
@@ -155,7 +180,7 @@
         dq = jnp.dot(kt, ds_buf[: tiles * BLK], preferred_element_type=F32).T
         dq = (dq * inv_root).astype(BF)
         for i in range(per):
-            out_ref[per * b + i, 0] = dq[i * BLK : (i + 1) * BLK]
+            out_ref[per * b + i, :BLK] = dq[i * BLK : (i + 1) * BLK]
         for row, v in ((0, sa), (1, sb)):
             v = jnp.sum(v, axis=0, keepdims=True)
             slope_ref[row : row + 1] += sum(v[:, i * BLK : (i + 1) * BLK] for i in range(per))
@@ -174,10 +199,20 @@
         return 0
 
     lax.fori_loop(0, blocks, step, 0)
+    line = lax.broadcasted_iota(jnp.int32, (16, BLK), 0)
+    pieces = jnp.zeros((16, BLK), F32)
+    for row in range(2):
+        rest = jnp.broadcast_to(slope_ref[row : row + 1], (16, BLK))
+        for i in range(3):
+            piece = rest.astype(BF).astype(F32)
+            rest = rest - piece
+            pieces = jnp.where(line == 3 * row + i, piece, pieces)
+    pieces = pieces.astype(BF)
     for s in range(TASKS):
         here = slice(s * BLK, (s + 1) * BLK)
-        out_ref[s, 1] = (dk_acc[here] * inv_root).astype(BF)
-        out_ref[s, 2] = dv_acc[here].astype(BF)
+        out_ref[s, BLK : 2 * BLK] = (dk_acc[here] * inv_root).astype(BF)
+        out_ref[s, 2 * BLK : 3 * BLK] = dv_acc[here].astype(BF)
+        out_ref[s, 3 * BLK :] = pieces
 
 
 def local(
@@ -226,24 +261,39 @@
     wide = by_page(blocks[:, -1], ends) > (low + NARROW) * BLK
     window = jnp.stack([low, wide.astype(jnp.int32)])
 
+    def swap_heads(parts):
+        own, out = parts[0], [None] * 4
+        for gap in (2, 1, 3):
+            swap = [(i, i ^ gap) for i in range(4)]
+            out[gap] = lax.ppermute(parts[gap], "head", swap)
+        return [own] + out[1:]
+
     hbm = pl.BlockSpec(memory_space=pltpu.HBM)
     by_head = pl.pallas_call(
         pack_self,
-        out_shape=sds((4, 4, 32, HEADS * HS), BF),
+        out_shape=[sds((4, 32, HEADS * HS), BF)] * 4,
         in_specs=[hbm] * 4,
-        out_specs=hbm,
+        out_specs=[pl.BlockSpec(memory_space=pltpu.VMEM)] * 4,
         scratch_shapes=[pltpu.SemaphoreType.DMA((4, 4))],
     )(self_queries, self_keys, self_values, self_cotangent)
-    by_head = lax.all_to_all(by_head, "head", split_axis=0, concat_axis=0, tiled=True)
-    sent = vmem_call(pack_tasks, sds((TASKS, 4, BLK, HS), BF))(
-        text_queries, memory_keys, memory_values, text_cotangent, by_head
+    task_shape = sds((TASKS, 4, BLK, HS), BF)
+    vm = pl.BlockSpec(memory_space=pltpu.VMEM)
+    sent = vmem_call(pack_text, task_shape)(
+        text_queries, memory_keys, memory_values, text_cotangent
     )
+    by_head = swap_heads(by_head)
+    sent = vmem_call(
+        pack_heads,
+        task_shape,
+        in_specs=[vm] * 4 + [hbm],
+        out_specs=hbm,
+        scratch_shapes=[pltpu.VMEM((HEADS, 4, BLK, HS), BF), pltpu.SemaphoreType.DMA],
+        input_output_aliases={4: 0},
+    )(*by_head, sent)
     held = lax.all_to_all(sent, "seq", split_axis=0, concat_axis=0, tiled=True)
-
-    vm = pl.BlockSpec(memory_space=pltpu.VMEM)
-    back, slope_part = vmem_call(
+    back = vmem_call(
         attend,
-        (sds((TASKS, 3, BLK, HS), BF), sds((8, BLK), F32)),
+        sds((TASKS, 3 * BLK + 16, HS), BF),
         in_specs=[pl.BlockSpec(memory_space=pltpu.SMEM)] + [vm] * 5,
         scratch_shapes=[
             pltpu.VMEM((patches, HS), BF),
@@ -254,38 +304,32 @@
             pltpu.VMEM((patches, QB), BF),
             pltpu.VMEM((patches, HS), F32),
             pltpu.VMEM((patches, HS), F32),
+            pltpu.VMEM((8, BLK), F32),
         ],
     )(window, key_row * sa, key_col * sb, key_id.astype(F32), q_info, held)
 
-    slope_sum = jnp.sum(slope_part[:2], axis=1) / jnp.where(
-        is_text, 1.0, slope * LOG2E
-    )
-    mine = jnp.arange(HEADS) == task - TEXT_TASKS
-    slope_all = jnp.where(mine[None, :], slope_sum[:, None], 0.0)
-    def add_over(total, axis, size, gaps):
-        for gap in gaps:
-            swap = [(i, i ^ gap) for i in range(size)]
-            total = total + lax.ppermute(total, axis, swap)
-        return total
-
-    slope_all = add_over(slope_all, "dp", 4, (1, 2))
-    slope_all = add_over(slope_all, "seq", TASKS, (1,))
     back = lax.all_to_all(back, "seq", split_axis=0, concat_axis=0, tiled=True)
-    back, slope_all = lax.optimization_barrier((back, slope_all))
-    slope_grad = add_over(slope_all, "seq", TASKS, (2, 4, 8)) * (-1.0 / patches)
-
-    text_dq, mem_dk, mem_dv, self_out = vmem_call(
+    part = sds((3, 32, HEADS * HS), BF)
+    text_dq, mem_dk, mem_dv, slope_sum, *self_out = vmem_call(
         unpack_tasks,
         (
             sds(text_queries.shape, BF),
             sds(memory_keys.shape, BF),
             sds(memory_values.shape, BF),
-            sds((4, HEADS, 3, 32, HS), BF),
+            sds((2, 8, BLK), F32),
+            *(part,) * 4,
         ),
     )(back)
-    self_out = lax.all_to_all(self_out, "head", split_axis=0, concat_axis=0, tiled=True)
+    self_out = swap_heads(self_out)
+    slope_sum, self_out[2] = lax.optimization_barrier((slope_sum, self_out[2]))
+    slope_sum = jnp.sum(slope_sum[:, :HEADS], axis=2) / (slopes * (LOG2E * -patches))
+    near, far, last = (
+        lax.ppermute(slope_sum, "dp", [(i, i ^ gap) for i in range(4)])
+        for gap in (1, 2, 3)
+    )
+    slope_grad = (slope_sum + near) + (far + last)
     shape = sds(self_queries.shape, BF)
-    self_dq, self_dk, self_dv = vmem_call(unpack_self, (shape, shape, shape))(self_out)
+    self_dq, self_dk, self_dv = vmem_call(unpack_self, (shape, shape, shape))(*self_out)
     return self_dq, self_dk, self_dv, slope_grad, text_dq, mem_dk, mem_dv
 
 

time: 182 us -> 157 us (0.86)
  waiting for transfers between devices: 64.3 us -> 27.8 us
  blocking collectives: 15.2 us -> 47.2 us
  Pallas kernels: 43.1 us -> 23.9 us
  starting transfers between devices: 25 us -> 22 us
  local copies, waits for them, and re-layouts: 3.54 us -> 5.92 us
    all_to_all x1, blocking collectives: 15.2 us -> 47.2 us  [local(): back = lax.all_to_all(back, 'seq', split_axis=0, concat_axis=0, tiled=True)]
    all_to_all x2 -> x0, waiting for transfers between devices: 27.7 us -> none  [the longest x1 27.7 us: local(): back = lax.all_to_all(back, 'seq', split_axis=0, concat_axis=0, tiled=True)]
    pallas_call x4 -> x5, Pallas kernels: 42 us -> 23 us  [the longest x1 17.5 us: local(): vmem_call(attend, sds((TASKS, 3 * BLK + 16, HS), BF), in_specs=[pl.BlockS...]
    ppermute x6 -> x9, waiting for transfers between devices: 17.3 us -> 8.58 us  [the longest x6 7.86 us: swap_heads(): out[gap] = lax.ppermute(parts[gap], 'head', swap)]
    all_to_all x2 -> x0, starting transfers between devices: 8.2 us -> none  [the longest x1 4.73 us: local(): back = lax.all_to_all(back, 'seq', split_axis=0, concat_axis=0, tiled=True)]
    ppermute x6 -> x9, starting transfers between devices: 8.09 us -> 13 us  [the longest x6 8.88 us: swap_heads(): out[gap] = lax.ppermute(parts[gap], 'head', swap)]
    unnamed x19 -> x18, local copies, waits for them, and re-layouts: 1.28 us -> 3.8 us
  transfers between devices with their start and end apart: 9 -> 10, of which waited for: 8 -> 6; matrix products, arithmetic and copies ran while one was open for 15% -> 17% of each run, Pallas kernels for 0% -> 2%
where the time goes in v4:
time: 157 us; the launch traced here: 156 us
  blocking collectives  47.2 us (30%)
  waiting for transfers between devices  27.8 us (18%)
  other arithmetic  24.6 us (16%)
  Pallas kernels  23.9 us (15%)
  starting transfers between devices  22 us (14%)
  local copies, waits for them, and re-layouts  5.92 us (4%)
  between operations  4.75 us (3%)
    all_to_all x1, blocking collectives, local(): back = lax.all_to_all(back, 'seq', split_axis=0, concat_axis=0, tiled=True)  47.2 us
    all_to_all x1, waiting for transfers between devices, local(): held = lax.all_to_all(sent, 'seq', split_axis=0, concat_axis=0, tiled=True)  19.3 us
    pallas_call x1, Pallas kernels, local(): vmem_call(attend, sds((TASKS, 3 * BLK + 16, HS), BF), in_specs=[pl.BlockS...  17.5 us
    mul x1, other arithmetic, local(): key_col * sb  14.4 us
    all_to_all x1, starting transfers between devices, local(): held = lax.all_to_all(sent, 'seq', split_axis=0, concat_axis=0, tiled=True)  8.95 us
    ppermute x6, starting transfers between devices, swap_heads(): out[gap] = lax.ppermute(parts[gap], 'head', swap)  8.88 us
    ppermute x6, waiting for transfers between devices, swap_heads(): out[gap] = lax.ppermute(parts[gap], 'head', swap)  7.86 us
    ppermute x3, starting transfers between devices, local(): lax.ppermute(slope_sum, 'dp', [(i, i ^ gap) for i in range(4)])  4.14 us
  transfers between devices with their start and end apart: 10, of which 6 were waited for; matrix products, arithmetic and copies ran while one was open for 17% of the time, Pallas kernels for 2%

profile of v4, /device:TPU:8, one launch (start us, length us, event | category | flops | bytes accessed | tf_op | source)
XLA Modules:
  0.0 156.3 jit_solution(16491227261680478176)
XLA Ops:
  0.6 2.1 %shard_map.171 = (bf16[4,32,640]{2,1,0:T(8,128)(2,1)}, bf16[4,32,640]{2,1,0:T(8,128)(2,1)}, bf16[4,32,640]{2,1,0:T(8,128)(2,1)}, bf16[4,32,640]{2,1,0:T(8,128)(2,1)}) custom-call(bf16[1,32,2560]{2,1,0:T(8,128)(2,1)} %q_ref.1, bf16[1,32,2560]{2,1,0:T(8,128)(2,1)} %k_ref.1, bf16[1,32,2560]{2,1,0:T(8,128)(2,1)} %v_ref.1, bf16[1,32,2560]{2,1,0:T(8,128)(2,1)} %g_ref.1), custom_call_target="tpu_custom_call" | custom-call | tf_op jit(solution)/shard_map/pallas_call | solution.py:272
  2.7 1.6 %collective-permute-start = (bf16[4,32,640]{2,1,0:T(8,128)(2,1)}, bf16[4,32,640]{2,1,0:T(8,128)(2,1)S(1)}, u32[]{:S(2)}, u32[]{:S(2)}) collective-permute-start(bf16[4,32,640]{2,1,0:T(8,128)(2,1)} %get-tuple-element.25), channel_id=1, source_target_pairs={{0,4},{4,0},{8,12},{12,8},{1,5},{5,1},{9,13},{13,9},{2,6},{6,2},{1... | collective-permute-start | bytes 491528 | tf_op jit(solution)/shard_map/ppermute | solution.py:268
  4.3 2.7 %collective-permute-start.1 = (bf16[4,32,640]{2,1,0:T(8,128)(2,1)}, bf16[4,32,640]{2,1,0:T(8,128)(2,1)S(1)}, u32[]{:S(2)}, u32[]{:S(2)}) collective-permute-start(bf16[4,32,640]{2,1,0:T(8,128)(2,1)} %get-tuple-element.26), channel_id=1, source_target_pairs={{0,8},{4,12},{8,0},{12,4},{1,9},{5,13},{9,1},{13,5},{2,10},{6,14},... | collective-permute-start | bytes 491528 | tf_op jit(solution)/shard_map/ppermute | solution.py:268
  7.5 1.0 copy-done
  8.5 1.0 copy-done.1
  9.4 0.9 copy-done.2
  10.3 0.9 copy-done.3
  11.3 1.6 %shard_map.172.text_ref = bf16[16,4,128,128]{3,2,1,0:T(8,128)(2,1)} custom-call(bf16[1,256,640]{2,1,0:T(8,128)(2,1)S(1)} %copy-done, bf16[1,128,640]{2,1,0:T(8,128)(2,1)S(1)} %copy-done.2, bf16[1,128,640]{2,1,0:T(8,128)(2,1)S(1)} %copy-done.3, bf16[1,256,640]{2,1,0:T(8,128)(2,1)S(1)} %copy-done.1), custom_call_target="tpu_custom_call" | custom-call | tf_op jit(solution)/shard_map/pallas_call | solution.py:281
  12.9 1.9 %collective-permute-done.1.s2_ref = bf16[4,32,640]{2,1,0:T(8,128)(2,1)S(1)} collective-permute-done((bf16[4,32,640]{2,1,0:T(8,128)(2,1)}, bf16[4,32,640]{2,1,0:T(8,128)(2,1)S(1)}, u32[]{:S(2)}, u32[]{:S(2)}) %collective-permute-start.1) | collective-permute-done | bytes 163872 | tf_op jit(solution)/shard_map/ppermute | solution.py:268
  14.7 2.4 %collective-permute-done.2.s3_ref = bf16[4,32,640]{2,1,0:T(8,128)(2,1)S(1)} collective-permute-done((bf16[4,32,640]{2,1,0:T(8,128)(2,1)}, bf16[4,32,640]{2,1,0:T(8,128)(2,1)S(1)}, u32[]{:S(2)}, u32[]{:S(2)}) %collective-permute-start.2) | collective-permute-done | bytes 163872 | tf_op jit(solution)/shard_map/ppermute | solution.py:268
  17.2 1.0 shard_map.173
  18.2 8.9 %all-to-all-start = ((bf16[16,4,128,128]{3,2,1,0:T(8,128)(2,1)}), bf16[16,4,128,128]{3,2,1,0:T(8,128)(2,1)}, u32[]{:S(2)}, u32[]{:S(2)}) async-start(bf16[16,4,128,128]{3,2,1,0:T(8,128)(2,1)} %shard_map.173), calls=%async_computation | async-start | bytes 4194304 | tf_op jit(solution)/shard_map/all_to_all | solution.py:293
  36.5 1.9 %broadcast_select_fusion.1 = (s32[2048]{0:T(1024)S(1)}, s32[2048]{0:T(1024)S(1)}) fusion(s32[]{:T(128)} %bitcast.8, s32[]{:T(128)} %bitcast.7, s32[]{:T(128)S(6)} %add.120, s32[]{:T(128)S(6)} %add.118, s32[]{:T(128)} %bitcast.1), kind=kLoop, calls=%fused_computation.40 | loop fusion | flops 22528 | bytes 16404 | tf_op jit(solution)/shard_map/jit(_where)/select_n | solution.py:237
  38.5 4.0 %convert_multiply_fusion.2 = (f32[1,2048]{1,0:T(1,128)S(1)}, f32[1,2048]{1,0:T(1,128)S(1)}) fusion(f32[]{:T(128)} %bitcast.10, s32[]{:T(128)S(6)} %add.120, s32[]{:T(128)S(6)} %add.118, s32[]{:T(128)} %bitcast.1, s32[]{:T(128)} %bitcast.8, s32[]{:T(128)} %bitcast.7, s32[]{:T(128)} %bitcast.6, s32[]{:T(128)} %bitcast.5, f32[]{:T(128)} %bitcast.9), kind=kLoop, calls=%fused_computation.25 | loop fusion | flops 67584 | bytes 16420 | tf_op jit(solution)/shard_map/mul | solution.py:257
  42.5 14.4 %convert_multiply_fusion = (f32[2048,128]{1,0:T(8,128)S(1)}, f32[2048,128]{1,0:T(8,128)S(1)}) fusion(f32[]{:T(128)} %bitcast.10, s32[2048]{0:T(1024)S(1)} %get-tuple-element.61, s32[]{:T(128)} %bitcast.6, s32[]{:T(128)} %bitcast.5, s32[2048]{0:T(1024)S(1)} %get-tuple-element.62, s32[]{:T(128)} %bitcast.1, pred[2048]{0:T(1024)(128)(4,1)S(1)} %get-tuple-element.59, ...), kind=kLoop, calls=%fused_computation.1 | loop fusion | flops 5242880 | bytes 2117652 | tf_op jit(solution)/shard_map/mul | solution.py:309
  56.9 19.3 %all-to-all-done.in_ref = bf16[16,4,128,128]{3,2,1,0:T(8,128)(2,1)} async-done(((bf16[16,4,128,128]{3,2,1,0:T(8,128)(2,1)}), bf16[16,4,128,128]{3,2,1,0:T(8,128)(2,1)}, u32[]{:S(2)}, u32[]{:S(2)}) %all-to-all-start) | async-done | bytes 2097184 | tf_op jit(solution)/shard_map/all_to_all | solution.py:293
  76.5 17.5 %shard_map.174 = bf16[16,400,128]{2,1,0:T(8,128)(2,1)S(1)} custom-call(s32[2,8]{1,0:T(2,128)S(1)} %pad_add_fusion.win_ref, f32[2048,128]{1,0:T(8,128)S(1)} %get-tuple-element.46.ka_ref, f32[2048,128]{1,0:T(8,128)S(1)} %get-tuple-element.45.kb_ref, f32[2048,128]{1,0:T(8,128)S(1)} %iota.81.kp_ref, f32[8,2048]{1,0:T(8,128)S(1)} %maximum_maximum_fusion.qi_ref, ...), custom_call_target="tpu_custom_call" | custom-call | tf_op jit(solution)/shard_map/pallas_call | solution.py:294
  94.1 47.2 %all_to_all.10.in_ref = bf16[16,400,128]{2,1,0:T(8,128)(2,1)S(1)} all-to-all(bf16[16,400,128]{2,1,0:T(8,128)(2,1)S(1)} %shard_map.174), channel_id=1, replica_groups=mesh['seq'=16,'head'=4,'dp'=4] {'seq'}, dimensions={0} | all-to-all | bytes 3276800 | tf_op jit(solution)/shard_map/all_to_all | solution.py:311
  141.3 1.0 shard_map.175
  142.3 1.3 collective-permute-start.3
  143.6 2.8 %collective-permute-start.5 = (bf16[3,32,640]{2,1,0:T(8,128)(2,1)S(1)}, bf16[3,32,640]{2,1,0:T(8,128)(2,1)S(1)}, u32[]{:S(2)}, u32[]{:S(2)}) collective-permute-start(bf16[3,32,640]{2,1,0:T(8,128)(2,1)S(1)} %get-tuple-element.33), channel_id=1, source_target_pairs={{0,12},{4,8},{8,4},{12,0},{1,13},{5,9},{9,5},{13,1},{2,14},{6,10},... | collective-permute-start | bytes 368648 | tf_op jit(solution)/shard_map/ppermute | solution.py:268
  146.4 3.6 %collective-permute-done.4.s2_ref = bf16[3,32,640]{2,1,0:T(8,128)(2,1)S(1)} collective-permute-done((bf16[3,32,640]{2,1,0:T(8,128)(2,1)S(1)}, bf16[3,32,640]{2,1,0:T(8,128)(2,1)S(1)}, u32[]{:S(2)}, u32[]{:S(2)}) %collective-permute-start.4) | collective-permute-done | bytes 122912 | tf_op jit(solution)/shard_map/ppermute | solution.py:268
  150.4 0.9 collective-permute-start.7
  151.4 2.8 %collective-permute-start.6 = (f32[2,5]{1,0:T(2,128)S(1)}, f32[2,5]{1,0:T(2,128)S(1)}, u32[]{:S(2)}, u32[]{:S(2)}) collective-permute-start(f32[2,5]{1,0:T(2,128)S(1)} %multiply_divide_fusion), channel_id=1, source_target_pairs={{0,1},{1,0},{2,3},{3,2},{4,5},{5,4},{6,7},{7,6},{8,9},{9,8},{10,11... | collective-permute-start | bytes 128 | tf_op jit(solution)/shard_map/ppermute | solution.py:327
  (44 shorter events, 8.9 us)
Async XLA Ops:
  2.7 10.2 %collective-permute-start = (bf16[4,32,640]{2,1,0:T(8,128)(2,1)}, bf16[4,32,640]{2,1,0:T(8,128)(2,1)S(1)}, u32[]{:S(2)}, u32[]{:S(2)}) collective-permute-start(bf16[4,32,640]{2,1,0:T(8,128)(2,1)} %get-tuple-element.25), channel_id=1, source_target_pairs={{0,4},{4,0},{8,12},{12,8},{1,5},{5,1},{9,13},{13,9},{2,6},{6,2},{1... | collective-permute-start | bytes 491528 | tf_op jit(solution)/shard_map/ppermute | solution.py:268
  4.3 10.5 %collective-permute-start.1 = (bf16[4,32,640]{2,1,0:T(8,128)(2,1)}, bf16[4,32,640]{2,1,0:T(8,128)(2,1)S(1)}, u32[]{:S(2)}, u32[]{:S(2)}) collective-permute-start(bf16[4,32,640]{2,1,0:T(8,128)(2,1)} %get-tuple-element.26), channel_id=1, source_target_pairs={{0,8},{4,12},{8,0},{12,4},{1,9},{5,13},{9,1},{13,5},{2,10},{6,14},... | collective-permute-start | bytes 491528 | tf_op jit(solution)/shard_map/ppermute | solution.py:268
  7.0 10.2 %collective-permute-start.2 = (bf16[4,32,640]{2,1,0:T(8,128)(2,1)}, bf16[4,32,640]{2,1,0:T(8,128)(2,1)S(1)}, u32[]{:S(2)}, u32[]{:S(2)}) collective-permute-start(bf16[4,32,640]{2,1,0:T(8,128)(2,1)} %get-tuple-element.27), channel_id=1, source_target_pairs={{0,12},{4,8},{8,4},{12,0},{1,13},{5,9},{9,5},{13,1},{2,14},{6,10},... | collective-permute-start | bytes 491528 | tf_op jit(solution)/shard_map/ppermute | solution.py:268
  7.5 1.0 copy-start
  8.5 1.0 copy-start.1
  9.4 0.9 copy-start.2
  10.3 0.9 copy-start.3
  11.3 5.9 %copy-start.4 = (bf16[4,32,640]{2,1,0:T(8,128)(2,1)S(1)}, bf16[4,32,640]{2,1,0:T(8,128)(2,1)}, u32[]{:S(2)}) copy-start(bf16[4,32,640]{2,1,0:T(8,128)(2,1)} %get-tuple-element.24.s0_ref) | copy-start | bytes 491524
  18.1 9.0 %copy-start.7 = (f32[2,5]{1,0:T(2,128)S(1)}, f32[2,5]{1,0:T(2,128)}, u32[]{:S(2)}) copy-start(f32[2,5]{1,0:T(2,128)} %param.20) | copy-start | bytes 124
  18.1 10.9 %copy-start.5 = (s32[1,4]{1,0:T(1,128)S(1)}, s32[1,4]{1,0:T(1,128)}, u32[]{:S(2)}) copy-start(s32[1,4]{1,0:T(1,128)} %param.21) | copy-start | bytes 52
  18.1 14.1 %copy-start.8 = (s32[1,4096]{1,0:T(1,128)S(1)}, s32[1,4096]{1,0:T(1,128)}, u32[]{:S(2)}) copy-start(s32[1,4096]{1,0:T(1,128)} %param.23) | copy-start | bytes 49156
  18.2 17.8 %copy-start.6 = (s32[1,4]{1,0:T(1,128)S(1)}, s32[1,4]{1,0:T(1,128)}, u32[]{:S(2)}) copy-start(s32[1,4]{1,0:T(1,128)} %param.22) | copy-start | bytes 52
  18.2 58.0 %all-to-all-start = ((bf16[16,4,128,128]{3,2,1,0:T(8,128)(2,1)}), bf16[16,4,128,128]{3,2,1,0:T(8,128)(2,1)}, u32[]{:S(2)}, u32[]{:S(2)}) async-start(bf16[16,4,128,128]{3,2,1,0:T(8,128)(2,1)} %shard_map.173), calls=%async_computation | async-start | bytes 4194304 | tf_op jit(solution)/shard_map/all_to_all | solution.py:293
  142.3 7.7 %collective-permute-start.4 = (bf16[3,32,640]{2,1,0:T(8,128)(2,1)S(1)}, bf16[3,32,640]{2,1,0:T(8,128)(2,1)S(1)}, u32[]{:S(2)}, u32[]{:S(2)}) collective-permute-start(bf16[3,32,640]{2,1,0:T(8,128)(2,1)S(1)} %get-tuple-element.31), channel_id=1, source_target_pairs={{0,8},{4,12},{8,0},{12,4},{1,9},{5,13},{9,1},{13,5},{2,10},{6,14},... | collective-permute-start | bytes 368648 | tf_op jit(solution)/shard_map/ppermute | solution.py:268
  142.3 11.9 %collective-permute-start.3 = (bf16[3,32,640]{2,1,0:T(8,128)(2,1)S(1)}, bf16[3,32,640]{2,1,0:T(8,128)(2,1)S(1)}, u32[]{:S(2)}, u32[]{:S(2)}) collective-permute-start(bf16[3,32,640]{2,1,0:T(8,128)(2,1)S(1)} %get-tuple-element.29), channel_id=1, source_target_pairs={{0,4},{4,0},{8,12},{12,8},{1,5},{5,1},{9,13},{13,9},{2,6},{6,2},{1... | collective-permute-start | bytes 368648 | tf_op jit(solution)/shard_map/ppermute | solution.py:268
  143.6 10.6 %collective-permute-start.5 = (bf16[3,32,640]{2,1,0:T(8,128)(2,1)S(1)}, bf16[3,32,640]{2,1,0:T(8,128)(2,1)S(1)}, u32[]{:S(2)}, u32[]{:S(2)}) collective-permute-start(bf16[3,32,640]{2,1,0:T(8,128)(2,1)S(1)} %get-tuple-element.33), channel_id=1, source_target_pairs={{0,12},{4,8},{8,4},{12,0},{1,13},{5,9},{9,5},{13,1},{2,14},{6,10},... | collective-permute-start | bytes 368648 | tf_op jit(solution)/shard_map/ppermute | solution.py:268
  150.0 5.0 %collective-permute-start.8 = (f32[2,5]{1,0:T(2,128)S(1)}, f32[2,5]{1,0:T(2,128)S(1)}, u32[]{:S(2)}, u32[]{:S(2)}) collective-permute-start(f32[2,5]{1,0:T(2,128)S(1)} %multiply_divide_fusion), channel_id=1, source_target_pairs={{0,3},{1,2},{2,1},{3,0},{4,7},{5,6},{6,5},{7,4},{8,11},{9,10},{10,... | collective-permute-start | bytes 128 | tf_op jit(solution)/shard_map/ppermute | solution.py:327
  150.4 5.1 %collective-permute-start.7 = (f32[2,5]{1,0:T(2,128)S(1)}, f32[2,5]{1,0:T(2,128)S(1)}, u32[]{:S(2)}, u32[]{:S(2)}) collective-permute-start(f32[2,5]{1,0:T(2,128)S(1)} %multiply_divide_fusion), channel_id=1, source_target_pairs={{0,2},{1,3},{2,0},{3,1},{4,6},{5,7},{6,4},{7,5},{8,10},{9,11},{10,... | collective-permute-start | bytes 128 | tf_op jit(solution)/shard_map/ppermute | solution.py:327
  151.4 4.3 %collective-permute-start.6 = (f32[2,5]{1,0:T(2,128)S(1)}, f32[2,5]{1,0:T(2,128)S(1)}, u32[]{:S(2)}, u32[]{:S(2)}) collective-permute-start(f32[2,5]{1,0:T(2,128)S(1)} %multiply_divide_fusion), channel_id=1, source_target_pairs={{0,1},{1,0},{2,3},{3,2},{4,5},{5,4},{6,7},{7,6},{8,9},{9,8},{10,11... | collective-permute-start | bytes 128 | tf_op jit(solution)/shard_map/ppermute | solution.py:327

commit v5 on v4

--- a/solution.py
+++ b/solution.py
@@ -17,7 +17,7 @@
 BLK = 128
 HS = 128
 QB = 256
-NARROW = 9
+SIZES = (6, 9, 12, 16)
 
 
 def vmem_call(body, out_shapes, **kw):
@@ -106,15 +106,13 @@
 
 def attend(
     win_ref, ka_ref, kb_ref, kp_ref, qi_ref, in_ref, out_ref,
-    k_buf, v_buf, kt_buf, t_buf, d_buf, ds_buf, dk_acc, dv_acc, slope_ref,
+    kt_buf, t_buf, d_buf, ds_buf, dk_acc, dv_acc, slope_ref,
 ):
     inv_root = HS ** (-0.5)
     blocks = TASKS * BLK // QB
     per = QB // BLK
     for s in range(TASKS):
-        k_buf[s * BLK : (s + 1) * BLK] = in_ref[s, 1]
-        v_buf[s * BLK : (s + 1) * BLK] = in_ref[s, 2]
-        kt_buf[s] = in_ref[s, 1].astype(F32).T.astype(BF)
+        kt_buf[s] = in_ref[s, 1].T
     dk_acc[...] = jnp.zeros_like(dk_acc)
     dv_acc[...] = jnp.zeros_like(dv_acc)
     slope_ref[...] = jnp.zeros_like(slope_ref)
@@ -140,9 +138,9 @@
         top = jnp.full((8, QB), -jnp.inf, F32)
         for t in range(tiles):
             r = rows(t)
-            s = lax.dot_general(k_buf[r], q, nt, preferred_element_type=F32)
+            s = lax.dot_general(in_ref[first + t, 1], q, nt, preferred_element_type=F32)
             d_buf[t * BLK : (t + 1) * BLK] = lax.dot_general(
-                v_buf[r], g, nt, preferred_element_type=F32
+                in_ref[first + t, 2], g, nt, preferred_element_type=F32
             )
             gap = jnp.abs(wide_lanes(ka_ref[r]) - qa) + jnp.abs(wide_lanes(kb_ref[r]) - qb)
             logit = jnp.where(
@@ -186,15 +184,11 @@
             slope_ref[row : row + 1] += sum(v[:, i * BLK : (i + 1) * BLK] for i in range(per))
 
     def step(b, _):
-        wide = win_ref[1, b]
-
-        @pl.when(wide == 0)
-        def _():
-            work(b, win_ref[0, b], NARROW)
-
-        @pl.when(wide != 0)
-        def _():
-            work(b, 0, TASKS)
+        for kind, tiles in enumerate(SIZES):
+
+            @pl.when(win_ref[1, b] == kind)
+            def _(tiles=tiles):
+                work(b, win_ref[0, b], tiles)
 
         return 0
 
@@ -257,9 +251,14 @@
     q_info = jnp.stack([pos_row * sa, pos_col * sb, q_id.astype(F32)])
     q_info = jnp.concatenate([q_info, jnp.zeros((5, patches), F32)])
     blocks = q_id.reshape(-1, QB)
-    low = jnp.minimum(by_page(blocks[:, 0], starts) // BLK, TASKS - NARROW)
-    wide = by_page(blocks[:, -1], ends) > (low + NARROW) * BLK
-    window = jnp.stack([low, wide.astype(jnp.int32)])
+    low = by_page(blocks[:, 0], starts) // BLK
+    high = (by_page(blocks[:, -1], ends) + BLK - 1) // BLK
+    first, kind = jnp.zeros_like(low), jnp.full_like(low, len(SIZES) - 1)
+    for i in reversed(range(len(SIZES) - 1)):
+        at = jnp.minimum(low, TASKS - SIZES[i])
+        fits = high <= at + SIZES[i]
+        first, kind = jnp.where(fits, at, first), jnp.where(fits, i, kind)
+    window = jnp.stack([first, kind])
 
     def swap_heads(parts):
         own, out = parts[0], [None] * 4
@@ -296,8 +295,6 @@
         sds((TASKS, 3 * BLK + 16, HS), BF),
         in_specs=[pl.BlockSpec(memory_space=pltpu.SMEM)] + [vm] * 5,
         scratch_shapes=[
-            pltpu.VMEM((patches, HS), BF),
-            pltpu.VMEM((patches, HS), BF),
             pltpu.VMEM((TASKS, HS, BLK), BF),
             pltpu.VMEM((patches, QB), F32),
             pltpu.VMEM((patches, QB), F32),
@@ -321,7 +318,7 @@
         ),
     )(back)
     self_out = swap_heads(self_out)
-    slope_sum, self_out[2] = lax.optimization_barrier((slope_sum, self_out[2]))
+    slope_sum, self_out[1] = lax.optimization_barrier((slope_sum, self_out[1]))
     slope_sum = jnp.sum(slope_sum[:, :HEADS], axis=2) / (slopes * (LOG2E * -patches))
     near, far, last = (
         lax.ppermute(slope_sum, "dp", [(i, i ^ gap) for i in range(4)])

time: 157 us -> 156 us (level); the launches traced: 156 us -> 154 us
  Pallas kernels: 23.9 us -> 20.2 us
  starting transfers between devices: 22 us -> 24.2 us
    pallas_call x1, Pallas kernels: 17.5 us -> 13.8 us  [local(): vmem_call(attend, sds((TASKS, 3 * BLK + 16, HS), BF), in_specs=[pl.BlockS...]
    ppermute x6, waiting for transfers between devices: 7.86 us -> 5.73 us  [swap_heads(): out[gap] = lax.ppermute(parts[gap], 'head', swap)]
    ppermute x3, starting transfers between devices: 4.14 us -> 5.73 us  [local(): lax.ppermute(slope_sum, 'dp', [(i, i ^ gap) for i in range(4)])]
  transfers between devices with their start and end apart: 10 -> 10, of which waited for: 6 -> 5; matrix products, arithmetic and copies ran while one was open for 17% -> 17% of each run, Pallas kernels for 2% -> 2%
where the time goes in v5:
time: 156 us; the launch traced here: 154 us
  blocking collectives  47.2 us (30%)
  waiting for transfers between devices  26.8 us (17%)
  other arithmetic  24.6 us (16%)
  starting transfers between devices  24.2 us (16%)
  Pallas kernels  20.2 us (13%)
  local copies, waits for them, and re-layouts  5.92 us (4%)
  between operations  4.74 us (3%)
    all_to_all x1, blocking collectives, local(): back = lax.all_to_all(back, 'seq', split_axis=0, concat_axis=0, tiled=True)  47.2 us
    all_to_all x1, waiting for transfers between devices, local(): held = lax.all_to_all(sent, 'seq', split_axis=0, concat_axis=0, tiled=True)  19.3 us
    mul x1, other arithmetic, local(): key_col * sb  14.4 us
    pallas_call x1, Pallas kernels, local(): vmem_call(attend, sds((TASKS, 3 * BLK + 16, HS), BF), in_specs=[pl.BlockS...  13.8 us
    ppermute x6, starting transfers between devices, swap_heads(): out[gap] = lax.ppermute(parts[gap], 'head', swap)  9.48 us
    all_to_all x1, starting transfers between devices, local(): held = lax.all_to_all(sent, 'seq', split_axis=0, concat_axis=0, tiled=True)  8.95 us
    ppermute x6, waiting for transfers between devices, swap_heads(): out[gap] = lax.ppermute(parts[gap], 'head', swap)  5.73 us
    ppermute x3, starting transfers between devices, local(): lax.ppermute(slope_sum, 'dp', [(i, i ^ gap) for i in range(4)])  5.73 us
  transfers between devices with their start and end apart: 10, of which 5 were waited for; matrix products, arithmetic and copies ran while one was open for 17% of the time, Pallas kernels for 2%

profile of v5, /device:TPU:8, one launch (start us, length us, event | category | flops | bytes accessed | tf_op | source)
XLA Modules:
  0.0 153.6 jit_solution(10138444429548402692)
XLA Ops:
  0.6 2.1 %shard_map.171 = (bf16[4,32,640]{2,1,0:T(8,128)(2,1)}, bf16[4,32,640]{2,1,0:T(8,128)(2,1)}, bf16[4,32,640]{2,1,0:T(8,128)(2,1)}, bf16[4,32,640]{2,1,0:T(8,128)(2,1)}) custom-call(bf16[1,32,2560]{2,1,0:T(8,128)(2,1)} %q_ref.1, bf16[1,32,2560]{2,1,0:T(8,128)(2,1)} %k_ref.1, bf16[1,32,2560]{2,1,0:T(8,128)(2,1)} %v_ref.1, bf16[1,32,2560]{2,1,0:T(8,128)(2,1)} %g_ref.1), custom_call_target="tpu_custom_call" | custom-call | tf_op jit(solution)/shard_map/pallas_call | solution.py:271
  2.7 1.6 %collective-permute-start = (bf16[4,32,640]{2,1,0:T(8,128)(2,1)}, bf16[4,32,640]{2,1,0:T(8,128)(2,1)S(1)}, u32[]{:S(2)}, u32[]{:S(2)}) collective-permute-start(bf16[4,32,640]{2,1,0:T(8,128)(2,1)} %get-tuple-element.25), channel_id=1, source_target_pairs={{0,4},{4,0},{8,12},{12,8},{1,5},{5,1},{9,13},{13,9},{2,6},{6,2},{1... | collective-permute-start | bytes 491528 | tf_op jit(solution)/shard_map/ppermute | solution.py:267
  4.3 2.7 %collective-permute-start.1 = (bf16[4,32,640]{2,1,0:T(8,128)(2,1)}, bf16[4,32,640]{2,1,0:T(8,128)(2,1)S(1)}, u32[]{:S(2)}, u32[]{:S(2)}) collective-permute-start(bf16[4,32,640]{2,1,0:T(8,128)(2,1)} %get-tuple-element.26), channel_id=1, source_target_pairs={{0,8},{4,12},{8,0},{12,4},{1,9},{5,13},{9,1},{13,5},{2,10},{6,14},... | collective-permute-start | bytes 491528 | tf_op jit(solution)/shard_map/ppermute | solution.py:267
  7.5 1.0 copy-done
  8.5 1.0 copy-done.1
  11.3 1.6 %shard_map.172.text_ref = bf16[16,4,128,128]{3,2,1,0:T(8,128)(2,1)} custom-call(bf16[1,256,640]{2,1,0:T(8,128)(2,1)S(1)} %copy-done, bf16[1,128,640]{2,1,0:T(8,128)(2,1)S(1)} %copy-done.2, bf16[1,128,640]{2,1,0:T(8,128)(2,1)S(1)} %copy-done.3, bf16[1,256,640]{2,1,0:T(8,128)(2,1)S(1)} %copy-done.1), custom_call_target="tpu_custom_call" | custom-call | tf_op jit(solution)/shard_map/pallas_call | solution.py:280
  12.9 1.9 %collective-permute-done.1.s2_ref = bf16[4,32,640]{2,1,0:T(8,128)(2,1)S(1)} collective-permute-done((bf16[4,32,640]{2,1,0:T(8,128)(2,1)}, bf16[4,32,640]{2,1,0:T(8,128)(2,1)S(1)}, u32[]{:S(2)}, u32[]{:S(2)}) %collective-permute-start.1) | collective-permute-done | bytes 163872 | tf_op jit(solution)/shard_map/ppermute | solution.py:267
  14.7 2.4 %collective-permute-done.2.s3_ref = bf16[4,32,640]{2,1,0:T(8,128)(2,1)S(1)} collective-permute-done((bf16[4,32,640]{2,1,0:T(8,128)(2,1)}, bf16[4,32,640]{2,1,0:T(8,128)(2,1)S(1)}, u32[]{:S(2)}, u32[]{:S(2)}) %collective-permute-start.2) | collective-permute-done | bytes 163872 | tf_op jit(solution)/shard_map/ppermute | solution.py:267
  17.2 1.0 shard_map.173
  18.2 8.9 %all-to-all-start = ((bf16[16,4,128,128]{3,2,1,0:T(8,128)(2,1)}), bf16[16,4,128,128]{3,2,1,0:T(8,128)(2,1)}, u32[]{:S(2)}, u32[]{:S(2)}) async-start(bf16[16,4,128,128]{3,2,1,0:T(8,128)(2,1)} %shard_map.173), calls=%async_computation | async-start | bytes 4194304 | tf_op jit(solution)/shard_map/all_to_all | solution.py:292
  36.5 1.9 %broadcast_select_fusion.1 = (s32[2048]{0:T(1024)S(1)}, s32[2048]{0:T(1024)S(1)}) fusion(s32[]{:T(128)} %bitcast.8, s32[]{:T(128)} %bitcast.7, s32[]{:T(128)S(6)} %add.181, s32[]{:T(128)S(6)} %add.179, s32[]{:T(128)} %bitcast.1), kind=kLoop, calls=%fused_computation.41 | loop fusion | flops 22528 | bytes 16404 | tf_op jit(solution)/shard_map/jit(_where)/select_n | solution.py:231
  38.5 4.0 %convert_multiply_fusion.2 = (f32[1,2048]{1,0:T(1,128)S(1)}, f32[1,2048]{1,0:T(1,128)S(1)}) fusion(f32[]{:T(128)} %bitcast.10, s32[]{:T(128)S(6)} %add.181, s32[]{:T(128)S(6)} %add.179, s32[]{:T(128)} %bitcast.1, s32[]{:T(128)} %bitcast.8, s32[]{:T(128)} %bitcast.7, s32[]{:T(128)} %bitcast.6, s32[]{:T(128)} %bitcast.5, f32[]{:T(128)} %bitcast.9), kind=kLoop, calls=%fused_computation.25 | loop fusion | flops 67584 | bytes 16420 | tf_op jit(solution)/shard_map/mul | solution.py:251
  42.5 14.4 %convert_multiply_fusion = (f32[2048,128]{1,0:T(8,128)S(1)}, f32[2048,128]{1,0:T(8,128)S(1)}) fusion(f32[]{:T(128)} %bitcast.10, s32[2048]{0:T(1024)S(1)} %get-tuple-element.63, s32[]{:T(128)} %bitcast.6, s32[]{:T(128)} %bitcast.5, s32[2048]{0:T(1024)S(1)} %get-tuple-element.64, s32[]{:T(128)} %bitcast.1, pred[2048]{0:T(1024)(128)(4,1)S(1)} %get-tuple-element.61, ...), kind=kLoop, calls=%fused_computation.1 | loop fusion | flops 5242880 | bytes 2117652 | tf_op jit(solution)/shard_map/mul | solution.py:306
  56.9 19.3 %all-to-all-done.in_ref = bf16[16,4,128,128]{3,2,1,0:T(8,128)(2,1)} async-done(((bf16[16,4,128,128]{3,2,1,0:T(8,128)(2,1)}), bf16[16,4,128,128]{3,2,1,0:T(8,128)(2,1)}, u32[]{:S(2)}, u32[]{:S(2)}) %all-to-all-start) | async-done | bytes 2097184 | tf_op jit(solution)/shard_map/all_to_all | solution.py:292
  76.5 13.8 %shard_map.174 = bf16[16,400,128]{2,1,0:T(8,128)(2,1)S(1)} custom-call(s32[2,8]{1,0:T(2,128)S(1)} %pad_add_fusion.win_ref, f32[2048,128]{1,0:T(8,128)S(1)} %get-tuple-element.46.ka_ref, f32[2048,128]{1,0:T(8,128)S(1)} %get-tuple-element.45.kb_ref, f32[2048,128]{1,0:T(8,128)S(1)} %iota.81.kp_ref, f32[8,2048]{1,0:T(8,128)S(1)} %maximum_maximum_fusion.qi_ref, ...), custom_call_target="tpu_custom_call" | custom-call | tf_op jit(solution)/shard_map/pallas_call | solution.py:293
  90.3 47.2 %all_to_all.10.in_ref = bf16[16,400,128]{2,1,0:T(8,128)(2,1)S(1)} all-to-all(bf16[16,400,128]{2,1,0:T(8,128)(2,1)S(1)} %shard_map.174), channel_id=1, replica_groups=mesh['seq'=16,'head'=4,'dp'=4] {'seq'}, dimensions={0} | all-to-all | bytes 3276800 | tf_op jit(solution)/shard_map/all_to_all | solution.py:308
  137.5 1.0 shard_map.175
  138.5 1.9 %collective-permute-start.4 = (bf16[3,32,640]{2,1,0:T(8,128)(2,1)S(1)}, bf16[3,32,640]{2,1,0:T(8,128)(2,1)S(1)}, u32[]{:S(2)}, u32[]{:S(2)}) collective-permute-start(bf16[3,32,640]{2,1,0:T(8,128)(2,1)S(1)} %get-tuple-element.32), channel_id=1, source_target_pairs={{0,8},{4,12},{8,0},{12,4},{1,9},{5,13},{9,1},{13,5},{2,10},{6,14},... | collective-permute-start | bytes 368648 | tf_op jit(solution)/shard_map/ppermute | solution.py:267
  140.4 2.8 %collective-permute-start.5 = (bf16[3,32,640]{2,1,0:T(8,128)(2,1)S(1)}, bf16[3,32,640]{2,1,0:T(8,128)(2,1)S(1)}, u32[]{:S(2)}, u32[]{:S(2)}) collective-permute-start(bf16[3,32,640]{2,1,0:T(8,128)(2,1)S(1)} %get-tuple-element.33), channel_id=1, source_target_pairs={{0,12},{4,8},{8,4},{12,0},{1,13},{5,9},{9,5},{13,1},{2,14},{6,10},... | collective-permute-start | bytes 368648 | tf_op jit(solution)/shard_map/ppermute | solution.py:267
  143.2 1.4 collective-permute-done.3.s1_ref
  144.7 3.3 %collective-permute-start.8 = (f32[2,5]{1,0:T(2,128)S(1)}, f32[2,5]{1,0:T(2,128)S(1)}, u32[]{:S(2)}, u32[]{:S(2)}) collective-permute-start(f32[2,5]{1,0:T(2,128)S(1)} %multiply_divide_fusion), channel_id=1, source_target_pairs={{0,3},{1,2},{2,1},{3,0},{4,7},{5,6},{6,5},{7,4},{8,11},{9,10},{10,... | collective-permute-start | bytes 128 | tf_op jit(solution)/shard_map/ppermute | solution.py:324
  148.0 1.4 collective-permute-start.7
  149.4 1.1 collective-permute-start.6
  151.3 1.8 %collective-permute-done.7 = f32[2,5]{1,0:T(2,128)S(1)} collective-permute-done((f32[2,5]{1,0:T(2,128)S(1)}, f32[2,5]{1,0:T(2,128)S(1)}, u32[]{:S(2)}, u32[]{:S(2)}) %collective-permute-start.7) | collective-permute-done | bytes 72 | tf_op jit(solution)/shard_map/ppermute | solution.py:324
  (43 shorter events, 9.6 us)
Async XLA Ops:
  2.7 10.2 %collective-permute-start = (bf16[4,32,640]{2,1,0:T(8,128)(2,1)}, bf16[4,32,640]{2,1,0:T(8,128)(2,1)S(1)}, u32[]{:S(2)}, u32[]{:S(2)}) collective-permute-start(bf16[4,32,640]{2,1,0:T(8,128)(2,1)} %get-tuple-element.25), channel_id=1, source_target_pairs={{0,4},{4,0},{8,12},{12,8},{1,5},{5,1},{9,13},{13,9},{2,6},{6,2},{1... | collective-permute-start | bytes 491528 | tf_op jit(solution)/shard_map/ppermute | solution.py:267
  4.3 10.5 %collective-permute-start.1 = (bf16[4,32,640]{2,1,0:T(8,128)(2,1)}, bf16[4,32,640]{2,1,0:T(8,128)(2,1)S(1)}, u32[]{:S(2)}, u32[]{:S(2)}) collective-permute-start(bf16[4,32,640]{2,1,0:T(8,128)(2,1)} %get-tuple-element.26), channel_id=1, source_target_pairs={{0,8},{4,12},{8,0},{12,4},{1,9},{5,13},{9,1},{13,5},{2,10},{6,14},... | collective-permute-start | bytes 491528 | tf_op jit(solution)/shard_map/ppermute | solution.py:267
  7.0 10.2 %collective-permute-start.2 = (bf16[4,32,640]{2,1,0:T(8,128)(2,1)}, bf16[4,32,640]{2,1,0:T(8,128)(2,1)S(1)}, u32[]{:S(2)}, u32[]{:S(2)}) collective-permute-start(bf16[4,32,640]{2,1,0:T(8,128)(2,1)} %get-tuple-element.27), channel_id=1, source_target_pairs={{0,12},{4,8},{8,4},{12,0},{1,13},{5,9},{9,5},{13,1},{2,14},{6,10},... | collective-permute-start | bytes 491528 | tf_op jit(solution)/shard_map/ppermute | solution.py:267
  7.5 1.0 copy-start
  8.5 1.0 copy-start.1
  9.4 0.9 copy-start.2
  10.3 0.9 copy-start.3
  11.3 5.9 %copy-start.4 = (bf16[4,32,640]{2,1,0:T(8,128)(2,1)S(1)}, bf16[4,32,640]{2,1,0:T(8,128)(2,1)}, u32[]{:S(2)}) copy-start(bf16[4,32,640]{2,1,0:T(8,128)(2,1)} %get-tuple-element.24.s0_ref) | copy-start | bytes 491524
  18.1 9.0 %copy-start.7 = (f32[2,5]{1,0:T(2,128)S(1)}, f32[2,5]{1,0:T(2,128)}, u32[]{:S(2)}) copy-start(f32[2,5]{1,0:T(2,128)} %param.20) | copy-start | bytes 124
  18.1 10.9 %copy-start.5 = (s32[1,4]{1,0:T(1,128)S(1)}, s32[1,4]{1,0:T(1,128)}, u32[]{:S(2)}) copy-start(s32[1,4]{1,0:T(1,128)} %param.21) | copy-start | bytes 52
  18.2 14.1 %copy-start.8 = (s32[1,4096]{1,0:T(1,128)S(1)}, s32[1,4096]{1,0:T(1,128)}, u32[]{:S(2)}) copy-start(s32[1,4096]{1,0:T(1,128)} %param.23) | copy-start | bytes 49156
  18.2 17.7 %copy-start.6 = (s32[1,4]{1,0:T(1,128)S(1)}, s32[1,4]{1,0:T(1,128)}, u32[]{:S(2)}) copy-start(s32[1,4]{1,0:T(1,128)} %param.22) | copy-start | bytes 52
  18.2 58.0 %all-to-all-start = ((bf16[16,4,128,128]{3,2,1,0:T(8,128)(2,1)}), bf16[16,4,128,128]{3,2,1,0:T(8,128)(2,1)}, u32[]{:S(2)}, u32[]{:S(2)}) async-start(bf16[16,4,128,128]{3,2,1,0:T(8,128)(2,1)} %shard_map.173), calls=%async_computation | async-start | bytes 4194304 | tf_op jit(solution)/shard_map/all_to_all | solution.py:292
  138.5 6.1 %collective-permute-start.3 = (bf16[3,32,640]{2,1,0:T(8,128)(2,1)S(1)}, bf16[3,32,640]{2,1,0:T(8,128)(2,1)S(1)}, u32[]{:S(2)}, u32[]{:S(2)}) collective-permute-start(bf16[3,32,640]{2,1,0:T(8,128)(2,1)S(1)} %get-tuple-element.30), channel_id=1, source_target_pairs={{0,4},{4,0},{8,12},{12,8},{1,5},{5,1},{9,13},{13,9},{2,6},{6,2},{1... | collective-permute-start | bytes 368648 | tf_op jit(solution)/shard_map/ppermute | solution.py:267
  138.5 12.0 %collective-permute-start.4 = (bf16[3,32,640]{2,1,0:T(8,128)(2,1)S(1)}, bf16[3,32,640]{2,1,0:T(8,128)(2,1)S(1)}, u32[]{:S(2)}, u32[]{:S(2)}) collective-permute-start(bf16[3,32,640]{2,1,0:T(8,128)(2,1)S(1)} %get-tuple-element.32), channel_id=1, source_target_pairs={{0,8},{4,12},{8,0},{12,4},{1,9},{5,13},{9,1},{13,5},{2,10},{6,14},... | collective-permute-start | bytes 368648 | tf_op jit(solution)/shard_map/ppermute | solution.py:267
  140.4 10.0 %collective-permute-start.5 = (bf16[3,32,640]{2,1,0:T(8,128)(2,1)S(1)}, bf16[3,32,640]{2,1,0:T(8,128)(2,1)S(1)}, u32[]{:S(2)}, u32[]{:S(2)}) collective-permute-start(bf16[3,32,640]{2,1,0:T(8,128)(2,1)S(1)} %get-tuple-element.33), channel_id=1, source_target_pairs={{0,12},{4,8},{8,4},{12,0},{1,13},{5,9},{9,5},{13,1},{2,14},{6,10},... | collective-permute-start | bytes 368648 | tf_op jit(solution)/shard_map/ppermute | solution.py:267
  144.7 6.6 %collective-permute-start.8 = (f32[2,5]{1,0:T(2,128)S(1)}, f32[2,5]{1,0:T(2,128)S(1)}, u32[]{:S(2)}, u32[]{:S(2)}) collective-permute-start(f32[2,5]{1,0:T(2,128)S(1)} %multiply_divide_fusion), channel_id=1, source_target_pairs={{0,3},{1,2},{2,1},{3,0},{4,7},{5,6},{6,5},{7,4},{8,11},{9,10},{10,... | collective-permute-start | bytes 128 | tf_op jit(solution)/shard_map/ppermute | solution.py:324
  148.0 5.1 %collective-permute-start.7 = (f32[2,5]{1,0:T(2,128)S(1)}, f32[2,5]{1,0:T(2,128)S(1)}, u32[]{:S(2)}, u32[]{:S(2)}) collective-permute-start(f32[2,5]{1,0:T(2,128)S(1)} %multiply_divide_fusion), channel_id=1, source_target_pairs={{0,2},{1,3},{2,0},{3,1},{4,6},{5,7},{6,4},{7,5},{8,10},{9,11},{10,... | collective-permute-start | bytes 128 | tf_op jit(solution)/shard_map/ppermute | solution.py:324
  149.4 3.7 %collective-permute-start.6 = (f32[2,5]{1,0:T(2,128)S(1)}, f32[2,5]{1,0:T(2,128)S(1)}, u32[]{:S(2)}, u32[]{:S(2)}) collective-permute-start(f32[2,5]{1,0:T(2,128)S(1)} %multiply_divide_fusion), channel_id=1, source_target_pairs={{0,1},{1,0},{2,3},{3,2},{4,5},{5,4},{6,7},{7,6},{8,9},{9,8},{10,11... | collective-permute-start | bytes 128 | tf_op jit(solution)/shard_map/ppermute | solution.py:324

commit v6 on v5

--- a/solution.py
+++ b/solution.py
@@ -24,7 +24,7 @@
     return pl.pallas_call(
         body,
         out_shape=out_shapes,
-        compiler_params=pltpu.CompilerParams(vmem_limit_bytes=48 * 2**20),
+        compiler_params=pltpu.CompilerParams(vmem_limit_bytes=24 * 2**20),
         **kw,
     )
 
@@ -105,14 +105,28 @@
 
 
 def attend(
-    win_ref, ka_ref, kb_ref, kp_ref, qi_ref, in_ref, out_ref,
-    kt_buf, t_buf, d_buf, ds_buf, dk_acc, dv_acc, slope_ref,
+    win_ref, page_ref, qi_ref, in_ref, out_ref,
+    ka_ref, kb_ref, kp_ref, kt_buf, t_buf, d_buf, ds_buf, dk_acc, dv_acc, slope_ref,
 ):
     inv_root = HS ** (-0.5)
     blocks = TASKS * BLK // QB
     per = QB // BLK
     for s in range(TASKS):
+        here = slice(s * BLK, (s + 1) * BLK)
         kt_buf[s] = in_ref[s, 1].T
+        pos = (lax.broadcasted_iota(jnp.int32, (BLK, BLK), 0) + s * BLK).astype(F32)
+        begin, width, inv, page = (jnp.full((BLK, BLK), v, F32) for v in (0.0, page_ref[3, 0], page_ref[4, 0], 0.0))
+        for i in range(1, 4):
+            later = pos >= page_ref[2, i]
+            begin = jnp.where(later, page_ref[2, i], begin)
+            width = jnp.where(later, page_ref[3, i], width)
+            inv = jnp.where(later, page_ref[4, i], inv)
+            page = jnp.where(later, float(i), page)
+        off = pos - begin
+        row = jnp.floor((off + 0.5) * inv)
+        ka_ref[here] = row * page_ref[0, 0]
+        kb_ref[here] = (off - row * width) * page_ref[1, 0]
+        kp_ref[here] = page
     dk_acc[...] = jnp.zeros_like(dk_acc)
     dv_acc[...] = jnp.zeros_like(dv_acc)
     slope_ref[...] = jnp.zeros_like(slope_ref)
@@ -234,15 +248,22 @@
     def layout(pos):
         ids = sum((pos >= e).astype(jnp.int32) for e in ends[:3])
         width = by_page(ids, [widths[i] for i in range(4)])
-        off = pos - by_page(ids, starts)
-        row = off // width
-        return ids, row.astype(F32), (off - row * width).astype(F32)
+        off = (pos - by_page(ids, starts)).astype(F32)
+        row = jnp.floor((off + 0.5) / width.astype(F32))
+        return ids, row, off - row * width.astype(F32)
 
     own = jnp.clip(task - TEXT_TASKS, 0, HEADS - 1)
     slope = jnp.where(is_text, 0.0, lax.dynamic_slice_in_dim(slopes, own, 1, 1)[:, 0])
     sa, sb = slope[0] * LOG2E, slope[1] * LOG2E
-    key_id, key_row, key_col = layout(
-        lax.broadcasted_iota(jnp.int32, (patches, BLK), 0)
+    as_row = lambda values: jnp.stack([jnp.asarray(v, F32) for v in values])
+    pages = jnp.stack(
+        [
+            as_row([sa] * 4),
+            as_row([sb] * 4),
+            as_row(starts),
+            widths.astype(F32),
+            1.0 / widths.astype(F32),
+        ]
     )
     pos_id, pos_row, pos_col = layout(jnp.arange(patches, dtype=jnp.int32))
     halves = text_page[0].reshape(TASKS, 2, BLK)
@@ -293,8 +314,11 @@
     back = vmem_call(
         attend,
         sds((TASKS, 3 * BLK + 16, HS), BF),
-        in_specs=[pl.BlockSpec(memory_space=pltpu.SMEM)] + [vm] * 5,
+        in_specs=[pl.BlockSpec(memory_space=pltpu.SMEM)] * 2 + [vm] * 2,
         scratch_shapes=[
+            pltpu.VMEM((patches, BLK), F32),
+            pltpu.VMEM((patches, BLK), F32),
+            pltpu.VMEM((patches, BLK), F32),
             pltpu.VMEM((TASKS, HS, BLK), BF),
             pltpu.VMEM((patches, QB), F32),
             pltpu.VMEM((patches, QB), F32),
@@ -303,7 +327,7 @@
             pltpu.VMEM((patches, HS), F32),
             pltpu.VMEM((8, BLK), F32),
         ],
-    )(window, key_row * sa, key_col * sb, key_id.astype(F32), q_info, held)
+    )(window, pages, q_info, held)
 
     back = lax.all_to_all(back, "seq", split_axis=0, concat_axis=0, tiled=True)
     part = sds((3, 32, HEADS * HS), BF)
@@ -317,14 +341,12 @@
             *(part,) * 4,
         ),
     )(back)
+    slope_sum = slope_sum + lax.ppermute(slope_sum, "dp", [(i, i ^ 1) for i in range(4)])
     self_out = swap_heads(self_out)
     slope_sum, self_out[1] = lax.optimization_barrier((slope_sum, self_out[1]))
-    slope_sum = jnp.sum(slope_sum[:, :HEADS], axis=2) / (slopes * (LOG2E * -patches))
-    near, far, last = (
-        lax.ppermute(slope_sum, "dp", [(i, i ^ gap) for i in range(4)])
-        for gap in (1, 2, 3)
-    )
-    slope_grad = (slope_sum + near) + (far + last)
+    slope_sum = slope_sum + lax.ppermute(slope_sum, "dp", [(i, i ^ 2) for i in range(4)])
+    slope_sum = jnp.sum(slope_sum[:, :HEADS], axis=2)
+    slope_grad = slope_sum / (slopes * (LOG2E * -patches))
     shape = sds(self_queries.shape, BF)
     self_dq, self_dk, self_dv = vmem_call(unpack_self, (shape, shape, shape))(*self_out)
     return self_dq, self_dk, self_dv, slope_grad, text_dq, mem_dk, mem_dv

time: 156 us -> 154 us (0.987); the launches traced: 154 us -> 153 us
  waiting for transfers between devices: 26.8 us -> 47.6 us
  other arithmetic: 24.6 us -> 6.4 us
  starting transfers between devices: 24.2 us -> 19.8 us
    all_to_all x1, waiting for transfers between devices: 19.3 us -> 36.9 us  [local(): held = lax.all_to_all(sent, 'seq', split_axis=0, concat_axis=0, tiled=True)]
    mul x1 -> x0, other arithmetic: 14.4 us -> none  [local(): key_col * sb]
    ppermute x3 -> x2, waiting for transfers between devices: 1.77 us -> 5.89 us  [the longest x1 3.65 us: local(): lax.ppermute(slope_sum, 'dp', [(i, i ^ 1) for i in range(4)])]
    ppermute x3 -> x2, starting transfers between devices: 5.73 us -> 1.62 us  [the longest x1 1.62 us: local(): lax.ppermute(slope_sum, 'dp', [(i, i ^ 2) for i in range(4)])]
    select_n x1 -> x0, other arithmetic: 1.95 us -> none  [by_page(): out = jnp.where(ids == i, per_page[i], out)]
  transfers between devices with their start and end apart: 10 -> 9, of which waited for: 5 -> 6; matrix products, arithmetic and copies ran while one was open for 17% -> 5% of each run, Pallas kernels for 2% -> 2%
where the time goes in v6:
time: 154 us; the launch traced here: 153 us
  waiting for transfers between devices  47.6 us (31%)
  blocking collectives  47 us (31%)
  Pallas kernels  21.5 us (14%)
  starting transfers between devices  19.8 us (13%)
  other arithmetic  6.4 us (4%)
  local copies, waits for them, and re-layouts  5.62 us (4%)
  between operations  5.37 us (3%)
    all_to_all x1, blocking collectives, local(): back = lax.all_to_all(back, 'seq', split_axis=0, concat_axis=0, tiled=True)  47 us
    all_to_all x1, waiting for transfers between devices, local(): held = lax.all_to_all(sent, 'seq', split_axis=0, concat_axis=0, tiled=True)  36.9 us
    pallas_call x1, Pallas kernels, local(): vmem_call(attend, sds((TASKS, 3 * BLK + 16, HS), BF), in_specs=[pl.BlockS...  15.1 us
    ppermute x6, starting transfers between devices, swap_heads(): out[gap] = lax.ppermute(parts[gap], 'head', swap)  9.48 us
    all_to_all x1, starting transfers between devices, local(): held = lax.all_to_all(sent, 'seq', split_axis=0, concat_axis=0, tiled=True)  8.72 us
    ppermute x6, waiting for transfers between devices, swap_heads(): out[gap] = lax.ppermute(parts[gap], 'head', swap)  4.73 us
    unnamed x18, local copies, waits for them, and re-layouts  3.8 us
    ppermute x1, waiting for transfers between devices, local(): lax.ppermute(slope_sum, 'dp', [(i, i ^ 1) for i in range(4)])  3.65 us
  transfers between devices with their start and end apart: 9, of which 6 were waited for; matrix products, arithmetic and copies ran while one was open for 5% of the time, Pallas kernels for 2%

profile of v6, /device:TPU:8, one launch (start us, length us, event | category | flops | bytes accessed | tf_op | source)
XLA Modules:
  0.0 153.3 jit_solution(6105590072741801460)
XLA Ops:
  0.6 2.1 %shard_map.171 = (bf16[4,32,640]{2,1,0:T(8,128)(2,1)}, bf16[4,32,640]{2,1,0:T(8,128)(2,1)}, bf16[4,32,640]{2,1,0:T(8,128)(2,1)}, bf16[4,32,640]{2,1,0:T(8,128)(2,1)}) custom-call(bf16[1,32,2560]{2,1,0:T(8,128)(2,1)} %q_ref.1, bf16[1,32,2560]{2,1,0:T(8,128)(2,1)} %k_ref.1, bf16[1,32,2560]{2,1,0:T(8,128)(2,1)} %v_ref.1, bf16[1,32,2560]{2,1,0:T(8,128)(2,1)} %g_ref.1), custom_call_target="tpu_custom_call" | custom-call | tf_op jit(solution)/shard_map/pallas_call | solution.py:292
  2.7 1.6 %collective-permute-start = (bf16[4,32,640]{2,1,0:T(8,128)(2,1)}, bf16[4,32,640]{2,1,0:T(8,128)(2,1)S(1)}, u32[]{:S(2)}, u32[]{:S(2)}) collective-permute-start(bf16[4,32,640]{2,1,0:T(8,128)(2,1)} %get-tuple-element.25), channel_id=1, source_target_pairs={{0,4},{4,0},{8,12},{12,8},{1,5},{5,1},{9,13},{13,9},{2,6},{6,2},{1... | collective-permute-start | bytes 491528 | tf_op jit(solution)/shard_map/ppermute | solution.py:288
  4.3 2.7 %collective-permute-start.1 = (bf16[4,32,640]{2,1,0:T(8,128)(2,1)}, bf16[4,32,640]{2,1,0:T(8,128)(2,1)S(1)}, u32[]{:S(2)}, u32[]{:S(2)}) collective-permute-start(bf16[4,32,640]{2,1,0:T(8,128)(2,1)} %get-tuple-element.26), channel_id=1, source_target_pairs={{0,8},{4,12},{8,0},{12,4},{1,9},{5,13},{9,1},{13,5},{2,10},{6,14},... | collective-permute-start | bytes 491528 | tf_op jit(solution)/shard_map/ppermute | solution.py:288
  7.5 1.0 copy-done
  8.5 1.0 copy-done.1
  9.4 0.9 copy-done.2
  10.3 0.9 copy-done.3
  11.3 1.6 %shard_map.172.text_ref = bf16[16,4,128,128]{3,2,1,0:T(8,128)(2,1)} custom-call(bf16[1,256,640]{2,1,0:T(8,128)(2,1)S(1)} %copy-done, bf16[1,128,640]{2,1,0:T(8,128)(2,1)S(1)} %copy-done.2, bf16[1,128,640]{2,1,0:T(8,128)(2,1)S(1)} %copy-done.3, bf16[1,256,640]{2,1,0:T(8,128)(2,1)S(1)} %copy-done.1), custom_call_target="tpu_custom_call" | custom-call | tf_op jit(solution)/shard_map/pallas_call | solution.py:301
  12.9 1.8 %collective-permute-done.1.s2_ref = bf16[4,32,640]{2,1,0:T(8,128)(2,1)S(1)} collective-permute-done((bf16[4,32,640]{2,1,0:T(8,128)(2,1)}, bf16[4,32,640]{2,1,0:T(8,128)(2,1)S(1)}, u32[]{:S(2)}, u32[]{:S(2)}) %collective-permute-start.1) | collective-permute-done | bytes 163872 | tf_op jit(solution)/shard_map/ppermute | solution.py:288
  14.7 2.4 %collective-permute-done.2.s3_ref = bf16[4,32,640]{2,1,0:T(8,128)(2,1)S(1)} collective-permute-done((bf16[4,32,640]{2,1,0:T(8,128)(2,1)}, bf16[4,32,640]{2,1,0:T(8,128)(2,1)S(1)}, u32[]{:S(2)}, u32[]{:S(2)}) %collective-permute-start.2) | collective-permute-done | bytes 163872 | tf_op jit(solution)/shard_map/ppermute | solution.py:288
  17.2 1.0 shard_map.173
  18.2 8.7 %all-to-all-start = ((bf16[16,4,128,128]{3,2,1,0:T(8,128)(2,1)}), bf16[16,4,128,128]{3,2,1,0:T(8,128)(2,1)S(1)}, u32[]{:S(2)}, u32[]{:S(2)}) async-start(bf16[16,4,128,128]{3,2,1,0:T(8,128)(2,1)} %shard_map.173), calls=%async_computation | async-start | bytes 4194304 | tf_op jit(solution)/shard_map/all_to_all | solution.py:313
  34.3 0.8 add_reduce_fusion
  35.7 3.3 %subtract_multiply_fusion = (f32[1,2048]{1,0:T(1,128)S(1)}, f32[1,2048]{1,0:T(1,128)S(1)}) fusion(f32[]{:T(128)} %bitcast.6, s32[]{:T(128)S(6)} %add.174, s32[]{:T(128)S(6)} %add.172, s32[]{:T(128)} %bitcast.1, s32[]{:T(128)} %bitcast.14, s32[]{:T(128)} %bitcast.13, s32[]{:T(128)} %bitcast.12, s32[]{:T(128)} %bitcast.11, f32[]{:T(128)} %bitcast.5), kind=kLoop, calls=%fused_computation.18 | loop fusion | flops 55296 | bytes 16420 | tf_op jit(solution)/shard_map/mul | solution.py:272
  39.1 36.9 %all-to-all-done.in_ref = bf16[16,4,128,128]{3,2,1,0:T(8,128)(2,1)S(1)} async-done(((bf16[16,4,128,128]{3,2,1,0:T(8,128)(2,1)}), bf16[16,4,128,128]{3,2,1,0:T(8,128)(2,1)S(1)}, u32[]{:S(2)}, u32[]{:S(2)}) %all-to-all-start) | async-done | bytes 2097184 | tf_op jit(solution)/shard_map/all_to_all | solution.py:313
  76.1 15.1 %shard_map.174 = bf16[16,400,128]{2,1,0:T(8,128)(2,1)S(1)} custom-call(s32[2,8]{1,0:T(2,128)S(1)} %pad_add_fusion.win_ref, f32[5,4]{1,0:T(8,128)S(1)} %stack.52.page_ref, f32[8,2048]{1,0:T(8,128)S(1)} %maximum_maximum_fusion.qi_ref, bf16[16,4,128,128]{3,2,1,0:T(8,128)(2,1)S(1)} %all-to-all-done.in_ref), custom_call_target="tpu_custom_call" | custom-call | tf_op jit(solution)/shard_map/pallas_call | solution.py:314
  91.2 47.0 %all_to_all.10.in_ref = bf16[16,400,128]{2,1,0:T(8,128)(2,1)S(1)} all-to-all(bf16[16,400,128]{2,1,0:T(8,128)(2,1)S(1)} %shard_map.174), channel_id=1, replica_groups=mesh['seq'=16,'head'=4,'dp'=4] {'seq'}, dimensions={0} | all-to-all | bytes 3276800 | tf_op jit(solution)/shard_map/all_to_all | solution.py:332
  138.1 1.0 shard_map.175
  139.1 1.9 %collective-permute-start.5 = (bf16[3,32,640]{2,1,0:T(8,128)(2,1)S(1)}, bf16[3,32,640]{2,1,0:T(8,128)(2,1)S(1)}, u32[]{:S(2)}, u32[]{:S(2)}) collective-permute-start(bf16[3,32,640]{2,1,0:T(8,128)(2,1)S(1)} %get-tuple-element.32), channel_id=1, source_target_pairs={{0,8},{4,12},{8,0},{12,4},{1,9},{5,13},{9,1},{13,5},{2,10},{6,14},... | collective-permute-start | bytes 368648 | tf_op jit(solution)/shard_map/ppermute | solution.py:288
  141.1 2.8 %collective-permute-start.6 = (bf16[3,32,640]{2,1,0:T(8,128)(2,1)S(1)}, bf16[3,32,640]{2,1,0:T(8,128)(2,1)S(1)}, u32[]{:S(2)}, u32[]{:S(2)}) collective-permute-start(bf16[3,32,640]{2,1,0:T(8,128)(2,1)S(1)} %get-tuple-element.33), channel_id=1, source_target_pairs={{0,12},{4,8},{8,4},{12,0},{1,13},{5,9},{9,5},{13,1},{2,14},{6,10},... | collective-permute-start | bytes 368648 | tf_op jit(solution)/shard_map/ppermute | solution.py:288
  143.8 3.6 %collective-permute-done.3 = f32[2,8,128]{2,1,0:T(8,128)S(1)} collective-permute-done((f32[2,8,128]{2,1,0:T(8,128)S(1)}, f32[2,8,128]{2,1,0:T(8,128)S(1)}, u32[]{:S(2)}, u32[]{:S(2)}) %collective-permute-start.3) | collective-permute-done | bytes 8224 | tf_op jit(solution)/shard_map/ppermute | solution.py:344
  147.5 1.6 %collective-permute-start.7 = (f32[2,8,128]{2,1,0:T(8,128)S(1)}, f32[2,8,128]{2,1,0:T(8,128)S(1)}, u32[]{:S(2)}, u32[]{:S(2)}) collective-permute-start(f32[2,8,128]{2,1,0:T(8,128)S(1)} %add.184), channel_id=1, source_target_pairs={{0,2},{1,3},{2,0},{3,1},{4,6},{5,7},{6,4},{7,5},{8,10},{9,11},{10,... | collective-permute-start | bytes 24584 | tf_op jit(solution)/shard_map/ppermute | solution.py:347
  149.6 0.8 shard_map.176
  150.4 2.2 %collective-permute-done.7 = f32[2,8,128]{2,1,0:T(8,128)S(1)} collective-permute-done((f32[2,8,128]{2,1,0:T(8,128)S(1)}, f32[2,8,128]{2,1,0:T(8,128)S(1)}, u32[]{:S(2)}, u32[]{:S(2)}) %collective-permute-start.7) | collective-permute-done | bytes 8224 | tf_op jit(solution)/shard_map/ppermute | solution.py:347
  (42 shorter events, 5.1 us)
Async XLA Ops:
  2.7 10.2 %collective-permute-start = (bf16[4,32,640]{2,1,0:T(8,128)(2,1)}, bf16[4,32,640]{2,1,0:T(8,128)(2,1)S(1)}, u32[]{:S(2)}, u32[]{:S(2)}) collective-permute-start(bf16[4,32,640]{2,1,0:T(8,128)(2,1)} %get-tuple-element.25), channel_id=1, source_target_pairs={{0,4},{4,0},{8,12},{12,8},{1,5},{5,1},{9,13},{13,9},{2,6},{6,2},{1... | collective-permute-start | bytes 491528 | tf_op jit(solution)/shard_map/ppermute | solution.py:288
  4.3 10.5 %collective-permute-start.1 = (bf16[4,32,640]{2,1,0:T(8,128)(2,1)}, bf16[4,32,640]{2,1,0:T(8,128)(2,1)S(1)}, u32[]{:S(2)}, u32[]{:S(2)}) collective-permute-start(bf16[4,32,640]{2,1,0:T(8,128)(2,1)} %get-tuple-element.26), channel_id=1, source_target_pairs={{0,8},{4,12},{8,0},{12,4},{1,9},{5,13},{9,1},{13,5},{2,10},{6,14},... | collective-permute-start | bytes 491528 | tf_op jit(solution)/shard_map/ppermute | solution.py:288
  7.0 10.2 %collective-permute-start.2 = (bf16[4,32,640]{2,1,0:T(8,128)(2,1)}, bf16[4,32,640]{2,1,0:T(8,128)(2,1)S(1)}, u32[]{:S(2)}, u32[]{:S(2)}) collective-permute-start(bf16[4,32,640]{2,1,0:T(8,128)(2,1)} %get-tuple-element.27), channel_id=1, source_target_pairs={{0,12},{4,8},{8,4},{12,0},{1,13},{5,9},{9,5},{13,1},{2,14},{6,10},... | collective-permute-start | bytes 491528 | tf_op jit(solution)/shard_map/ppermute | solution.py:288
  7.5 1.0 copy-start
  8.5 1.0 copy-start.1
  9.4 0.9 copy-start.2
  10.3 0.9 copy-start.3
  11.3 5.9 %copy-start.4 = (bf16[4,32,640]{2,1,0:T(8,128)(2,1)S(1)}, bf16[4,32,640]{2,1,0:T(8,128)(2,1)}, u32[]{:S(2)}) copy-start(bf16[4,32,640]{2,1,0:T(8,128)(2,1)} %get-tuple-element.24.s0_ref) | copy-start | bytes 491524
  18.1 8.8 %copy-start.7 = (f32[2,5]{1,0:T(2,128)S(1)}, f32[2,5]{1,0:T(2,128)}, u32[]{:S(2)}) copy-start(f32[2,5]{1,0:T(2,128)} %param.20) | copy-start | bytes 124
  18.1 10.7 %copy-start.6 = (s32[1,4]{1,0:T(1,128)S(1)}, s32[1,4]{1,0:T(1,128)}, u32[]{:S(2)}) copy-start(s32[1,4]{1,0:T(1,128)} %param.22) | copy-start | bytes 52
  18.2 10.7 %copy-start.5 = (s32[1,4]{1,0:T(1,128)S(1)}, s32[1,4]{1,0:T(1,128)}, u32[]{:S(2)}) copy-start(s32[1,4]{1,0:T(1,128)} %param.21) | copy-start | bytes 52
  18.2 14.5 %copy-start.8 = (s32[1,4096]{1,0:T(1,128)S(1)}, s32[1,4096]{1,0:T(1,128)}, u32[]{:S(2)}) copy-start(s32[1,4096]{1,0:T(1,128)} %param.23) | copy-start | bytes 49156
  18.2 57.9 %all-to-all-start = ((bf16[16,4,128,128]{3,2,1,0:T(8,128)(2,1)}), bf16[16,4,128,128]{3,2,1,0:T(8,128)(2,1)S(1)}, u32[]{:S(2)}, u32[]{:S(2)}) async-start(bf16[16,4,128,128]{3,2,1,0:T(8,128)(2,1)} %shard_map.173), calls=%async_computation | async-start | bytes 4194304 | tf_op jit(solution)/shard_map/all_to_all | solution.py:313
  139.1 8.4 %collective-permute-start.4 = (bf16[3,32,640]{2,1,0:T(8,128)(2,1)S(1)}, bf16[3,32,640]{2,1,0:T(8,128)(2,1)S(1)}, u32[]{:S(2)}, u32[]{:S(2)}) collective-permute-start(bf16[3,32,640]{2,1,0:T(8,128)(2,1)S(1)} %get-tuple-element.30), channel_id=1, source_target_pairs={{0,4},{4,0},{8,12},{12,8},{1,5},{5,1},{9,13},{13,9},{2,6},{6,2},{1... | collective-permute-start | bytes 368648 | tf_op jit(solution)/shard_map/ppermute | solution.py:288
  139.1 10.0 %collective-permute-start.5 = (bf16[3,32,640]{2,1,0:T(8,128)(2,1)S(1)}, bf16[3,32,640]{2,1,0:T(8,128)(2,1)S(1)}, u32[]{:S(2)}, u32[]{:S(2)}) collective-permute-start(bf16[3,32,640]{2,1,0:T(8,128)(2,1)S(1)} %get-tuple-element.32), channel_id=1, source_target_pairs={{0,8},{4,12},{8,0},{12,4},{1,9},{5,13},{9,1},{13,5},{2,10},{6,14},... | collective-permute-start | bytes 368648 | tf_op jit(solution)/shard_map/ppermute | solution.py:288
  141.1 8.5 %collective-permute-start.6 = (bf16[3,32,640]{2,1,0:T(8,128)(2,1)S(1)}, bf16[3,32,640]{2,1,0:T(8,128)(2,1)S(1)}, u32[]{:S(2)}, u32[]{:S(2)}) collective-permute-start(bf16[3,32,640]{2,1,0:T(8,128)(2,1)S(1)} %get-tuple-element.33), channel_id=1, source_target_pairs={{0,12},{4,8},{8,4},{12,0},{1,13},{5,9},{9,5},{13,1},{2,14},{6,10},... | collective-permute-start | bytes 368648 | tf_op jit(solution)/shard_map/ppermute | solution.py:288
  143.8 3.7 %collective-permute-start.3 = (f32[2,8,128]{2,1,0:T(8,128)S(1)}, f32[2,8,128]{2,1,0:T(8,128)S(1)}, u32[]{:S(2)}, u32[]{:S(2)}) collective-permute-start(f32[2,8,128]{2,1,0:T(8,128)S(1)} %get-tuple-element.29), channel_id=1, source_target_pairs={{0,1},{1,0},{2,3},{3,2},{4,5},{5,4},{6,7},{7,6},{8,9},{9,8},{10,11... | collective-permute-start | bytes 24584 | tf_op jit(solution)/shard_map/ppermute | solution.py:344
  147.5 5.2 %collective-permute-start.7 = (f32[2,8,128]{2,1,0:T(8,128)S(1)}, f32[2,8,128]{2,1,0:T(8,128)S(1)}, u32[]{:S(2)}, u32[]{:S(2)}) collective-permute-start(f32[2,8,128]{2,1,0:T(8,128)S(1)} %add.184), channel_id=1, source_target_pairs={{0,2},{1,3},{2,0},{3,1},{4,6},{5,7},{6,4},{7,5},{8,10},{9,11},{10,... | collective-permute-start | bytes 24584 | tf_op jit(solution)/shard_map/ppermute | solution.py:347

commit v7 on v6

--- a/solution.py
+++ b/solution.py
@@ -71,37 +71,32 @@
     copy.wait()
 
 
-def unpack_tasks(
-    in_ref, tq_ref, mk_ref, mv_ref, slope_ref, s0_ref, s1_ref, s2_ref, s3_ref
-):
-    me = lax.axis_index("head")
+def unpack_tasks(in_ref, tq_ref, mk_ref, mv_ref, slope_ref, self_ref):
     k, v = (slice(i * BLK, (i + 1) * BLK) for i in (1, 2))
     slope_ref[...] = jnp.zeros_like(slope_ref)
     for h in range(HEADS):
         cols = slice(h * HS, (h + 1) * HS)
+        for a in range(3):
+            for x in range(4):
+                at = a * BLK + x * 32
+                self_ref[x, a, :, cols] = in_ref[TEXT_TASKS + h, at : at + 32]
         for j in range(2):
             tq_ref[0, j * BLK : (j + 1) * BLK, cols] = in_ref[2 * h + j, :BLK]
         mk = in_ref[2 * h, k].astype(F32) + in_ref[2 * h + 1, k].astype(F32)
         mv = in_ref[2 * h, v].astype(F32) + in_ref[2 * h + 1, v].astype(F32)
         mk_ref[0, :, cols] = mk.astype(BF)
         mv_ref[0, :, cols] = mv.astype(BF)
-        for gap, ref in enumerate((s0_ref, s1_ref, s2_ref, s3_ref)):
-            for a in range(3):
-                at = pl.ds(pl.multiple_of(a * BLK + (me ^ gap) * 32, 32), 32)
-                ref[a, :, cols] = in_ref[TEXT_TASKS + h, at]
         pieces = in_ref[TEXT_TASKS + h, 3 * BLK :].astype(F32)
         for i in range(2):
             whole = pieces[3 * i : 3 * i + 1] + pieces[3 * i + 1 : 3 * i + 2]
             slope_ref[i, h : h + 1] = whole + pieces[3 * i + 2 : 3 * i + 3]
 
 
-def unpack_self(s0_ref, s1_ref, s2_ref, s3_ref, q_ref, k_ref, v_ref):
-    me = lax.axis_index("head")
+def unpack_self(in_ref, q_ref, k_ref, v_ref):
     width = HEADS * HS
-    for gap, part in enumerate((s0_ref, s1_ref, s2_ref, s3_ref)):
-        at = pl.ds(pl.multiple_of((me ^ gap) * width, HS), width)
+    for x in range(4):
         for a, ref in enumerate((q_ref, k_ref, v_ref)):
-            ref[0, :, at] = part[a]
+            ref[0, :, x * width : (x + 1) * width] = in_ref[x, a]
 
 
 def attend(
@@ -330,25 +325,24 @@
     )(window, pages, q_info, held)
 
     back = lax.all_to_all(back, "seq", split_axis=0, concat_axis=0, tiled=True)
-    part = sds((3, 32, HEADS * HS), BF)
-    text_dq, mem_dk, mem_dv, slope_sum, *self_out = vmem_call(
+    text_dq, mem_dk, mem_dv, slope_sum, self_out = vmem_call(
         unpack_tasks,
         (
             sds(text_queries.shape, BF),
             sds(memory_keys.shape, BF),
             sds(memory_values.shape, BF),
             sds((2, 8, BLK), F32),
-            *(part,) * 4,
+            sds((4, 3, 32, HEADS * HS), BF),
         ),
     )(back)
-    slope_sum = slope_sum + lax.ppermute(slope_sum, "dp", [(i, i ^ 1) for i in range(4)])
-    self_out = swap_heads(self_out)
-    slope_sum, self_out[1] = lax.optimization_barrier((slope_sum, self_out[1]))
-    slope_sum = slope_sum + lax.ppermute(slope_sum, "dp", [(i, i ^ 2) for i in range(4)])
+    self_out = lax.all_to_all(self_out, "head", split_axis=0, concat_axis=0, tiled=True)
+    for gap in (1, 2):
+        swap = [(i, i ^ gap) for i in range(4)]
+        slope_sum = slope_sum + lax.ppermute(slope_sum, "dp", swap)
     slope_sum = jnp.sum(slope_sum[:, :HEADS], axis=2)
     slope_grad = slope_sum / (slopes * (LOG2E * -patches))
     shape = sds(self_queries.shape, BF)
-    self_dq, self_dk, self_dv = vmem_call(unpack_self, (shape, shape, shape))(*self_out)
+    self_dq, self_dk, self_dv = vmem_call(unpack_self, (shape, shape, shape))(self_out)
     return self_dq, self_dk, self_dv, slope_grad, text_dq, mem_dk, mem_dv
 
 

time: 154 us -> 155 us (level)
    ppermute x6 -> x3, starting transfers between devices: 9.48 us -> 4.79 us  [swap_heads(): out[gap] = lax.ppermute(parts[gap], 'head', swap)]
    all_to_all x0 -> x1, starting transfers between devices: none -> 3.47 us  [local(): lax.all_to_all(self_out, 'head', split_axis=0, concat_axis=0, tiled=True)]
    ppermute x2, starting transfers between devices: 1.62 us -> 4.24 us  [local(): slope_sum = slope_sum + lax.ppermute(slope_sum, 'dp', swap)]
    ppermute x6 -> x3, waiting for transfers between devices: 4.73 us -> 4.25 us  [swap_heads(): out[gap] = lax.ppermute(parts[gap], 'head', swap)]
  transfers between devices with their start and end apart: 9 -> 7, of which waited for: 6 -> 6; matrix products, arithmetic and copies ran while one was open for 5% -> 5% of each run, Pallas kernels for 2% -> 1%
where the time goes in v7:
time: 155 us; the launch traced here: 153 us
  blocking collectives  47.4 us (31%)
  waiting for transfers between devices  46.1 us (30%)
  Pallas kernels  21.2 us (14%)
  starting transfers between devices  21.2 us (14%)
  other arithmetic  6.4 us (4%)
  local copies, waits for them, and re-layouts  5.62 us (4%)
  between operations  5.38 us (3%)
    all_to_all x1, blocking collectives, local(): back = lax.all_to_all(back, 'seq', split_axis=0, concat_axis=0, tiled=True)  47.4 us
    all_to_all x1, waiting for transfers between devices, local(): held = lax.all_to_all(sent, 'seq', split_axis=0, concat_axis=0, tiled=True)  36.9 us
    pallas_call x1, Pallas kernels, local(): vmem_call(attend, sds((TASKS, 3 * BLK + 16, HS), BF), in_specs=[pl.BlockS...  14.6 us
    all_to_all x1, starting transfers between devices, local(): held = lax.all_to_all(sent, 'seq', split_axis=0, concat_axis=0, tiled=True)  8.72 us
    ppermute x3, starting transfers between devices, swap_heads(): out[gap] = lax.ppermute(parts[gap], 'head', swap)  4.79 us
    ppermute x2, waiting for transfers between devices, local(): slope_sum = slope_sum + lax.ppermute(slope_sum, 'dp', swap)  4.65 us
    ppermute x3, waiting for transfers between devices, swap_heads(): out[gap] = lax.ppermute(parts[gap], 'head', swap)  4.25 us
    ppermute x2, starting transfers between devices, local(): slope_sum = slope_sum + lax.ppermute(slope_sum, 'dp', swap)  4.24 us
  transfers between devices with their start and end apart: 7, of which 6 were waited for; matrix products, arithmetic and copies ran while one was open for 5% of the time, Pallas kernels for 1%

profile of v7, /device:TPU:8, one launch (start us, length us, event | category | flops | bytes accessed | tf_op | source)
XLA Modules:
  0.0 153.4 jit_solution(12232551971237029077)
XLA Ops:
  0.6 2.1 %shard_map.171 = (bf16[4,32,640]{2,1,0:T(8,128)(2,1)}, bf16[4,32,640]{2,1,0:T(8,128)(2,1)}, bf16[4,32,640]{2,1,0:T(8,128)(2,1)}, bf16[4,32,640]{2,1,0:T(8,128)(2,1)}) custom-call(bf16[1,32,2560]{2,1,0:T(8,128)(2,1)} %q_ref.1, bf16[1,32,2560]{2,1,0:T(8,128)(2,1)} %k_ref.1, bf16[1,32,2560]{2,1,0:T(8,128)(2,1)} %v_ref.1, bf16[1,32,2560]{2,1,0:T(8,128)(2,1)} %g_ref.1), custom_call_target="tpu_custom_call" | custom-call | tf_op jit(solution)/shard_map/pallas_call | solution.py:287
  2.7 1.6 %collective-permute-start = (bf16[4,32,640]{2,1,0:T(8,128)(2,1)}, bf16[4,32,640]{2,1,0:T(8,128)(2,1)S(1)}, u32[]{:S(2)}, u32[]{:S(2)}) collective-permute-start(bf16[4,32,640]{2,1,0:T(8,128)(2,1)} %get-tuple-element.20), channel_id=1, source_target_pairs={{0,4},{4,0},{8,12},{12,8},{1,5},{5,1},{9,13},{13,9},{2,6},{6,2},{1... | collective-permute-start | bytes 491528 | tf_op jit(solution)/shard_map/ppermute | solution.py:283
  4.3 2.7 %collective-permute-start.1 = (bf16[4,32,640]{2,1,0:T(8,128)(2,1)}, bf16[4,32,640]{2,1,0:T(8,128)(2,1)S(1)}, u32[]{:S(2)}, u32[]{:S(2)}) collective-permute-start(bf16[4,32,640]{2,1,0:T(8,128)(2,1)} %get-tuple-element.21), channel_id=1, source_target_pairs={{0,8},{4,12},{8,0},{12,4},{1,9},{5,13},{9,1},{13,5},{2,10},{6,14},... | collective-permute-start | bytes 491528 | tf_op jit(solution)/shard_map/ppermute | solution.py:283
  7.5 1.0 copy-done
  8.5 1.0 copy-done.1
  9.4 0.9 copy-done.2
  10.3 0.9 copy-done.3
  11.3 1.6 %shard_map.172.text_ref = bf16[16,4,128,128]{3,2,1,0:T(8,128)(2,1)} custom-call(bf16[1,256,640]{2,1,0:T(8,128)(2,1)S(1)} %copy-done, bf16[1,128,640]{2,1,0:T(8,128)(2,1)S(1)} %copy-done.2, bf16[1,128,640]{2,1,0:T(8,128)(2,1)S(1)} %copy-done.3, bf16[1,256,640]{2,1,0:T(8,128)(2,1)S(1)} %copy-done.1), custom_call_target="tpu_custom_call" | custom-call | tf_op jit(solution)/shard_map/pallas_call | solution.py:296
  12.9 1.8 %collective-permute-done.1.s2_ref = bf16[4,32,640]{2,1,0:T(8,128)(2,1)S(1)} collective-permute-done((bf16[4,32,640]{2,1,0:T(8,128)(2,1)}, bf16[4,32,640]{2,1,0:T(8,128)(2,1)S(1)}, u32[]{:S(2)}, u32[]{:S(2)}) %collective-permute-start.1) | collective-permute-done | bytes 163872 | tf_op jit(solution)/shard_map/ppermute | solution.py:283
  14.7 2.4 %collective-permute-done.2.s3_ref = bf16[4,32,640]{2,1,0:T(8,128)(2,1)S(1)} collective-permute-done((bf16[4,32,640]{2,1,0:T(8,128)(2,1)}, bf16[4,32,640]{2,1,0:T(8,128)(2,1)S(1)}, u32[]{:S(2)}, u32[]{:S(2)}) %collective-permute-start.2) | collective-permute-done | bytes 163872 | tf_op jit(solution)/shard_map/ppermute | solution.py:283
  17.2 1.0 shard_map.173
  18.2 8.7 %all-to-all-start = ((bf16[16,4,128,128]{3,2,1,0:T(8,128)(2,1)}), bf16[16,4,128,128]{3,2,1,0:T(8,128)(2,1)S(1)}, u32[]{:S(2)}, u32[]{:S(2)}) async-start(bf16[16,4,128,128]{3,2,1,0:T(8,128)(2,1)} %shard_map.173), calls=%async_computation | async-start | bytes 4194304 | tf_op jit(solution)/shard_map/all_to_all | solution.py:308
  34.3 0.8 add_reduce_fusion
  35.7 3.3 %subtract_multiply_fusion = (f32[1,2048]{1,0:T(1,128)S(1)}, f32[1,2048]{1,0:T(1,128)S(1)}) fusion(f32[]{:T(128)} %bitcast.6, s32[]{:T(128)S(6)} %add.174, s32[]{:T(128)S(6)} %add.172, s32[]{:T(128)} %bitcast.1, s32[]{:T(128)} %bitcast.14, s32[]{:T(128)} %bitcast.13, s32[]{:T(128)} %bitcast.12, s32[]{:T(128)} %bitcast.11, f32[]{:T(128)} %bitcast.5), kind=kLoop, calls=%fused_computation.18 | loop fusion | flops 55296 | bytes 16420 | tf_op jit(solution)/shard_map/mul | solution.py:267
  39.1 36.9 %all-to-all-done.in_ref = bf16[16,4,128,128]{3,2,1,0:T(8,128)(2,1)S(1)} async-done(((bf16[16,4,128,128]{3,2,1,0:T(8,128)(2,1)}), bf16[16,4,128,128]{3,2,1,0:T(8,128)(2,1)S(1)}, u32[]{:S(2)}, u32[]{:S(2)}) %all-to-all-start) | async-done | bytes 2097184 | tf_op jit(solution)/shard_map/all_to_all | solution.py:308
  76.1 14.6 %shard_map.174 = bf16[16,400,128]{2,1,0:T(8,128)(2,1)S(1)} custom-call(s32[2,8]{1,0:T(2,128)S(1)} %pad_add_fusion.win_ref, f32[5,4]{1,0:T(8,128)S(1)} %stack.52.page_ref, f32[8,2048]{1,0:T(8,128)S(1)} %maximum_maximum_fusion.qi_ref, bf16[16,4,128,128]{3,2,1,0:T(8,128)(2,1)S(1)} %all-to-all-done.in_ref), custom_call_target="tpu_custom_call" | custom-call | tf_op jit(solution)/shard_map/pallas_call | solution.py:309
  90.7 47.4 %all_to_all.15.in_ref = bf16[16,400,128]{2,1,0:T(8,128)(2,1)S(1)} all-to-all(bf16[16,400,128]{2,1,0:T(8,128)(2,1)S(1)} %shard_map.174), channel_id=1, replica_groups=mesh['seq'=16,'head'=4,'dp'=4] {'seq'}, dimensions={0} | all-to-all | bytes 3276800 | tf_op jit(solution)/shard_map/all_to_all | solution.py:327
  138.1 1.2 shard_map.175
  139.2 3.5 %all-to-all-start.2 = ((bf16[4,3,32,640]{3,2,1,0:T(8,128)(2,1)}), bf16[4,3,32,640]{3,2,1,0:T(8,128)(2,1)S(1)}, u32[]{:S(2)}, u32[]{:S(2)}) async-start(bf16[4,3,32,640]{3,2,1,0:T(8,128)(2,1)} %get-tuple-element.23), calls=%async_computation.2 | async-start | bytes 983040 | tf_op jit(solution)/shard_map/all_to_all | solution.py:338
  142.7 1.3 collective-permute-start.3
  144.0 2.4 %collective-permute-done.3 = f32[2,8,128]{2,1,0:T(8,128)S(1)} collective-permute-done((f32[2,8,128]{2,1,0:T(8,128)S(1)}, f32[2,8,128]{2,1,0:T(8,128)S(1)}, u32[]{:S(2)}, u32[]{:S(2)}) %collective-permute-start.3) | collective-permute-done | bytes 8224 | tf_op jit(solution)/shard_map/ppermute | solution.py:341
  146.5 2.9 %collective-permute-start.4 = (f32[2,8,128]{2,1,0:T(8,128)S(1)}, f32[2,8,128]{2,1,0:T(8,128)S(1)}, u32[]{:S(2)}, u32[]{:S(2)}) collective-permute-start(f32[2,8,128]{2,1,0:T(8,128)S(1)} %add.184), channel_id=1, source_target_pairs={{0,2},{1,3},{2,0},{3,1},{4,6},{5,7},{6,4},{7,5},{8,10},{9,11},{10,... | collective-permute-start | bytes 24584 | tf_op jit(solution)/shard_map/ppermute | solution.py:341
  149.4 2.2 %collective-permute-done.4 = f32[2,8,128]{2,1,0:T(8,128)S(1)} collective-permute-done((f32[2,8,128]{2,1,0:T(8,128)S(1)}, f32[2,8,128]{2,1,0:T(8,128)S(1)}, u32[]{:S(2)}, u32[]{:S(2)}) %collective-permute-start.4) | collective-permute-done | bytes 8224 | tf_op jit(solution)/shard_map/ppermute | solution.py:341
  152.6 0.8 shard_map.176
  (38 shorter events, 4.9 us)
Async XLA Ops:
  2.7 10.2 %collective-permute-start = (bf16[4,32,640]{2,1,0:T(8,128)(2,1)}, bf16[4,32,640]{2,1,0:T(8,128)(2,1)S(1)}, u32[]{:S(2)}, u32[]{:S(2)}) collective-permute-start(bf16[4,32,640]{2,1,0:T(8,128)(2,1)} %get-tuple-element.20), channel_id=1, source_target_pairs={{0,4},{4,0},{8,12},{12,8},{1,5},{5,1},{9,13},{13,9},{2,6},{6,2},{1... | collective-permute-start | bytes 491528 | tf_op jit(solution)/shard_map/ppermute | solution.py:283
  4.3 10.5 %collective-permute-start.1 = (bf16[4,32,640]{2,1,0:T(8,128)(2,1)}, bf16[4,32,640]{2,1,0:T(8,128)(2,1)S(1)}, u32[]{:S(2)}, u32[]{:S(2)}) collective-permute-start(bf16[4,32,640]{2,1,0:T(8,128)(2,1)} %get-tuple-element.21), channel_id=1, source_target_pairs={{0,8},{4,12},{8,0},{12,4},{1,9},{5,13},{9,1},{13,5},{2,10},{6,14},... | collective-permute-start | bytes 491528 | tf_op jit(solution)/shard_map/ppermute | solution.py:283
  7.0 10.2 %collective-permute-start.2 = (bf16[4,32,640]{2,1,0:T(8,128)(2,1)}, bf16[4,32,640]{2,1,0:T(8,128)(2,1)S(1)}, u32[]{:S(2)}, u32[]{:S(2)}) collective-permute-start(bf16[4,32,640]{2,1,0:T(8,128)(2,1)} %get-tuple-element.22), channel_id=1, source_target_pairs={{0,12},{4,8},{8,4},{12,0},{1,13},{5,9},{9,5},{13,1},{2,14},{6,10},... | collective-permute-start | bytes 491528 | tf_op jit(solution)/shard_map/ppermute | solution.py:283
  7.5 1.0 copy-start
  8.5 1.0 copy-start.1
  9.4 0.9 copy-start.2
  10.3 0.9 copy-start.3
  11.3 5.9 %copy-start.4 = (bf16[4,32,640]{2,1,0:T(8,128)(2,1)S(1)}, bf16[4,32,640]{2,1,0:T(8,128)(2,1)}, u32[]{:S(2)}) copy-start(bf16[4,32,640]{2,1,0:T(8,128)(2,1)} %get-tuple-element.19.s0_ref) | copy-start | bytes 491524
  18.1 8.8 %copy-start.7 = (f32[2,5]{1,0:T(2,128)S(1)}, f32[2,5]{1,0:T(2,128)}, u32[]{:S(2)}) copy-start(f32[2,5]{1,0:T(2,128)} %param.20) | copy-start | bytes 124
  18.1 10.7 %copy-start.6 = (s32[1,4]{1,0:T(1,128)S(1)}, s32[1,4]{1,0:T(1,128)}, u32[]{:S(2)}) copy-start(s32[1,4]{1,0:T(1,128)} %param.22) | copy-start | bytes 52
  18.2 10.7 %copy-start.5 = (s32[1,4]{1,0:T(1,128)S(1)}, s32[1,4]{1,0:T(1,128)}, u32[]{:S(2)}) copy-start(s32[1,4]{1,0:T(1,128)} %param.21) | copy-start | bytes 52
  18.2 14.5 %copy-start.8 = (s32[1,4096]{1,0:T(1,128)S(1)}, s32[1,4096]{1,0:T(1,128)}, u32[]{:S(2)}) copy-start(s32[1,4096]{1,0:T(1,128)} %param.23) | copy-start | bytes 49156
  18.2 57.9 %all-to-all-start = ((bf16[16,4,128,128]{3,2,1,0:T(8,128)(2,1)}), bf16[16,4,128,128]{3,2,1,0:T(8,128)(2,1)S(1)}, u32[]{:S(2)}, u32[]{:S(2)}) async-start(bf16[16,4,128,128]{3,2,1,0:T(8,128)(2,1)} %shard_map.173), calls=%async_computation | async-start | bytes 4194304 | tf_op jit(solution)/shard_map/all_to_all | solution.py:308
  139.2 13.3 %all-to-all-start.2 = ((bf16[4,3,32,640]{3,2,1,0:T(8,128)(2,1)}), bf16[4,3,32,640]{3,2,1,0:T(8,128)(2,1)S(1)}, u32[]{:S(2)}, u32[]{:S(2)}) async-start(bf16[4,3,32,640]{3,2,1,0:T(8,128)(2,1)} %get-tuple-element.23), calls=%async_computation.2 | async-start | bytes 983040 | tf_op jit(solution)/shard_map/all_to_all | solution.py:338
  142.7 3.7 %collective-permute-start.3 = (f32[2,8,128]{2,1,0:T(8,128)S(1)}, f32[2,8,128]{2,1,0:T(8,128)S(1)}, u32[]{:S(2)}, u32[]{:S(2)}) collective-permute-start(f32[2,8,128]{2,1,0:T(8,128)S(1)} %get-tuple-element.27), channel_id=1, source_target_pairs={{0,1},{1,0},{2,3},{3,2},{4,5},{5,4},{6,7},{7,6},{8,9},{9,8},{10,11... | collective-permute-start | bytes 24584 | tf_op jit(solution)/shard_map/ppermute | solution.py:341
  146.5 5.2 %collective-permute-start.4 = (f32[2,8,128]{2,1,0:T(8,128)S(1)}, f32[2,8,128]{2,1,0:T(8,128)S(1)}, u32[]{:S(2)}, u32[]{:S(2)}) collective-permute-start(f32[2,8,128]{2,1,0:T(8,128)S(1)} %add.184), channel_id=1, source_target_pairs={{0,2},{1,3},{2,0},{3,1},{4,6},{5,7},{6,4},{7,5},{8,10},{9,11},{10,... | collective-permute-start | bytes 24584 | tf_op jit(solution)/shard_map/ppermute | solution.py:341

commit v8 on v7

--- a/solution.py
+++ b/solution.py
@@ -71,9 +71,8 @@
     copy.wait()
 
 
-def unpack_tasks(in_ref, tq_ref, mk_ref, mv_ref, slope_ref, self_ref):
+def unpack_tasks(in_ref, tq_ref, mk_ref, mv_ref, self_ref):
     k, v = (slice(i * BLK, (i + 1) * BLK) for i in (1, 2))
-    slope_ref[...] = jnp.zeros_like(slope_ref)
     for h in range(HEADS):
         cols = slice(h * HS, (h + 1) * HS)
         for a in range(3):
@@ -86,10 +85,6 @@
         mv = in_ref[2 * h, v].astype(F32) + in_ref[2 * h + 1, v].astype(F32)
         mk_ref[0, :, cols] = mk.astype(BF)
         mv_ref[0, :, cols] = mv.astype(BF)
-        pieces = in_ref[TEXT_TASKS + h, 3 * BLK :].astype(F32)
-        for i in range(2):
-            whole = pieces[3 * i : 3 * i + 1] + pieces[3 * i + 1 : 3 * i + 2]
-            slope_ref[i, h : h + 1] = whole + pieces[3 * i + 2 : 3 * i + 3]
 
 
 def unpack_self(in_ref, q_ref, k_ref, v_ref):
@@ -100,7 +95,7 @@
 
 
 def attend(
-    win_ref, page_ref, qi_ref, in_ref, out_ref,
+    win_ref, page_ref, qi_ref, in_ref, out_ref, sum_ref,
     ka_ref, kb_ref, kp_ref, kt_buf, t_buf, d_buf, ds_buf, dk_acc, dv_acc, slope_ref,
 ):
     inv_root = HS ** (-0.5)
@@ -202,20 +197,15 @@
         return 0
 
     lax.fori_loop(0, blocks, step, 0)
-    line = lax.broadcasted_iota(jnp.int32, (16, BLK), 0)
-    pieces = jnp.zeros((16, BLK), F32)
-    for row in range(2):
-        rest = jnp.broadcast_to(slope_ref[row : row + 1], (16, BLK))
-        for i in range(3):
-            piece = rest.astype(BF).astype(F32)
-            rest = rest - piece
-            pieces = jnp.where(line == 3 * row + i, piece, pieces)
-    pieces = pieces.astype(BF)
+    line = lax.broadcasted_iota(jnp.int32, (BLK, BLK), 0)
+    slot = win_ref[2, 0]
+    sum_ref[...] = jnp.where(
+        line == slot, slope_ref[0:1], jnp.where(line == slot + 1, slope_ref[1:2], 0.0)
+    )
     for s in range(TASKS):
         here = slice(s * BLK, (s + 1) * BLK)
         out_ref[s, BLK : 2 * BLK] = (dk_acc[here] * inv_root).astype(BF)
         out_ref[s, 2 * BLK : 3 * BLK] = dv_acc[here].astype(BF)
-        out_ref[s, 3 * BLK :] = pieces
 
 
 def local(
@@ -274,7 +264,8 @@
         at = jnp.minimum(low, TASKS - SIZES[i])
         fits = high <= at + SIZES[i]
         first, kind = jnp.where(fits, at, first), jnp.where(fits, i, kind)
-    window = jnp.stack([first, kind])
+    slot = jnp.where((task >= TEXT_TASKS) & (task < TEXT_TASKS + HEADS), 2 * own, -2)
+    window = jnp.stack([first, kind, jnp.full_like(first, slot)])
 
     def swap_heads(parts):
         own, out = parts[0], [None] * 4
@@ -306,9 +297,9 @@
         input_output_aliases={4: 0},
     )(*by_head, sent)
     held = lax.all_to_all(sent, "seq", split_axis=0, concat_axis=0, tiled=True)
-    back = vmem_call(
+    back, slope_sum = vmem_call(
         attend,
-        sds((TASKS, 3 * BLK + 16, HS), BF),
+        (sds((TASKS, 3 * BLK, HS), BF), sds((BLK, BLK), F32)),
         in_specs=[pl.BlockSpec(memory_space=pltpu.SMEM)] * 2 + [vm] * 2,
         scratch_shapes=[
             pltpu.VMEM((patches, BLK), F32),
@@ -324,23 +315,20 @@
         ],
     )(window, pages, q_info, held)
 
+    slope_sum = lax.psum(slope_sum, ("seq", "dp"))
+    slope_sum = jnp.sum(slope_sum[: 2 * HEADS], axis=1).reshape(HEADS, 2).T
+    slope_grad = slope_sum / (slopes * (LOG2E * -patches))
     back = lax.all_to_all(back, "seq", split_axis=0, concat_axis=0, tiled=True)
-    text_dq, mem_dk, mem_dv, slope_sum, self_out = vmem_call(
+    text_dq, mem_dk, mem_dv, self_out = vmem_call(
         unpack_tasks,
         (
             sds(text_queries.shape, BF),
             sds(memory_keys.shape, BF),
             sds(memory_values.shape, BF),
-            sds((2, 8, BLK), F32),
             sds((4, 3, 32, HEADS * HS), BF),
         ),
     )(back)
     self_out = lax.all_to_all(self_out, "head", split_axis=0, concat_axis=0, tiled=True)
-    for gap in (1, 2):
-        swap = [(i, i ^ gap) for i in range(4)]
-        slope_sum = slope_sum + lax.ppermute(slope_sum, "dp", swap)
-    slope_sum = jnp.sum(slope_sum[:, :HEADS], axis=2)
-    slope_grad = slope_sum / (slopes * (LOG2E * -patches))
     shape = sds(self_queries.shape, BF)
     self_dq, self_dk, self_dv = vmem_call(unpack_self, (shape, shape, shape))(self_out)
     return self_dq, self_dk, self_dv, slope_grad, text_dq, mem_dk, mem_dv

time: 155 us -> 297 us (1.92)
  waiting for transfers between devices: 46.1 us -> 219 us
  blocking collectives: 47.4 us -> 0 us
  between operations: 5.38 us -> 18.8 us
    psum x0 -> x1, waiting for transfers between devices: none -> 140 us  [local(): slope_sum = lax.psum(slope_sum, ('seq', 'dp'))]
    all_to_all x1 -> x0, blocking collectives: 47.4 us -> none  [local(): back = lax.all_to_all(back, 'seq', split_axis=0, concat_axis=0, tiled=True)]
    all_to_all x0 -> x1, waiting for transfers between devices: none -> 37.4 us  [local(): back = lax.all_to_all(back, 'seq', split_axis=0, concat_axis=0, tiled=True)]
    all_to_all x0 -> x1, starting transfers between devices: none -> 5.91 us  [local(): back = lax.all_to_all(back, 'seq', split_axis=0, concat_axis=0, tiled=True)]
    ppermute x2 -> x0, waiting for transfers between devices: 4.65 us -> none  [local(): slope_sum = slope_sum + lax.ppermute(slope_sum, 'dp', swap)]
    ppermute x2 -> x0, starting transfers between devices: 4.24 us -> none  [local(): slope_sum = slope_sum + lax.ppermute(slope_sum, 'dp', swap)]
  transfers between devices with their start and end apart: 7 -> 7, of which waited for: 6 -> 5; matrix products, arithmetic and copies ran while one was open for 5% -> 3% of each run, Pallas kernels for 1% -> 1%
where the time goes in v8:
time: 297 us; the launch traced here: 296 us
  waiting for transfers between devices  219 us (74%)
  starting transfers between devices  22.9 us (8%)
  Pallas kernels  20.9 us (7%)
  between operations  18.8 us (6%)
  local copies, waits for them, and re-layouts  7.7 us (3%)
  other arithmetic  6.61 us (2%)
    psum x1, waiting for transfers between devices, local(): slope_sum = lax.psum(slope_sum, ('seq', 'dp'))  140 us
    all_to_all x1, waiting for transfers between devices, local(): back = lax.all_to_all(back, 'seq', split_axis=0, concat_axis=0, tiled=True)  37.4 us
    all_to_all x1, waiting for transfers between devices, local(): held = lax.all_to_all(sent, 'seq', split_axis=0, concat_axis=0, tiled=True)  36.8 us
    pallas_call x1, Pallas kernels, local(): vmem_call(attend, (sds((TASKS, 3 * BLK, HS), BF), sds((BLK, BLK), F32)),...  14.2 us
    all_to_all x1, starting transfers between devices, local(): held = lax.all_to_all(sent, 'seq', split_axis=0, concat_axis=0, tiled=True)  8.72 us
  transfers between devices with their start and end apart: 7, of which 5 were waited for; matrix products, arithmetic and copies ran while one was open for 3% of the time, Pallas kernels for 1%

profile of v8, /device:TPU:8, one launch (start us, length us, event | category | flops | bytes accessed | tf_op | source)
XLA Modules:
  0.0 295.7 jit_solution(9307846401654193581)
XLA Ops:
  7.2 2.1 shard_map.171
  9.2 1.6 collective-permute-start
  10.8 2.7 collective-permute-start.1
  14.0 1.0 copy-done.1
  15.0 1.0 copy-done.2
  16.0 0.9 copy-done.3
  16.9 0.9 copy-done.4
  17.8 1.6 shard_map.172.text_ref
  19.4 1.8 collective-permute-done.1.s2_ref
  21.3 2.4 collective-permute-done.2.s3_ref
  23.7 1.0 shard_map.173
  24.7 8.7 %all-to-all-start = ((bf16[16,4,128,128]{3,2,1,0:T(8,128)(2,1)}), bf16[16,4,128,128]{3,2,1,0:T(8,128)(2,1)S(1)}, u32[]{:S(2)}, u32[]{:S(2)}) async-start(bf16[16,4,128,128]{3,2,1,0:T(8,128)(2,1)} %shard_map.173), calls=%async_computation | async-start | bytes 4194304 | tf_op jit(solution)/shard_map/all_to_all | solution.py:299
  41.5 0.8 add_reduce_fusion
  42.4 3.3 %subtract_multiply_fusion = (f32[1,2048]{1,0:T(1,128)S(1)}, f32[1,2048]{1,0:T(1,128)S(1)}) fusion(f32[]{:T(128)} %bitcast.6, s32[]{:T(128)S(6)} %add.170, s32[]{:T(128)S(6)} %add.168, s32[]{:T(128)} %bitcast.1, s32[]{:T(128)} %bitcast.14, s32[]{:T(128)} %bitcast.13, s32[]{:T(128)} %bitcast.12, s32[]{:T(128)} %bitcast.11, f32[]{:T(128)} %bitcast.5), kind=kLoop, calls=%fused_computation.17 | loop fusion | flops 55296 | bytes 16420 | tf_op jit(solution)/shard_map/mul | solution.py:257
  45.8 36.8 %all-to-all-done.in_ref = bf16[16,4,128,128]{3,2,1,0:T(8,128)(2,1)S(1)} async-done(((bf16[16,4,128,128]{3,2,1,0:T(8,128)(2,1)}), bf16[16,4,128,128]{3,2,1,0:T(8,128)(2,1)S(1)}, u32[]{:S(2)}, u32[]{:S(2)}) %all-to-all-start) | async-done | bytes 2097184 | tf_op jit(solution)/shard_map/all_to_all | solution.py:299
  82.6 14.2 %shard_map.174 = (bf16[16,384,128]{2,1,0:T(8,128)(2,1)S(1)}, f32[128,128]{1,0:T(8,128)}) custom-call(s32[3,8]{1,0:T(4,128)S(1)} %add_add_fusion.win_ref, f32[5,4]{1,0:T(8,128)S(1)} %stack.52.page_ref, f32[8,2048]{1,0:T(8,128)S(1)} %maximum_maximum_fusion.qi_ref, bf16[16,4,128,128]{3,2,1,0:T(8,128)(2,1)S(1)} %all-to-all-done.in_ref), custom_call_target="tpu_custom_call" | custom-call | tf_op jit(solution)/shard_map/pallas_call | solution.py:300
  96.9 1.2 copy-done
  98.0 5.9 %all-to-all-start.1 = ((bf16[16,384,128]{2,1,0:T(8,128)(2,1)}), bf16[16,384,128]{2,1,0:T(8,128)(2,1)S(1)}, u32[]{:S(2)}, u32[]{:S(2)}) async-start(bf16[16,384,128]{2,1,0:T(8,128)(2,1)} %copy-done), calls=%async_computation.1 | async-start | bytes 3145728 | tf_op jit(solution)/shard_map/all_to_all | solution.py:321
  104.7 37.4 %all-to-all-done.1.in_ref = bf16[16,384,128]{2,1,0:T(8,128)(2,1)S(1)} async-done(((bf16[16,384,128]{2,1,0:T(8,128)(2,1)}), bf16[16,384,128]{2,1,0:T(8,128)(2,1)S(1)}, u32[]{:S(2)}, u32[]{:S(2)}) %all-to-all-start.1) | async-done | bytes 1572896 | tf_op jit(solution)/shard_map/all_to_all | solution.py:321
  142.0 1.2 shard_map.175
  143.2 3.5 %all-to-all-start.2 = ((bf16[4,3,32,640]{3,2,1,0:T(8,128)(2,1)}), bf16[4,3,32,640]{3,2,1,0:T(8,128)(2,1)S(1)}, u32[]{:S(2)}, u32[]{:S(2)}) async-start(bf16[4,3,32,640]{3,2,1,0:T(8,128)(2,1)} %get-tuple-element.25), calls=%async_computation.2 | async-start | bytes 983040 | tf_op jit(solution)/shard_map/all_to_all | solution.py:331
  146.8 139.7 %all-reduce.2.cloned.1.call-done = f32[128,128]{1,0:T(8,128)} async-done(((f32[128,128]{1,0:T(8,128)}), f32[128,128]{1,0:T(8,128)}) %all-reduce.2.cloned.1.call-update) | async-done | bytes 65552 | tf_op jit(solution)/shard_map/psum | solution.py:318
  286.5 0.8 slice_reduce_fusion
  288.0 0.8 shard_map.176
  (43 shorter events, 5.6 us)
Async XLA Ops:
  9.2 10.2 %collective-permute-start = (bf16[4,32,640]{2,1,0:T(8,128)(2,1)}, bf16[4,32,640]{2,1,0:T(8,128)(2,1)S(1)}, u32[]{:S(2)}, u32[]{:S(2)}) collective-permute-start(bf16[4,32,640]{2,1,0:T(8,128)(2,1)} %get-tuple-element.21), channel_id=1, source_target_pairs={{0,4},{4,0},{8,12},{12,8},{1,5},{5,1},{9,13},{13,9},{2,6},{6,2},{1... | collective-permute-start | bytes 491528 | tf_op jit(solution)/shard_map/ppermute | solution.py:274
  10.8 10.5 %collective-permute-start.1 = (bf16[4,32,640]{2,1,0:T(8,128)(2,1)}, bf16[4,32,640]{2,1,0:T(8,128)(2,1)S(1)}, u32[]{:S(2)}, u32[]{:S(2)}) collective-permute-start(bf16[4,32,640]{2,1,0:T(8,128)(2,1)} %get-tuple-element.22), channel_id=1, source_target_pairs={{0,8},{4,12},{8,0},{12,4},{1,9},{5,13},{9,1},{13,5},{2,10},{6,14},... | collective-permute-start | bytes 491528 | tf_op jit(solution)/shard_map/ppermute | solution.py:274
  13.5 10.2 %collective-permute-start.2 = (bf16[4,32,640]{2,1,0:T(8,128)(2,1)}, bf16[4,32,640]{2,1,0:T(8,128)(2,1)S(1)}, u32[]{:S(2)}, u32[]{:S(2)}) collective-permute-start(bf16[4,32,640]{2,1,0:T(8,128)(2,1)} %get-tuple-element.23), channel_id=1, source_target_pairs={{0,12},{4,8},{8,4},{12,0},{1,13},{5,9},{9,5},{13,1},{2,14},{6,10},... | collective-permute-start | bytes 491528 | tf_op jit(solution)/shard_map/ppermute | solution.py:274
  14.0 1.0 copy-start.1
  15.0 1.0 copy-start.2
  16.0 0.9 copy-start.3
  16.9 0.9 copy-start.4
  17.8 5.9 %copy-start.5 = (bf16[4,32,640]{2,1,0:T(8,128)(2,1)S(1)}, bf16[4,32,640]{2,1,0:T(8,128)(2,1)}, u32[]{:S(2)}) copy-start(bf16[4,32,640]{2,1,0:T(8,128)(2,1)} %get-tuple-element.20.s0_ref) | copy-start | bytes 491524
  24.7 8.8 %copy-start.6 = (s32[1,4]{1,0:T(1,128)S(1)}, s32[1,4]{1,0:T(1,128)}, u32[]{:S(2)}) copy-start(s32[1,4]{1,0:T(1,128)} %param.21) | copy-start | bytes 52
  24.7 12.0 %copy-start.8 = (f32[2,5]{1,0:T(2,128)S(1)}, f32[2,5]{1,0:T(2,128)}, u32[]{:S(2)}) copy-start(f32[2,5]{1,0:T(2,128)} %param.20) | copy-start | bytes 124
  24.7 13.9 %copy-start.9 = (s32[1,4096]{1,0:T(1,128)S(1)}, s32[1,4096]{1,0:T(1,128)}, u32[]{:S(2)}) copy-start(s32[1,4096]{1,0:T(1,128)} %param.23) | copy-start | bytes 49156
  24.7 15.3 %copy-start.7 = (s32[1,4]{1,0:T(1,128)S(1)}, s32[1,4]{1,0:T(1,128)}, u32[]{:S(2)}) copy-start(s32[1,4]{1,0:T(1,128)} %param.22) | copy-start | bytes 52
  24.7 57.9 %all-to-all-start = ((bf16[16,4,128,128]{3,2,1,0:T(8,128)(2,1)}), bf16[16,4,128,128]{3,2,1,0:T(8,128)(2,1)S(1)}, u32[]{:S(2)}, u32[]{:S(2)}) async-start(bf16[16,4,128,128]{3,2,1,0:T(8,128)(2,1)} %shard_map.173), calls=%async_computation | async-start | bytes 4194304 | tf_op jit(solution)/shard_map/all_to_all | solution.py:299
  96.9 1.2 copy-start
  98.0 44.0 %all-to-all-start.1 = ((bf16[16,384,128]{2,1,0:T(8,128)(2,1)}), bf16[16,384,128]{2,1,0:T(8,128)(2,1)S(1)}, u32[]{:S(2)}, u32[]{:S(2)}) async-start(bf16[16,384,128]{2,1,0:T(8,128)(2,1)} %copy-done), calls=%async_computation.1 | async-start | bytes 3145728 | tf_op jit(solution)/shard_map/all_to_all | solution.py:321
  104.0 182.5 %all-reduce.2.cloned.1.call-start = ((), (), s32[]{:S(2)}) async-start(), calls=%async_computation.3 | async-start | bytes 131072 | tf_op jit(solution)/shard_map/psum | solution.py:318
  143.2 144.8 %all-to-all-start.2 = ((bf16[4,3,32,640]{3,2,1,0:T(8,128)(2,1)}), bf16[4,3,32,640]{3,2,1,0:T(8,128)(2,1)S(1)}, u32[]{:S(2)}, u32[]{:S(2)}) async-start(bf16[4,3,32,640]{3,2,1,0:T(8,128)(2,1)} %get-tuple-element.25), calls=%async_computation.2 | async-start | bytes 983040 | tf_op jit(solution)/shard_map/all_to_all | solution.py:331
Sparse Core Ops, SparseCore 0:
  108.8 177.5 all-reduce.1

commit v9 on v7

--- a/solution.py
+++ b/solution.py
@@ -17,7 +17,7 @@
 BLK = 128
 HS = 128
 QB = 256
-SIZES = (6, 9, 12, 16)
+SIZES = (5, 7, 9, 11, 13, 16)
 
 
 def vmem_call(body, out_shapes, **kw):
@@ -336,9 +336,11 @@
         ),
     )(back)
     self_out = lax.all_to_all(self_out, "head", split_axis=0, concat_axis=0, tiled=True)
-    for gap in (1, 2):
-        swap = [(i, i ^ gap) for i in range(4)]
-        slope_sum = slope_sum + lax.ppermute(slope_sum, "dp", swap)
+    near, far, last = (
+        lax.ppermute(slope_sum, "dp", [(i, i ^ gap) for i in range(4)])
+        for gap in (1, 2, 3)
+    )
+    slope_sum = (slope_sum + near) + (far + last)
     slope_sum = jnp.sum(slope_sum[:, :HEADS], axis=2)
     slope_grad = slope_sum / (slopes * (LOG2E * -patches))
     shape = sds(self_queries.shape, BF)

time: 155 us -> 154 us (level)
  blocking collectives: 47.4 us -> 50 us
  Pallas kernels: 21.2 us -> 19 us
    all_to_all x1, blocking collectives: 47.4 us -> 50 us  [local(): back = lax.all_to_all(back, 'seq', split_axis=0, concat_axis=0, tiled=True)]
    all_to_all x1, waiting for transfers between devices: 0.29 us -> 2.58 us  [local(): lax.all_to_all(self_out, 'head', split_axis=0, concat_axis=0, tiled=True)]
    ppermute x2 -> x3, waiting for transfers between devices: 4.65 us -> 2.42 us  [local(): lax.ppermute(slope_sum, 'dp', [(i, i ^ gap) for i in range(4)])]
    pallas_call x1, Pallas kernels: 14.6 us -> 12.4 us  [local(): vmem_call(attend, sds((TASKS, 3 * BLK + 16, HS), BF), in_specs=[pl.BlockS...]
    ppermute x2 -> x3, starting transfers between devices: 4.24 us -> 4.17 us  [local(): lax.ppermute(slope_sum, 'dp', [(i, i ^ gap) for i in range(4)])]
  transfers between devices with their start and end apart: 7 -> 8, of which waited for: 6 -> 6; matrix products, arithmetic and copies ran while one was open for 5% -> 5% of each run, Pallas kernels for 1% -> 1%
where the time goes in v9:
time: 154 us
  blocking collectives  50 us (32%)
  waiting for transfers between devices  46.2 us (30%)
  starting transfers between devices  21.1 us (14%)
  Pallas kernels  19 us (12%)
  other arithmetic  6.4 us (4%)
  local copies, waits for them, and re-layouts  5.62 us (4%)
  between operations  5.39 us (4%)
    all_to_all x1, blocking collectives, local(): back = lax.all_to_all(back, 'seq', split_axis=0, concat_axis=0, tiled=True)  50 us
    all_to_all x1, waiting for transfers between devices, local(): held = lax.all_to_all(sent, 'seq', split_axis=0, concat_axis=0, tiled=True)  37 us
    pallas_call x1, Pallas kernels, local(): vmem_call(attend, sds((TASKS, 3 * BLK + 16, HS), BF), in_specs=[pl.BlockS...  12.4 us
    all_to_all x1, starting transfers between devices, local(): held = lax.all_to_all(sent, 'seq', split_axis=0, concat_axis=0, tiled=True)  8.71 us
    ppermute x3, starting transfers between devices, swap_heads(): out[gap] = lax.ppermute(parts[gap], 'head', swap)  4.79 us
    ppermute x3, waiting for transfers between devices, swap_heads(): out[gap] = lax.ppermute(parts[gap], 'head', swap)  4.26 us
    ppermute x3, starting transfers between devices, local(): lax.ppermute(slope_sum, 'dp', [(i, i ^ gap) for i in range(4)])  4.17 us
    unnamed x18, local copies, waits for them, and re-layouts  3.8 us
  transfers between devices with their start and end apart: 8, of which 6 were waited for; matrix products, arithmetic and copies ran while one was open for 5% of the time, Pallas kernels for 1%

profile of v9, /device:TPU:8, one launch (start us, length us, event | category | flops | bytes accessed | tf_op | source)
XLA Modules:
  0.0 153.7 jit_solution(7929544666942917698)
XLA Ops:
  0.6 2.1 %shard_map.171 = (bf16[4,32,640]{2,1,0:T(8,128)(2,1)}, bf16[4,32,640]{2,1,0:T(8,128)(2,1)}, bf16[4,32,640]{2,1,0:T(8,128)(2,1)}, bf16[4,32,640]{2,1,0:T(8,128)(2,1)}) custom-call(bf16[1,32,2560]{2,1,0:T(8,128)(2,1)} %q_ref.1, bf16[1,32,2560]{2,1,0:T(8,128)(2,1)} %k_ref.1, bf16[1,32,2560]{2,1,0:T(8,128)(2,1)} %v_ref.1, bf16[1,32,2560]{2,1,0:T(8,128)(2,1)} %g_ref.1), custom_call_target="tpu_custom_call" | custom-call | tf_op jit(solution)/shard_map/pallas_call | solution.py:287
  2.7 1.6 %collective-permute-start = (bf16[4,32,640]{2,1,0:T(8,128)(2,1)}, bf16[4,32,640]{2,1,0:T(8,128)(2,1)S(1)}, u32[]{:S(2)}, u32[]{:S(2)}) collective-permute-start(bf16[4,32,640]{2,1,0:T(8,128)(2,1)} %get-tuple-element.20), channel_id=1, source_target_pairs={{0,4},{4,0},{8,12},{12,8},{1,5},{5,1},{9,13},{13,9},{2,6},{6,2},{1... | collective-permute-start | bytes 491528 | tf_op jit(solution)/shard_map/ppermute | solution.py:283
  4.3 2.7 %collective-permute-start.1 = (bf16[4,32,640]{2,1,0:T(8,128)(2,1)}, bf16[4,32,640]{2,1,0:T(8,128)(2,1)S(1)}, u32[]{:S(2)}, u32[]{:S(2)}) collective-permute-start(bf16[4,32,640]{2,1,0:T(8,128)(2,1)} %get-tuple-element.21), channel_id=1, source_target_pairs={{0,8},{4,12},{8,0},{12,4},{1,9},{5,13},{9,1},{13,5},{2,10},{6,14},... | collective-permute-start | bytes 491528 | tf_op jit(solution)/shard_map/ppermute | solution.py:283
  7.5 1.0 copy-done
  8.5 1.0 copy-done.1
  9.4 0.9 copy-done.2
  10.3 0.9 copy-done.3
  11.3 1.6 %shard_map.172.text_ref = bf16[16,4,128,128]{3,2,1,0:T(8,128)(2,1)} custom-call(bf16[1,256,640]{2,1,0:T(8,128)(2,1)S(1)} %copy-done, bf16[1,128,640]{2,1,0:T(8,128)(2,1)S(1)} %copy-done.2, bf16[1,128,640]{2,1,0:T(8,128)(2,1)S(1)} %copy-done.3, bf16[1,256,640]{2,1,0:T(8,128)(2,1)S(1)} %copy-done.1), custom_call_target="tpu_custom_call" | custom-call | tf_op jit(solution)/shard_map/pallas_call | solution.py:296
  12.9 1.8 %collective-permute-done.1.s2_ref = bf16[4,32,640]{2,1,0:T(8,128)(2,1)S(1)} collective-permute-done((bf16[4,32,640]{2,1,0:T(8,128)(2,1)}, bf16[4,32,640]{2,1,0:T(8,128)(2,1)S(1)}, u32[]{:S(2)}, u32[]{:S(2)}) %collective-permute-start.1) | collective-permute-done | bytes 163872 | tf_op jit(solution)/shard_map/ppermute | solution.py:283
  14.7 2.4 %collective-permute-done.2.s3_ref = bf16[4,32,640]{2,1,0:T(8,128)(2,1)S(1)} collective-permute-done((bf16[4,32,640]{2,1,0:T(8,128)(2,1)}, bf16[4,32,640]{2,1,0:T(8,128)(2,1)S(1)}, u32[]{:S(2)}, u32[]{:S(2)}) %collective-permute-start.2) | collective-permute-done | bytes 163872 | tf_op jit(solution)/shard_map/ppermute | solution.py:283
  17.2 1.0 shard_map.173
  18.2 8.7 %all-to-all-start = ((bf16[16,4,128,128]{3,2,1,0:T(8,128)(2,1)}), bf16[16,4,128,128]{3,2,1,0:T(8,128)(2,1)S(1)}, u32[]{:S(2)}, u32[]{:S(2)}) async-start(bf16[16,4,128,128]{3,2,1,0:T(8,128)(2,1)} %shard_map.173), calls=%async_computation | async-start | bytes 4194304 | tf_op jit(solution)/shard_map/all_to_all | solution.py:308
  34.3 0.8 select_reduce_fusion
  35.7 3.3 %subtract_multiply_fusion = (f32[1,2048]{1,0:T(1,128)S(1)}, f32[1,2048]{1,0:T(1,128)S(1)}) fusion(f32[]{:T(128)} %bitcast.6, s32[]{:T(128)S(6)} %add.205, s32[]{:T(128)S(6)} %add.203, s32[]{:T(128)} %bitcast.1, s32[]{:T(128)} %bitcast.14, s32[]{:T(128)} %bitcast.13, s32[]{:T(128)} %bitcast.12, s32[]{:T(128)} %bitcast.11, f32[]{:T(128)} %bitcast.5), kind=kLoop, calls=%fused_computation.20 | loop fusion | flops 55296 | bytes 16420 | tf_op jit(solution)/shard_map/mul | solution.py:267
  39.1 37.0 %all-to-all-done.in_ref = bf16[16,4,128,128]{3,2,1,0:T(8,128)(2,1)S(1)} async-done(((bf16[16,4,128,128]{3,2,1,0:T(8,128)(2,1)}), bf16[16,4,128,128]{3,2,1,0:T(8,128)(2,1)S(1)}, u32[]{:S(2)}, u32[]{:S(2)}) %all-to-all-start) | async-done | bytes 2097184 | tf_op jit(solution)/shard_map/all_to_all | solution.py:308
  76.1 12.4 %shard_map.174 = bf16[16,400,128]{2,1,0:T(8,128)(2,1)S(1)} custom-call(s32[2,8]{1,0:T(2,128)S(1)} %pad_add_fusion.win_ref, f32[5,4]{1,0:T(8,128)S(1)} %stack.52.page_ref, f32[8,2048]{1,0:T(8,128)S(1)} %maximum_maximum_fusion.qi_ref, bf16[16,4,128,128]{3,2,1,0:T(8,128)(2,1)S(1)} %all-to-all-done.in_ref), custom_call_target="tpu_custom_call" | custom-call | tf_op jit(solution)/shard_map/pallas_call | solution.py:309
  88.5 50.0 %all_to_all.15.in_ref = bf16[16,400,128]{2,1,0:T(8,128)(2,1)S(1)} all-to-all(bf16[16,400,128]{2,1,0:T(8,128)(2,1)S(1)} %shard_map.174), channel_id=1, replica_groups=mesh['seq'=16,'head'=4,'dp'=4] {'seq'}, dimensions={0} | all-to-all | bytes 3276800 | tf_op jit(solution)/shard_map/all_to_all | solution.py:327
  138.4 1.2 shard_map.175
  139.6 3.5 %all-to-all-start.2 = ((bf16[4,3,32,640]{3,2,1,0:T(8,128)(2,1)}), bf16[4,3,32,640]{3,2,1,0:T(8,128)(2,1)S(1)}, u32[]{:S(2)}, u32[]{:S(2)}) async-start(bf16[4,3,32,640]{3,2,1,0:T(8,128)(2,1)} %get-tuple-element.23), calls=%async_computation.2 | async-start | bytes 983040 | tf_op jit(solution)/shard_map/all_to_all | solution.py:338
  143.2 2.9 %collective-permute-start.4 = (f32[2,8,128]{2,1,0:T(8,128)S(1)}, f32[2,8,128]{2,1,0:T(8,128)S(1)}, u32[]{:S(2)}, u32[]{:S(2)}) collective-permute-start(f32[2,8,128]{2,1,0:T(8,128)S(1)} %get-tuple-element.27), channel_id=1, source_target_pairs={{0,2},{1,3},{2,0},{3,1},{4,6},{5,7},{6,4},{7,5},{8,10},{9,11},{10,... | collective-permute-start | bytes 24584 | tf_op jit(solution)/shard_map/ppermute | solution.py:340
  146.0 1.2 collective-permute-start.3
  147.3 1.2 collective-permute-done.4
  148.4 1.3 collective-permute-done.3
  150.3 2.6 %all-to-all-done.2.in_ref = bf16[4,3,32,640]{3,2,1,0:T(8,128)(2,1)S(1)} async-done(((bf16[4,3,32,640]{3,2,1,0:T(8,128)(2,1)}), bf16[4,3,32,640]{3,2,1,0:T(8,128)(2,1)S(1)}, u32[]{:S(2)}, u32[]{:S(2)}) %all-to-all-start.2) | async-done | bytes 491552 | tf_op jit(solution)/shard_map/all_to_all | solution.py:338
  (39 shorter events, 5.5 us)
Async XLA Ops:
  2.7 10.2 %collective-permute-start = (bf16[4,32,640]{2,1,0:T(8,128)(2,1)}, bf16[4,32,640]{2,1,0:T(8,128)(2,1)S(1)}, u32[]{:S(2)}, u32[]{:S(2)}) collective-permute-start(bf16[4,32,640]{2,1,0:T(8,128)(2,1)} %get-tuple-element.20), channel_id=1, source_target_pairs={{0,4},{4,0},{8,12},{12,8},{1,5},{5,1},{9,13},{13,9},{2,6},{6,2},{1... | collective-permute-start | bytes 491528 | tf_op jit(solution)/shard_map/ppermute | solution.py:283
  4.3 10.5 %collective-permute-start.1 = (bf16[4,32,640]{2,1,0:T(8,128)(2,1)}, bf16[4,32,640]{2,1,0:T(8,128)(2,1)S(1)}, u32[]{:S(2)}, u32[]{:S(2)}) collective-permute-start(bf16[4,32,640]{2,1,0:T(8,128)(2,1)} %get-tuple-element.21), channel_id=1, source_target_pairs={{0,8},{4,12},{8,0},{12,4},{1,9},{5,13},{9,1},{13,5},{2,10},{6,14},... | collective-permute-start | bytes 491528 | tf_op jit(solution)/shard_map/ppermute | solution.py:283
  7.0 10.2 %collective-permute-start.2 = (bf16[4,32,640]{2,1,0:T(8,128)(2,1)}, bf16[4,32,640]{2,1,0:T(8,128)(2,1)S(1)}, u32[]{:S(2)}, u32[]{:S(2)}) collective-permute-start(bf16[4,32,640]{2,1,0:T(8,128)(2,1)} %get-tuple-element.22), channel_id=1, source_target_pairs={{0,12},{4,8},{8,4},{12,0},{1,13},{5,9},{9,5},{13,1},{2,14},{6,10},... | collective-permute-start | bytes 491528 | tf_op jit(solution)/shard_map/ppermute | solution.py:283
  7.5 1.0 copy-start
  8.5 1.0 copy-start.1
  9.4 0.9 copy-start.2
  10.3 0.9 copy-start.3
  11.3 5.9 %copy-start.4 = (bf16[4,32,640]{2,1,0:T(8,128)(2,1)S(1)}, bf16[4,32,640]{2,1,0:T(8,128)(2,1)}, u32[]{:S(2)}) copy-start(bf16[4,32,640]{2,1,0:T(8,128)(2,1)} %get-tuple-element.19.s0_ref) | copy-start | bytes 491524
  18.1 8.8 %copy-start.7 = (f32[2,5]{1,0:T(2,128)S(1)}, f32[2,5]{1,0:T(2,128)}, u32[]{:S(2)}) copy-start(f32[2,5]{1,0:T(2,128)} %param.20) | copy-start | bytes 124
  18.1 10.7 %copy-start.6 = (s32[1,4]{1,0:T(1,128)S(1)}, s32[1,4]{1,0:T(1,128)}, u32[]{:S(2)}) copy-start(s32[1,4]{1,0:T(1,128)} %param.22) | copy-start | bytes 52
  18.2 10.7 %copy-start.5 = (s32[1,4]{1,0:T(1,128)S(1)}, s32[1,4]{1,0:T(1,128)}, u32[]{:S(2)}) copy-start(s32[1,4]{1,0:T(1,128)} %param.21) | copy-start | bytes 52
  18.2 14.5 %copy-start.8 = (s32[1,4096]{1,0:T(1,128)S(1)}, s32[1,4096]{1,0:T(1,128)}, u32[]{:S(2)}) copy-start(s32[1,4096]{1,0:T(1,128)} %param.23) | copy-start | bytes 49156
  18.2 57.9 %all-to-all-start = ((bf16[16,4,128,128]{3,2,1,0:T(8,128)(2,1)}), bf16[16,4,128,128]{3,2,1,0:T(8,128)(2,1)S(1)}, u32[]{:S(2)}, u32[]{:S(2)}) async-start(bf16[16,4,128,128]{3,2,1,0:T(8,128)(2,1)} %shard_map.173), calls=%async_computation | async-start | bytes 4194304 | tf_op jit(solution)/shard_map/all_to_all | solution.py:308
  139.6 13.3 %all-to-all-start.2 = ((bf16[4,3,32,640]{3,2,1,0:T(8,128)(2,1)}), bf16[4,3,32,640]{3,2,1,0:T(8,128)(2,1)S(1)}, u32[]{:S(2)}, u32[]{:S(2)}) async-start(bf16[4,3,32,640]{3,2,1,0:T(8,128)(2,1)} %get-tuple-element.23), calls=%async_computation.2 | async-start | bytes 983040 | tf_op jit(solution)/shard_map/all_to_all | solution.py:338
  143.1 4.2 %collective-permute-start.5 = (f32[2,8,128]{2,1,0:T(8,128)S(1)}, f32[2,8,128]{2,1,0:T(8,128)S(1)}, u32[]{:S(2)}, u32[]{:S(2)}) collective-permute-start(f32[2,8,128]{2,1,0:T(8,128)S(1)} %get-tuple-element.27), channel_id=1, source_target_pairs={{0,3},{1,2},{2,1},{3,0},{4,7},{5,6},{6,5},{7,4},{8,11},{9,10},{10,... | collective-permute-start | bytes 24584 | tf_op jit(solution)/shard_map/ppermute | solution.py:340
  143.2 5.2 %collective-permute-start.4 = (f32[2,8,128]{2,1,0:T(8,128)S(1)}, f32[2,8,128]{2,1,0:T(8,128)S(1)}, u32[]{:S(2)}, u32[]{:S(2)}) collective-permute-start(f32[2,8,128]{2,1,0:T(8,128)S(1)} %get-tuple-element.27), channel_id=1, source_target_pairs={{0,2},{1,3},{2,0},{3,1},{4,6},{5,7},{6,4},{7,5},{8,10},{9,11},{10,... | collective-permute-start | bytes 24584 | tf_op jit(solution)/shard_map/ppermute | solution.py:340
  146.0 3.7 %collective-permute-start.3 = (f32[2,8,128]{2,1,0:T(8,128)S(1)}, f32[2,8,128]{2,1,0:T(8,128)S(1)}, u32[]{:S(2)}, u32[]{:S(2)}) collective-permute-start(f32[2,8,128]{2,1,0:T(8,128)S(1)} %get-tuple-element.27), channel_id=1, source_target_pairs={{0,1},{1,0},{2,3},{3,2},{4,5},{5,4},{6,7},{7,6},{8,9},{9,8},{10,11... | collective-permute-start | bytes 24584 | tf_op jit(solution)/shard_map/ppermute | solution.py:340

commit v10 on v9

--- a/solution.py
+++ b/solution.py
@@ -17,7 +17,7 @@
 BLK = 128
 HS = 128
 QB = 256
-SIZES = (5, 7, 9, 11, 13, 16)
+SIZES = (4, 6, 8, 9, 10, 12, 14, 16)
 
 
 def vmem_call(body, out_shapes, **kw):

time: 154 us -> 156 us (1.013); the launches traced: 154 us -> 153 us
  blocking collectives: 50 us -> 46.1 us
  Pallas kernels: 19 us -> 22.4 us
    all_to_all x1, blocking collectives: 50 us -> 46.1 us  [local(): back = lax.all_to_all(back, 'seq', split_axis=0, concat_axis=0, tiled=True)]
    pallas_call x1, Pallas kernels: 12.4 us -> 15.8 us  [local(): vmem_call(attend, sds((TASKS, 3 * BLK + 16, HS), BF), in_specs=[pl.BlockS...]
where the time goes in v10:
time: 156 us; the launch traced here: 153 us
  waiting for transfers between devices  46.2 us (30%)
  blocking collectives  46.1 us (30%)
  Pallas kernels  22.4 us (14%)
  starting transfers between devices  21.1 us (14%)
  other arithmetic  6.4 us (4%)
  local copies, waits for them, and re-layouts  5.62 us (4%)
  between operations  5.38 us (3%)
    all_to_all x1, blocking collectives, local(): back = lax.all_to_all(back, 'seq', split_axis=0, concat_axis=0, tiled=True)  46.1 us
    all_to_all x1, waiting for transfers between devices, local(): held = lax.all_to_all(sent, 'seq', split_axis=0, concat_axis=0, tiled=True)  37 us
    pallas_call x1, Pallas kernels, local(): vmem_call(attend, sds((TASKS, 3 * BLK + 16, HS), BF), in_specs=[pl.BlockS...  15.8 us
    all_to_all x1, starting transfers between devices, local(): held = lax.all_to_all(sent, 'seq', split_axis=0, concat_axis=0, tiled=True)  8.71 us
    ppermute x3, starting transfers between devices, swap_heads(): out[gap] = lax.ppermute(parts[gap], 'head', swap)  4.79 us
    ppermute x3, waiting for transfers between devices, swap_heads(): out[gap] = lax.ppermute(parts[gap], 'head', swap)  4.26 us
    ppermute x3, starting transfers between devices, local(): lax.ppermute(slope_sum, 'dp', [(i, i ^ gap) for i in range(4)])  4.18 us
    unnamed x18, local copies, waits for them, and re-layouts  3.8 us
  transfers between devices with their start and end apart: 8, of which 6 were waited for; matrix products, arithmetic and copies ran while one was open for 5% of the time, Pallas kernels for 1%

profile of v10, /device:TPU:8, one launch (start us, length us, event | category | flops | bytes accessed | tf_op | source)
XLA Modules:
  0.0 153.2 jit_solution(11662973461410566718)
XLA Ops:
  0.6 2.1 %shard_map.171 = (bf16[4,32,640]{2,1,0:T(8,128)(2,1)}, bf16[4,32,640]{2,1,0:T(8,128)(2,1)}, bf16[4,32,640]{2,1,0:T(8,128)(2,1)}, bf16[4,32,640]{2,1,0:T(8,128)(2,1)}) custom-call(bf16[1,32,2560]{2,1,0:T(8,128)(2,1)} %q_ref.1, bf16[1,32,2560]{2,1,0:T(8,128)(2,1)} %k_ref.1, bf16[1,32,2560]{2,1,0:T(8,128)(2,1)} %v_ref.1, bf16[1,32,2560]{2,1,0:T(8,128)(2,1)} %g_ref.1), custom_call_target="tpu_custom_call" | custom-call | tf_op jit(solution)/shard_map/pallas_call | solution.py:287
  2.7 1.6 %collective-permute-start = (bf16[4,32,640]{2,1,0:T(8,128)(2,1)}, bf16[4,32,640]{2,1,0:T(8,128)(2,1)S(1)}, u32[]{:S(2)}, u32[]{:S(2)}) collective-permute-start(bf16[4,32,640]{2,1,0:T(8,128)(2,1)} %get-tuple-element.20), channel_id=1, source_target_pairs={{0,4},{4,0},{8,12},{12,8},{1,5},{5,1},{9,13},{13,9},{2,6},{6,2},{1... | collective-permute-start | bytes 491528 | tf_op jit(solution)/shard_map/ppermute | solution.py:283
  4.3 2.7 %collective-permute-start.1 = (bf16[4,32,640]{2,1,0:T(8,128)(2,1)}, bf16[4,32,640]{2,1,0:T(8,128)(2,1)S(1)}, u32[]{:S(2)}, u32[]{:S(2)}) collective-permute-start(bf16[4,32,640]{2,1,0:T(8,128)(2,1)} %get-tuple-element.21), channel_id=1, source_target_pairs={{0,8},{4,12},{8,0},{12,4},{1,9},{5,13},{9,1},{13,5},{2,10},{6,14},... | collective-permute-start | bytes 491528 | tf_op jit(solution)/shard_map/ppermute | solution.py:283
  7.5 1.0 copy-done
  8.5 1.0 copy-done.1
  9.4 0.9 copy-done.2
  10.3 0.9 copy-done.3
  11.3 1.6 %shard_map.172.text_ref = bf16[16,4,128,128]{3,2,1,0:T(8,128)(2,1)} custom-call(bf16[1,256,640]{2,1,0:T(8,128)(2,1)S(1)} %copy-done, bf16[1,128,640]{2,1,0:T(8,128)(2,1)S(1)} %copy-done.2, bf16[1,128,640]{2,1,0:T(8,128)(2,1)S(1)} %copy-done.3, bf16[1,256,640]{2,1,0:T(8,128)(2,1)S(1)} %copy-done.1), custom_call_target="tpu_custom_call" | custom-call | tf_op jit(solution)/shard_map/pallas_call | solution.py:296
  12.9 1.8 %collective-permute-done.1.s2_ref = bf16[4,32,640]{2,1,0:T(8,128)(2,1)S(1)} collective-permute-done((bf16[4,32,640]{2,1,0:T(8,128)(2,1)}, bf16[4,32,640]{2,1,0:T(8,128)(2,1)S(1)}, u32[]{:S(2)}, u32[]{:S(2)}) %collective-permute-start.1) | collective-permute-done | bytes 163872 | tf_op jit(solution)/shard_map/ppermute | solution.py:283
  14.7 2.4 %collective-permute-done.2.s3_ref = bf16[4,32,640]{2,1,0:T(8,128)(2,1)S(1)} collective-permute-done((bf16[4,32,640]{2,1,0:T(8,128)(2,1)}, bf16[4,32,640]{2,1,0:T(8,128)(2,1)S(1)}, u32[]{:S(2)}, u32[]{:S(2)}) %collective-permute-start.2) | collective-permute-done | bytes 163872 | tf_op jit(solution)/shard_map/ppermute | solution.py:283
  17.2 1.0 shard_map.173
  18.2 8.7 %all-to-all-start = ((bf16[16,4,128,128]{3,2,1,0:T(8,128)(2,1)}), bf16[16,4,128,128]{3,2,1,0:T(8,128)(2,1)S(1)}, u32[]{:S(2)}, u32[]{:S(2)}) async-start(bf16[16,4,128,128]{3,2,1,0:T(8,128)(2,1)} %shard_map.173), calls=%async_computation | async-start | bytes 4194304 | tf_op jit(solution)/shard_map/all_to_all | solution.py:308
  34.3 0.8 select_reduce_fusion
  35.7 3.3 %subtract_multiply_fusion = (f32[1,2048]{1,0:T(1,128)S(1)}, f32[1,2048]{1,0:T(1,128)S(1)}) fusion(f32[]{:T(128)} %bitcast.6, s32[]{:T(128)S(6)} %add.233, s32[]{:T(128)S(6)} %add.231, s32[]{:T(128)} %bitcast.1, s32[]{:T(128)} %bitcast.14, s32[]{:T(128)} %bitcast.13, s32[]{:T(128)} %bitcast.12, s32[]{:T(128)} %bitcast.11, f32[]{:T(128)} %bitcast.5), kind=kLoop, calls=%fused_computation.20 | loop fusion | flops 55296 | bytes 16420 | tf_op jit(solution)/shard_map/mul | solution.py:267
  39.1 37.0 %all-to-all-done.in_ref = bf16[16,4,128,128]{3,2,1,0:T(8,128)(2,1)S(1)} async-done(((bf16[16,4,128,128]{3,2,1,0:T(8,128)(2,1)}), bf16[16,4,128,128]{3,2,1,0:T(8,128)(2,1)S(1)}, u32[]{:S(2)}, u32[]{:S(2)}) %all-to-all-start) | async-done | bytes 2097184 | tf_op jit(solution)/shard_map/all_to_all | solution.py:308
  76.1 15.8 %shard_map.174 = bf16[16,400,128]{2,1,0:T(8,128)(2,1)S(1)} custom-call(s32[2,8]{1,0:T(2,128)S(1)} %pad_add_fusion.win_ref, f32[5,4]{1,0:T(8,128)S(1)} %stack.52.page_ref, f32[8,2048]{1,0:T(8,128)S(1)} %maximum_maximum_fusion.qi_ref, bf16[16,4,128,128]{3,2,1,0:T(8,128)(2,1)S(1)} %all-to-all-done.in_ref), custom_call_target="tpu_custom_call" | custom-call | tf_op jit(solution)/shard_map/pallas_call | solution.py:309
  91.9 46.1 %all_to_all.15.in_ref = bf16[16,400,128]{2,1,0:T(8,128)(2,1)S(1)} all-to-all(bf16[16,400,128]{2,1,0:T(8,128)(2,1)S(1)} %shard_map.174), channel_id=1, replica_groups=mesh['seq'=16,'head'=4,'dp'=4] {'seq'}, dimensions={0} | all-to-all | bytes 3276800 | tf_op jit(solution)/shard_map/all_to_all | solution.py:327
  137.9 1.2 shard_map.175
  139.1 3.5 %all-to-all-start.2 = ((bf16[4,3,32,640]{3,2,1,0:T(8,128)(2,1)}), bf16[4,3,32,640]{3,2,1,0:T(8,128)(2,1)S(1)}, u32[]{:S(2)}, u32[]{:S(2)}) async-start(bf16[4,3,32,640]{3,2,1,0:T(8,128)(2,1)} %get-tuple-element.23), calls=%async_computation.2 | async-start | bytes 983040 | tf_op jit(solution)/shard_map/all_to_all | solution.py:338
  142.6 1.9 %collective-permute-start.5 = (f32[2,8,128]{2,1,0:T(8,128)S(1)}, f32[2,8,128]{2,1,0:T(8,128)S(1)}, u32[]{:S(2)}, u32[]{:S(2)}) collective-permute-start(f32[2,8,128]{2,1,0:T(8,128)S(1)} %get-tuple-element.27), channel_id=1, source_target_pairs={{0,3},{1,2},{2,1},{3,0},{4,7},{5,6},{6,5},{7,4},{8,11},{9,10},{10,... | collective-permute-start | bytes 24584 | tf_op jit(solution)/shard_map/ppermute | solution.py:340
  144.5 2.0 %collective-permute-start.4 = (f32[2,8,128]{2,1,0:T(8,128)S(1)}, f32[2,8,128]{2,1,0:T(8,128)S(1)}, u32[]{:S(2)}, u32[]{:S(2)}) collective-permute-start(f32[2,8,128]{2,1,0:T(8,128)S(1)} %get-tuple-element.27), channel_id=1, source_target_pairs={{0,2},{1,3},{2,0},{3,1},{4,6},{5,7},{6,4},{7,5},{8,10},{9,11},{10,... | collective-permute-start | bytes 24584 | tf_op jit(solution)/shard_map/ppermute | solution.py:340
  146.8 2.9 %collective-permute-done.4 = f32[2,8,128]{2,1,0:T(8,128)S(1)} collective-permute-done((f32[2,8,128]{2,1,0:T(8,128)S(1)}, f32[2,8,128]{2,1,0:T(8,128)S(1)}, u32[]{:S(2)}, u32[]{:S(2)}) %collective-permute-start.4) | collective-permute-done | bytes 8224 | tf_op jit(solution)/shard_map/ppermute | solution.py:340
  150.8 1.6 %all-to-all-done.2.in_ref = bf16[4,3,32,640]{3,2,1,0:T(8,128)(2,1)S(1)} async-done(((bf16[4,3,32,640]{3,2,1,0:T(8,128)(2,1)}), bf16[4,3,32,640]{3,2,1,0:T(8,128)(2,1)S(1)}, u32[]{:S(2)}, u32[]{:S(2)}) %all-to-all-start.2) | async-done | bytes 491552 | tf_op jit(solution)/shard_map/all_to_all | solution.py:338
  152.4 0.8 shard_map.176
  (39 shorter events, 5.3 us)
Async XLA Ops:
  2.7 10.2 %collective-permute-start = (bf16[4,32,640]{2,1,0:T(8,128)(2,1)}, bf16[4,32,640]{2,1,0:T(8,128)(2,1)S(1)}, u32[]{:S(2)}, u32[]{:S(2)}) collective-permute-start(bf16[4,32,640]{2,1,0:T(8,128)(2,1)} %get-tuple-element.20), channel_id=1, source_target_pairs={{0,4},{4,0},{8,12},{12,8},{1,5},{5,1},{9,13},{13,9},{2,6},{6,2},{1... | collective-permute-start | bytes 491528 | tf_op jit(solution)/shard_map/ppermute | solution.py:283
  4.3 10.5 %collective-permute-start.1 = (bf16[4,32,640]{2,1,0:T(8,128)(2,1)}, bf16[4,32,640]{2,1,0:T(8,128)(2,1)S(1)}, u32[]{:S(2)}, u32[]{:S(2)}) collective-permute-start(bf16[4,32,640]{2,1,0:T(8,128)(2,1)} %get-tuple-element.21), channel_id=1, source_target_pairs={{0,8},{4,12},{8,0},{12,4},{1,9},{5,13},{9,1},{13,5},{2,10},{6,14},... | collective-permute-start | bytes 491528 | tf_op jit(solution)/shard_map/ppermute | solution.py:283
  7.0 10.2 %collective-permute-start.2 = (bf16[4,32,640]{2,1,0:T(8,128)(2,1)}, bf16[4,32,640]{2,1,0:T(8,128)(2,1)S(1)}, u32[]{:S(2)}, u32[]{:S(2)}) collective-permute-start(bf16[4,32,640]{2,1,0:T(8,128)(2,1)} %get-tuple-element.22), channel_id=1, source_target_pairs={{0,12},{4,8},{8,4},{12,0},{1,13},{5,9},{9,5},{13,1},{2,14},{6,10},... | collective-permute-start | bytes 491528 | tf_op jit(solution)/shard_map/ppermute | solution.py:283
  7.5 1.0 copy-start
  8.5 1.0 copy-start.1
  9.4 0.9 copy-start.2
  10.3 0.9 copy-start.3
  11.3 5.9 %copy-start.4 = (bf16[4,32,640]{2,1,0:T(8,128)(2,1)S(1)}, bf16[4,32,640]{2,1,0:T(8,128)(2,1)}, u32[]{:S(2)}) copy-start(bf16[4,32,640]{2,1,0:T(8,128)(2,1)} %get-tuple-element.19.s0_ref) | copy-start | bytes 491524
  18.1 8.8 %copy-start.7 = (f32[2,5]{1,0:T(2,128)S(1)}, f32[2,5]{1,0:T(2,128)}, u32[]{:S(2)}) copy-start(f32[2,5]{1,0:T(2,128)} %param.20) | copy-start | bytes 124
  18.1 10.7 %copy-start.6 = (s32[1,4]{1,0:T(1,128)S(1)}, s32[1,4]{1,0:T(1,128)}, u32[]{:S(2)}) copy-start(s32[1,4]{1,0:T(1,128)} %param.22) | copy-start | bytes 52
  18.2 10.7 %copy-start.5 = (s32[1,4]{1,0:T(1,128)S(1)}, s32[1,4]{1,0:T(1,128)}, u32[]{:S(2)}) copy-start(s32[1,4]{1,0:T(1,128)} %param.21) | copy-start | bytes 52
  18.2 14.5 %copy-start.8 = (s32[1,4096]{1,0:T(1,128)S(1)}, s32[1,4096]{1,0:T(1,128)}, u32[]{:S(2)}) copy-start(s32[1,4096]{1,0:T(1,128)} %param.23) | copy-start | bytes 49156
  18.2 57.9 %all-to-all-start = ((bf16[16,4,128,128]{3,2,1,0:T(8,128)(2,1)}), bf16[16,4,128,128]{3,2,1,0:T(8,128)(2,1)S(1)}, u32[]{:S(2)}, u32[]{:S(2)}) async-start(bf16[16,4,128,128]{3,2,1,0:T(8,128)(2,1)} %shard_map.173), calls=%async_computation | async-start | bytes 4194304 | tf_op jit(solution)/shard_map/all_to_all | solution.py:308
  139.1 13.3 %all-to-all-start.2 = ((bf16[4,3,32,640]{3,2,1,0:T(8,128)(2,1)}), bf16[4,3,32,640]{3,2,1,0:T(8,128)(2,1)S(1)}, u32[]{:S(2)}, u32[]{:S(2)}) async-start(bf16[4,3,32,640]{3,2,1,0:T(8,128)(2,1)} %get-tuple-element.23), calls=%async_computation.2 | async-start | bytes 983040 | tf_op jit(solution)/shard_map/all_to_all | solution.py:338
  142.6 4.2 %collective-permute-start.5 = (f32[2,8,128]{2,1,0:T(8,128)S(1)}, f32[2,8,128]{2,1,0:T(8,128)S(1)}, u32[]{:S(2)}, u32[]{:S(2)}) collective-permute-start(f32[2,8,128]{2,1,0:T(8,128)S(1)} %get-tuple-element.27), channel_id=1, source_target_pairs={{0,3},{1,2},{2,1},{3,0},{4,7},{5,6},{6,5},{7,4},{8,11},{9,10},{10,... | collective-permute-start | bytes 24584 | tf_op jit(solution)/shard_map/ppermute | solution.py:340
  144.5 5.2 %collective-permute-start.4 = (f32[2,8,128]{2,1,0:T(8,128)S(1)}, f32[2,8,128]{2,1,0:T(8,128)S(1)}, u32[]{:S(2)}, u32[]{:S(2)}) collective-permute-start(f32[2,8,128]{2,1,0:T(8,128)S(1)} %get-tuple-element.27), channel_id=1, source_target_pairs={{0,2},{1,3},{2,0},{3,1},{4,6},{5,7},{6,4},{7,5},{8,10},{9,11},{10,... | collective-permute-start | bytes 24584 | tf_op jit(solution)/shard_map/ppermute | solution.py:340
  146.5 3.7 %collective-permute-start.3 = (f32[2,8,128]{2,1,0:T(8,128)S(1)}, f32[2,8,128]{2,1,0:T(8,128)S(1)}, u32[]{:S(2)}, u32[]{:S(2)}) collective-permute-start(f32[2,8,128]{2,1,0:T(8,128)S(1)} %get-tuple-element.27), channel_id=1, source_target_pairs={{0,1},{1,0},{2,3},{3,2},{4,5},{5,4},{6,7},{7,6},{8,9},{9,8},{10,11... | collective-permute-start | bytes 24584 | tf_op jit(solution)/shard_map/ppermute | solution.py:340
